TPU v7x, 32 devices: a whole 2x2x4 slice. The times are simulated.
32 devices in a mesh: section: 2 (over x), dp: 16 (over z, y, core).
Axes of the slice: x: 2, y: 2, z: 4, core: 2. Of those that a mesh axis runs over, the one named last changes fastest.
Arguments:
- embedded: bfloat16 [2, 32, 512, 768], P('section', 'dp'), may hold values from -6 to 6
- lengths: int32 [32], P('dp'), may hold values from 256 to 512, as said below
- positions: int32 [2, 32, 64], P('section', 'dp'), may hold values from 1 to 511, as said below
- labels: int32 [2, 32, 64], P('section', 'dp'), may hold values from 0 to 30719
- joint_weight: bfloat16 [2, 768, 2304], P('section'), may hold values from -0.21875 to 0.21875
- mixer_weight: bfloat16 [2, 768, 768], P('section'), may hold values from -0.875 to 0.875
- expand_weight: bfloat16 [2, 768, 3072], P('section'), may hold values from -0.21875 to 0.21875
- contract_weight: bfloat16 [2, 3072, 768], P('section'), may hold values from -0.109375 to 0.109375
- head_weight: bfloat16 [2, 768, 768], P('section'), may hold values from -0.21875 to 0.21875
- gains: float32 [2, 3, 768], P('section'), may hold values from 0.5 to 1.5
- biases: float32 [2, 8, 768], P('section'), may hold values from -2 to 2
- expand_bias: float32 [2, 3072], P('section'), may hold values from -2 to 2
- word_table: bfloat16 [30720, 768], P('dp'), may hold values from -0.4375 to 0.4375
- word_bias: bfloat16 [30720], P('dp'), may hold values from -3 to 3
Outputs:
- loss: float32 [2], P('section')
- logits: bfloat16 [2, 32, 64, 30720], P('section', 'dp')
- input_grads: float32 [2, 32, 512, 768], P('section', 'dp')
- joint_grad: float32 [2, 768, 2304], P('section', 'dp')
- mixer_grad: float32 [2, 768, 768], P('section', 'dp')
- expand_grad: float32 [2, 768, 3072], P('section', 'dp')
- contract_grad: float32 [2, 3072, 768], P('section', 'dp')
- head_grads: float32 [2, 768, 768], P('section', 'dp')
- gain_grads: float32 [2, 3, 768], P('section')
- bias_grads: float32 [2, 8, 768], P('section')
- expand_bias_grad: float32 [2, 3072], P('section')
- table_grads: float32 [30720, 768], P('dp')
- word_bias_grad: float32 [30720], P('dp')
Inputs may be any that keep to these rules, and one draw needn't show every extreme that they name: `lengths`: every passage is at least 256 long, and some passage is exactly 512. `positions`: distinct within each passage and section, each at least 1 and below that passage's length.
All inputs are finite; a program needn't handle non-finite values.
Results may differ from a plain program's by a relative error of at most 0.018.
Values may be sent and summed in bfloat16 or wider, within the bound.
No kernel may reach another device: no remote copies, remote signals or barrier semaphores. Data moves between devices by JAX's collectives and lax.ppermute only.
A program may use at most 512 MiB of HBM per device.

v0:
```python
import jax
import jax.numpy as jnp
from jax import lax
from jax.sharding import PartitionSpec as P

HEADS = 12


EPS = 1e-12
ROOT_HALF = 0.7071067811865476
INV_ROOT_TAU = 0.3989422804014327


def passed_along(block, axis, distance):
    devices = range(lax.axis_size(axis))
    route = [(i - distance, i) for i in devices if i - distance in devices]
    return lax.ppermute(block, axis, route)


def matmul(left, right):
    return jnp.dot(left, right, preferred_element_type=jnp.float32)


def outer_sum(left, right):
    return lax.dot_general(
        left, right, (((0,), (0,)), ((), ())), preferred_element_type=jnp.float32
    )


def back_mul(left, right):
    return lax.dot_general(
        left, right, (((1,), (1,)), ((), ())), preferred_element_type=jnp.float32
    )


def norm_forward(resid, gain, shift):
    centre = resid - jnp.mean(resid, axis=-1, keepdims=True)
    scale_inv = lax.rsqrt(jnp.mean(centre * centre, axis=-1, keepdims=True) + EPS)
    normed = centre * scale_inv
    return (normed * gain + shift, normed, scale_inv)


def norm_back(grad, normed, scale_inv, gain):
    scaled = grad * gain
    first_mean = jnp.mean(scaled, axis=-1, keepdims=True)
    second_mean = jnp.mean(scaled * normed, axis=-1, keepdims=True)
    return (
        scale_inv * (scaled - first_mean - normed * second_mean),
        jnp.sum(grad * normed, 0),
        jnp.sum(grad, 0),
    )


def gelu_slope(value):
    return (
        0.5 * (1.0 + lax.erf(value * ROOT_HALF))
        + value * jnp.exp(-0.5 * value * value) * INV_ROOT_TAU
    )


def key_scores(queries, keys, length):
    scores = jnp.einsum(
        "qhd,khd->hqk", queries, keys, preferred_element_type=jnp.float32
    ) * queries.shape[-1] ** (-0.5)
    visible = jnp.arange(keys.shape[0]) < length
    return jnp.where(visible[None, None, :], scores, -1000000000.0)


def kept_blank(lead, rows, width, hidden_units):
    head_dim = width // HEADS
    plain = jnp.bfloat16
    wide = jnp.float32
    return (
        jnp.zeros(lead + (rows, width), plain),
        jnp.zeros(lead + (rows, HEADS, head_dim), plain),
        jnp.zeros(lead + (rows, HEADS, head_dim), plain),
        jnp.zeros(lead + (rows, HEADS, head_dim), plain),
        jnp.zeros(lead + (HEADS, rows, 1), wide),
        jnp.zeros(lead + (rows, width), plain),
        jnp.zeros(lead + (rows, width), wide),
        jnp.zeros(lead + (rows, 1), wide),
        jnp.zeros(lead + (rows, width), plain),
        jnp.zeros(lead + (rows, hidden_units), plain),
        jnp.zeros(lead + (rows, width), wide),
        jnp.zeros(lead + (rows, 1), wide),
    )


def layer_forward(inputs, length, mats, gain, bias, expand_shift):
    joint, mixer, expand, contract = mats
    rows, width = inputs.shape
    inputs_low = inputs.astype(jnp.bfloat16)
    project = matmul(inputs_low, joint)

    def split_heads(block):
        return block.astype(jnp.bfloat16).reshape(rows, HEADS, width // HEADS)

    queries = split_heads(project[:, :width] + bias[0])
    keys = split_heads(project[:, width : 2 * width])
    values = split_heads(project[:, 2 * width :] + bias[1])
    scores = key_scores(queries, keys, length)
    peak = jnp.max(scores, axis=-1, keepdims=True)
    powers = jnp.exp(scores - peak)
    total = jnp.sum(powers, axis=-1, keepdims=True)
    attention = powers / total
    log_total = peak + jnp.log(total)
    context = jnp.einsum(
        "hqk,khd->qhd", attention.astype(jnp.bfloat16), values, preferred_element_type=jnp.float32
    )
    context = context.reshape(rows, width).astype(jnp.bfloat16)
    mixed = matmul(context, mixer) + bias[2]
    first, normed_one, scale_one = norm_forward(inputs + mixed, gain[0], bias[3])
    first_low = first.astype(jnp.bfloat16)
    hidden = matmul(first_low, expand) + expand_shift
    active = jax.nn.gelu(hidden, approximate=False).astype(jnp.bfloat16)
    branch = matmul(active, contract) + bias[4]
    output, normed_two, scale_two = norm_forward(first + branch, gain[1], bias[5])
    kept = (
        inputs_low,
        queries,
        keys,
        values,
        log_total,
        context,
        normed_one,
        scale_one,
        first_low,
        active,
        normed_two,
        scale_two,
    )
    return (output, kept)


def layer_backward(grad_out, kept, length, mats, gain, expand_shift):
    joint, mixer, expand, contract = mats
    (
        inputs_low,
        queries,
        keys,
        values,
        log_total,
        context,
        normed_one,
        scale_one,
        first_low,
        active,
        normed_two,
        scale_two,
    ) = kept
    rows, width = inputs_low.shape
    grad_two, gain_two, shift_two = norm_back(grad_out, normed_two, scale_two, gain[1])
    branch_grad = grad_two.astype(jnp.bfloat16)
    contract_part = outer_sum(active, branch_grad)
    hidden = matmul(first_low, expand) + expand_shift
    hidden_grad = (back_mul(branch_grad, contract) * gelu_slope(hidden)).astype(jnp.bfloat16)
    expand_part = outer_sum(first_low, hidden_grad)
    first_grad = grad_two + back_mul(hidden_grad, expand)
    grad_one, gain_one, shift_one = norm_back(first_grad, normed_one, scale_one, gain[0])
    mixed_grad = grad_one.astype(jnp.bfloat16)
    mixer_part = outer_sum(context, mixed_grad)
    context_grad = (
        back_mul(mixed_grad, mixer).astype(jnp.bfloat16).reshape(rows, HEADS, width // HEADS)
    )
    scores = key_scores(queries, keys, length)
    attention = jnp.exp(scores - log_total)
    attention_grad = jnp.einsum(
        "qhd,khd->hqk", context_grad, values, preferred_element_type=jnp.float32
    )
    inner = jnp.sum(attention_grad * attention, axis=-1, keepdims=True)
    score_grad = (attention * (attention_grad - inner)).astype(jnp.bfloat16)
    scale = queries.shape[-1] ** (-0.5)
    query_grad = (
        jnp.einsum("hqk,khd->qhd", score_grad, keys, preferred_element_type=jnp.float32) * scale
    )
    key_grad = (
        jnp.einsum("hqk,qhd->khd", score_grad, queries, preferred_element_type=jnp.float32) * scale
    )
    value_grad = jnp.einsum(
        "hqk,qhd->khd",
        attention.astype(jnp.bfloat16),
        context_grad,
        preferred_element_type=jnp.float32,
    )
    project_grad = jnp.concatenate(
        [
            part.reshape(rows, width).astype(jnp.bfloat16)
            for part in (query_grad, key_grad, value_grad)
        ],
        axis=1,
    )
    joint_part = outer_sum(inputs_low, project_grad)
    input_grad = grad_one + back_mul(project_grad, joint)
    column_sums = jnp.sum(project_grad, axis=0, dtype=jnp.float32)
    bias_part = jnp.stack(
        [
            column_sums[:width],
            column_sums[2 * width :],
            jnp.sum(mixed_grad, axis=0, dtype=jnp.float32),
            shift_one,
            jnp.sum(branch_grad, axis=0, dtype=jnp.float32),
            shift_two,
        ]
    )
    gain_part = jnp.stack([gain_one, gain_two])
    shift_part = jnp.sum(hidden_grad, axis=0, dtype=jnp.float32)
    return (
        input_grad,
        (joint_part, mixer_part, expand_part, contract_part),
        gain_part,
        bias_part,
        shift_part,
    )


def on_device(
    embedded,
    lengths,
    positions,
    labels,
    joint_weight,
    mixer_weight,
    expand_weight,
    contract_weight,
    head_weight,
    gains,
    biases,
    expand_bias,
    word_table,
    word_bias,
):
    section = lax.axis_index("section")
    decoder = section == 1
    inputs_all = embedded[0]
    count, rows, width = inputs_all.shape
    places = positions[0]
    masked = places.shape[-1]
    answers = labels[0].reshape(-1)
    mats = (joint_weight[0], mixer_weight[0], expand_weight[0], contract_weight[0])
    gain = gains[0]
    bias = biases[0]
    expand_shift = expand_bias[0]
    hidden_units = expand_shift.shape[0]
    first_row = (jnp.arange(rows) == 0)[:, None]
    kept_all = kept_blank((count + 1,), rows, width, hidden_units)
    hidden_all = jnp.zeros((count + 1, rows, width), jnp.float32)
    cls_in = jnp.zeros((width,), jnp.bfloat16)
    for step in range(count + 1):
        index = step - section
        valid = (index >= 0) & (index < count)
        slot = jnp.clip(index, 0, count - 1)
        store = jnp.where(valid, slot, count)
        inputs = lax.dynamic_index_in_dim(inputs_all, slot, 0, False).astype(jnp.float32)
        inputs = jnp.where(decoder & first_row, cls_in.astype(jnp.float32)[None, :], inputs)
        length = lengths[slot]

        def compute(operand):
            return layer_forward(operand, length, mats, gain, bias, expand_shift)

        def skip(operand):
            return (jnp.zeros_like(operand), kept_blank((), rows, width, hidden_units))

        output, kept = lax.cond(valid, compute, skip, inputs)
        kept_all = jax.tree.map(
            lambda buffer, value: lax.dynamic_update_index_in_dim(buffer, value, store, 0),
            kept_all,
            kept,
        )
        hidden_all = lax.dynamic_update_index_in_dim(hidden_all, output, store, 0)
        cls_in = passed_along(output[0].astype(jnp.bfloat16), "section", 1)
    picked = jnp.take_along_axis(hidden_all[:count], places[:, :, None], axis=1).reshape(-1, width)
    picked_low = picked.astype(jnp.bfloat16)
    head_matrix = head_weight[0]
    dense = matmul(picked_low, head_matrix) + bias[6]
    head_normed, normed_head, scale_head = norm_forward(
        jax.nn.gelu(dense, approximate=False), gain[2], bias[7]
    )
    head_low = head_normed.astype(jnp.bfloat16)
    slice_rows = word_table.shape[0]
    table_all, shift_all = (
        lax.all_gather(word_table, "dp", axis=0, tiled=True),
        lax.all_gather(word_bias, "dp", axis=0, tiled=True),
    )
    scores = back_mul(head_low, table_all) + shift_all.astype(jnp.float32)
    vocab = scores.shape[1]
    row_count = scores.shape[0]
    peak = jnp.max(scores, axis=-1, keepdims=True)
    log_total = peak + jnp.log(jnp.sum(jnp.exp(scores - peak), axis=-1, keepdims=True))
    label_score = jnp.take_along_axis(scores, answers[:, None], axis=1)[:, 0]
    cross = log_total[:, 0] - label_score
    loss_part = jnp.sum(cross)
    logits_out = scores.astype(jnp.bfloat16).reshape(1, count, masked, vocab)
    probable = jnp.exp(scores - log_total).at[jnp.arange(row_count), answers].add(-1.0)
    score_grad = (probable / masked).astype(jnp.bfloat16)
    word_shift_grad = jnp.sum(score_grad, axis=0, dtype=jnp.float32)
    head_grad = matmul(score_grad, table_all)
    table_grad = lax.psum_scatter(
        outer_sum(score_grad, head_low), "dp", scatter_dimension=0, tiled=True
    )
    act_grad, gain_head, shift_head = norm_back(head_grad, normed_head, scale_head, gain[2])
    dense_grad = (act_grad * gelu_slope(dense)).astype(jnp.bfloat16)
    head_part = outer_sum(picked_low, dense_grad)
    dense_shift = jnp.sum(dense_grad, axis=0, dtype=jnp.float32)
    picked_grad = back_mul(dense_grad, head_matrix).reshape(count, masked, width)
    passage_ids = jnp.arange(count)[:, None]
    head_back = (
        jnp.zeros((count, rows, width), jnp.float32).at[passage_ids, places].add(picked_grad)
    )
    grad_mats = tuple((jnp.zeros(matrix.shape, jnp.float32) for matrix in mats))
    grad_gain = jnp.zeros((2, width), jnp.float32)
    grad_bias = jnp.zeros((6, width), jnp.float32)
    grad_shift = jnp.zeros(expand_shift.shape, jnp.float32)
    input_grads = jnp.zeros((count, rows, width), jnp.float32)
    cls_grad = jnp.zeros((width,), jnp.bfloat16)
    for step in range(count + 1):
        index = step - 1 + section
        valid = (index >= 0) & (index < count)
        slot = jnp.clip(index, 0, count - 1)
        incoming = lax.dynamic_index_in_dim(head_back, slot, 0, False)
        incoming = incoming + jnp.where(first_row, cls_grad.astype(jnp.float32)[None, :], 0.0)
        kept = jax.tree.map(
            lambda buffer: lax.dynamic_index_in_dim(buffer, slot, 0, False), kept_all
        )
        length = lengths[slot]

        def back_compute(operand):
            return layer_backward(operand[0], operand[1], length, mats, gain, expand_shift)

        def back_skip(operand):
            return (
                jnp.zeros((rows, width), jnp.float32),
                tuple((jnp.zeros(matrix.shape, jnp.float32) for matrix in mats)),
                jnp.zeros((2, width), jnp.float32),
                jnp.zeros((6, width), jnp.float32),
                jnp.zeros((hidden_units,), jnp.float32),
            )

        input_grad, mat_parts, gain_part, bias_part, shift_part = lax.cond(
            valid, back_compute, back_skip, (incoming, kept)
        )
        grad_mats = tuple((total + part for total, part in zip(grad_mats, mat_parts)))
        grad_gain = grad_gain + gain_part
        grad_bias = grad_bias + bias_part
        grad_shift = grad_shift + shift_part
        input_grads = input_grads.at[slot].add(jnp.where(decoder & first_row, 0.0, input_grad))
        cls_grad = passed_along(input_grad[0].astype(jnp.bfloat16), "section", -1)
    gain_total = jnp.concatenate([grad_gain, gain_head[None, :]], 0)
    bias_total = jnp.concatenate([grad_bias, dense_shift[None, :], shift_head[None, :]], 0)
    gain_sum, bias_sum, shift_sum, word_sum, loss_sum = lax.psum(
        (gain_total, bias_total, grad_shift, word_shift_grad, loss_part), "dp"
    )
    joint_sum, mixer_sum, expand_sum, contract_sum, head_sum = (
        lax.psum_scatter(grad_mats[0], "dp", scatter_dimension=0, tiled=True),
        lax.psum_scatter(grad_mats[1], "dp", scatter_dimension=0, tiled=True),
        lax.psum_scatter(grad_mats[2], "dp", scatter_dimension=0, tiled=True),
        lax.psum_scatter(grad_mats[3], "dp", scatter_dimension=0, tiled=True),
        lax.psum_scatter(head_part, "dp", scatter_dimension=0, tiled=True),
    )
    word_part = lax.dynamic_slice_in_dim(word_sum, lax.axis_index("dp") * slice_rows, slice_rows)
    table_total, word_total = (
        lax.psum(table_grad.astype(jnp.bfloat16), "section").astype(jnp.float32),
        lax.psum(word_part.astype(jnp.bfloat16), "section").astype(jnp.float32),
    )
    loss = (loss_sum / (count * lax.axis_size("dp") * masked)).reshape(1)
    return (
        loss,
        logits_out,
        input_grads[None],
        joint_sum[None],
        mixer_sum[None],
        expand_sum[None],
        contract_sum[None],
        head_sum[None],
        gain_sum[None],
        bias_sum[None],
        shift_sum[None],
        table_total,
        word_total,
    )


def solution(mesh):
    in_specs = (
        P("section", "dp", None, None),
        P("dp"),
        P("section", "dp", None),
        P("section", "dp", None),
        P("section", None, None),
        P("section", None, None),
        P("section", None, None),
        P("section", None, None),
        P("section", None, None),
        P("section", None, None),
        P("section", None, None),
        P("section", None),
        P("dp", None),
        P("dp"),
    )
    out_specs = (
        P("section"),
        P("section", "dp", None, None),
        P("section", "dp", None, None),
        P("section", "dp", None),
        P("section", "dp", None),
        P("section", "dp", None),
        P("section", "dp", None),
        P("section", "dp", None),
        P("section", None, None),
        P("section", None, None),
        P("section", None),
        P("dp", None),
        P("dp"),
    )
    return jax.shard_map(
        on_device, mesh=mesh, in_specs=in_specs, out_specs=out_specs, check_vma=False
    )
```

profile of v0, /device:TPU:0, one launch (start us, length us, event | category | flops | bytes accessed | tf_op | source)
XLA Modules:
  0.0 1985.8 jit_solution(11036941285950764071)
XLA Ops:
  10.2 65.7 %conditional.6 = (f32[512,768]{1,0:T(8,128)S(1)}, bf16[1,512,768]{2,1,0:T(8,128)(2,1)}, bf16[1,512,12,64]{1,3,2,0:T(8,128)(2,1)}, bf16[1,512,12,64]{1,3,2,0:T(8,...) conditional(s32[]{:T(128)} %convert_element_type.537, ...), branch_computations={%region_0.1_spmd, %region_1.8_spmd} | conditional | flops 8209952256 | bytes 139557216 | solution.py:263
  48.8 19.0 fusion.4
  86.1 23.9 %all-gather = bf16[16,1,1920]{2,1,0:T(2,128)(2,1)S(1)} all-gather(bf16[1,1,1920]{2,1,0:T(2,128)(2,1)S(1)} %reshape.962), channel_id=1, replica_groups=mesh['section'=2,'dp'=16] {'dp'}, dimensions={0}, use_global_device_ids=true | all-gather | bytes 65280 | tf_op jit(solution)/shard_map/all_gather | solution.py:282
  112.1 55.1 %conditional.7 = (f32[512,768]{1,0:T(8,128)S(1)}, bf16[1,512,768]{2,1,0:T(8,128)(2,1)}, bf16[1,512,12,64]{1,3,2,0:T(8,128)(2,1)}, bf16[1,512,12,64]{1,3,2,0:T(8,...) conditional(s32[]{:T(128)} %convert_element_type.538, ...), branch_computations={%region_8.9_spmd, %region_9.16_spmd} | conditional | flops 8210738688 | bytes 146251584 | solution.py:263
  144.3 17.0 fusion.26
  169.9 19.8 conditional.8
  199.0 46.3 %all-gather.3.cloned.1.call-done = bf16[30720,768]{1,0:T(8,128)(2,1)} async-done(((bf16[1920,768]{1,0:T(8,128)(2,1)}), bf16[30720,768]{1,0:T(8,128)(2,1)}) %all-gather.3.cloned.1.call-update) | async-done | bytes 47185936 | tf_op jit(solution)/shard_map/all_gather | solution.py:281
  245.3 25.4 %fusion.328 = (f32[128]{0:T(128)S(1)}, f32[128,30720]{1,0:T(8,128)}) fusion(f32[30720]{0:T(1024)S(1)} %bitcast.537, bf16[30720,768]{1,0:T(8,128)(2,1)} %all-gather.3.cloned.1.call-done, f32[128,768]{1,0:T(8,128)S(1)} %get-tuple-element.1448, f32[768]{0:T(1024)S(1)} %copy-done.71, f32[768]{0:T(1024)S(1)} %copy-done.70, f32[128]{0:T(128)S(1)} %add_rsqrt_fusion.6, ...), kind=kOutput, calls=%fused_computation.642 | convolution fusion | flops 6048153600 | bytes 63438336 | tf_op jit(solution)/shard_map/dot_general | solution.py:31
  272.8 7.8 exponential_reduce_fusion
  281.2 20.3 %fusion.327 = (bf16[128,30720]{1,0:T(8,128)(2,1)}, f32[128,30720]{1,0:T(8,128)}) fusion(f32[128,30720]{1,0:T(8,128)} %get-tuple-element.1531, f32[128]{0:T(128)S(1)} %get-tuple-element.1446), kind=kLoop, calls=%fused_computation.641 | loop fusion | flops 7864320 | bytes 39322112 | tf_op jit(solution)/shard_map/convert_element_type | solution.py:292
  301.5 16.0 scatter_fusion
  317.5 37.3 %fusion.307 = f32[30720,768]{1,0:T(8,128)} fusion(f32[128,768]{1,0:T(8,128)S(1)} %get-tuple-element.1448, f32[768]{0:T(1024)S(1)} %copy-done.71, f32[768]{0:T(1024)S(1)} %copy-done.70, f32[128]{0:T(128)S(1)} %add_rsqrt_fusion.6, f32[128]{0:T(128)S(1)} %broadcast_multiply_fusion.20, f32[128,30720]{1,0:T(8,128)} %scatter_fusion), kind=kOutput, calls=%fused_computation.629 | convolution fusion | flops 6048153600 | bytes 110500864 | tf_op jit(solution)/shard_map/dot_general | solution.py:25
  409.6 801.7 %reduce-scatter.17.cloned.1.call-done = f32[1920,768]{1,0:T(8,128)} async-done(((f32[30720,768]{1,0:T(8,128)}), f32[1920,768]{1,0:T(8,128)}) %reduce-scatter.17.cloned.1.call-update) | async-done | bytes 5898256 | tf_op jit(solution)/shard_map/reduce_scatter | solution.py:297
  1216.0 23.9 %multiply_reduce_fusion.14 = (f32[768]{0:T(1024)}, f32[128]{0:T(128)}, f32[128]{0:T(128)}, f32[768]{0:T(1024)}, f32[128,768]{1,0:T(8,128)}) fusion(f32[128,768]{1,0:T(8,128)} %copy-done.12, f32[128]{0:T(128)} %copy-done.89, f32[128]{0:T(128)} %copy-done.88, f32[768]{0:T(1024)S(1)} %copy-done.70, bf16[30720,768]{1,0:T(8,128)(2,1)} %all-gather.3.cloned.1.call-done, ...), kind=kOutput, calls=%fused_computation.507 | convolution fusion | flops 6048544768 | bytes 63712256 | tf_op jit(solution)/shard_map/dot_general | solution.py:21
  1277.5 17.7 scatter_fusion.1
  1295.2 22.3 %conditional.9 = (f32[512,768]{1,0:T(8,128)}, f32[768,2304]{1,0:T(8,128)}, f32[768,768]{1,0:T(8,128)}, f32[768,3072]{1,0:T(8,128)}, f32[3072,768]{1,0:T(8,128)},...) conditional(s32[]{:T(128)} %convert_element_type.549, () %tuple.172, (f32[3,512,1]{1,2,0:T(1,128)}, ...), branch_computations={%region_35.36_spmd, %region_36.0_spmd} | conditional | flops 19033214976 | bytes 318239200 | solution.py:338
  1319.6 75.5 %collective-permute-done.2 = bf16[768]{0:T(1024)(128)(2,1)S(1)} collective-permute-done((bf16[768]{0:T(1024)(128)(2,1)S(1)}, bf16[768]{0:T(1024)(128)(2,1)S(1)}, u32[]{:S(2)}, u32[]{:S(2)}) %collective-permute-start.2) | collective-permute-done | bytes 1568 | tf_op jit(solution)/shard_map/ppermute | solution.py:17
  1396.0 93.2 %conditional.10 = (f32[512,768]{1,0:T(8,128)}, f32[768,2304]{1,0:T(8,128)}, f32[768,768]{1,0:T(8,128)}, f32[768,3072]{1,0:T(8,128)}, f32[3072,768]{1,0:T(8,128)}...) conditional(s32[]{:T(128)} %convert_element_type.552, () %tuple.174, (f32[3,512,1]{1,2,0:T(1,128)}, ...), branch_computations={%region_51.52_spmd, %region_52.66_spmd} | conditional | flops 19032035328 | bytes 306093056 | solution.py:338
  1406.3 8.6 fusion.155
  1440.2 8.5 fusion.180
  1454.8 8.7 multiply_reduce_fusion.8
  1495.5 89.6 %conditional.11 = (f32[512,768]{1,0:T(8,128)}, f32[768,2304]{1,0:T(8,128)}, f32[768,768]{1,0:T(8,128)S(1)}, f32[768,3072]{1,0:T(8,128)}, f32[3072,768]{1,0:T(8,1...) conditional(s32[]{:T(128)} %convert_element_type.555, () %tuple.176, (f32[3,512,1]{1,2,0:T(1,128)}, ...), branch_computations={%region_67.68_spmd, %region_68.82_spmd} | conditional | flops 19032035328 | bytes 321821792 | solution.py:338
  1504.9 8.8 fusion.218
  1537.1 8.5 fusion.243
  1551.8 8.6 multiply_reduce_fusion.11
  1589.4 11.5 add_add_fusion.6
  1601.0 15.3 add_add_fusion.5
  1616.4 14.0 add_add_fusion.4
  1646.8 61.0 %all-reduce.5 = (f32[]{:T(128)}, f32[1,3,768]{2,0,1:T(1,128)}, f32[1,8,768]{2,1,0:T(8,128)}, f32[1,3072]{1,0:T(1,128)}, bf16[30720]{0:T(1024)(128)(2,1)S(1)}) all-reduce(f32[]{:T(128)} %get-tuple-element.1445, f32[1,3,768]{2,0,1:T(1,128)S(1)} %broadcast_in_dim.599, ...), channel_id=1, replica_groups=mesh['section'=2,'dp'=16] {'dp'}, use_global_device_ids=true, to_apply=%region_29.30 | all-reduce | flops 42241 | bytes 276488 | tf_op jit(solution)/shard_map/psum | solution.py:349
  1722.9 22.5 %reduce-scatter.7.cloned.1.call-done = f32[48,2304]{1,0:T(8,128)} async-done(((f32[768,2304]{1,0:T(8,128)}), f32[48,2304]{1,0:T(8,128)}) %reduce-scatter.7.cloned.1.call-update) | async-done | bytes 442384 | tf_op jit(solution)/shard_map/reduce_scatter | solution.py:353
  1745.4 115.6 %reduce-scatter.11.cloned.1.call-done = f32[48,3072]{1,0:T(8,128)} async-done(((f32[768,3072]{1,0:T(8,128)}), f32[48,3072]{1,0:T(8,128)}) %reduce-scatter.11.cloned.1.call-update) | async-done | bytes 589840 | tf_op jit(solution)/shard_map/reduce_scatter | solution.py:355
  1861.0 116.4 %reduce-scatter.13.cloned.1.call-done = f32[192,768]{1,0:T(8,128)} async-done(((f32[3072,768]{1,0:T(8,128)}), f32[192,768]{1,0:T(8,128)}) %reduce-scatter.13.cloned.1.call-update) | async-done | bytes 589840 | tf_op jit(solution)/shard_map/reduce_scatter | solution.py:356
  (521 shorter events, 413.4 us)
Async XLA Ops:
  7.2 190.0 %copy-start = (bf16[1,768,768]{2,1,0:T(8,128)(2,1)S(1)}, bf16[1,768,768]{2,1,0:T(8,128)(2,1)}, u32[]{:S(2)}) copy-start(bf16[1,768,768]{2,1,0:T(8,128)(2,1)} %param.40) | copy-start | bytes 3538948
  7.2 238.1 %all-gather.3.cloned.1.call-start = ((), (), s32[]{:S(2)}) async-start(), calls=%async_computation.6 | async-start | bytes 50135040 | tf_op jit(solution)/shard_map/all_gather | solution.py:281
  8.0 1203.3 %reduce-scatter.17.cloned.1.call-start = ((), (), s32[]{:S(2)}) async-start(), calls=%async_computation.12 | async-start | bytes 100270080 | tf_op jit(solution)/shard_map/reduce_scatter | solution.py:297
  8.7 161.1 %copy-start.61 = (f32[1,3,768]{2,1,0:T(4,128)}, f32[1,3,768]{2,1,0:T(4,128)S(1)}, u32[]{:S(2)}) copy-start(f32[1,3,768]{2,1,0:T(4,128)S(1)} %copy.173) | copy-start | bytes 27652
  9.1 69.5 %copy-start.109 = (s32[1,2,64]{2,1,0:T(2,128)S(1)}, s32[1,2,64]{2,1,0:T(2,128)}, u32[]{:S(2)}) copy-start(s32[1,2,64]{2,1,0:T(2,128)} %param.35) | copy-start | bytes 1540
  9.1 69.7 %copy-start.92 = (bf16[1920]{0:T(1024)(128)(2,1)S(1)}, bf16[1920]{0:T(1024)(128)(2,1)}, u32[]{:S(2)}) copy-start(bf16[1920]{0:T(1024)(128)(2,1)} %param.45) | copy-start | bytes 11524
  9.1 71.6 %copy-start.96 = (s32[1,2,64]{2,1,0:T(2,128)S(1)}, s32[1,2,64]{2,1,0:T(2,128)}, u32[]{:S(2)}) copy-start(s32[1,2,64]{2,1,0:T(2,128)} %param.34) | copy-start | bytes 1540
  45.3 22.6 %copy-start.77 = (f32[512]{0:T(512)}, f32[512]{0:T(512)S(1)}, u32[]{:S(2)}) copy-start(f32[512]{0:T(512)S(1)} %add_rsqrt_fusion.1) | copy-start | bytes 6148 | tf_op jit(solution)/shard_map/cond
  45.3 22.6 %slice-start.10 = ((s8[4718592]{0:T(1024)(128)(4,1)}), s8[4194304]{0:T(1024)(128)(4,1)S(1)}, s32[]{:S(2)}) async-start(s8[4718592]{0:T(1024)(128)(4,1)} %bitcast.565), calls=%async_computation.24 | async-start | bytes 8388608 | tf_op jit(solution)/shard_map/cond
  76.0 36.1 %copy-start.64 = (f32[1,12,512,1]{2,1,3,0:T(8,128)}, f32[1,12,512,1]{2,1,3,0:T(8,128)S(1)}, u32[]{:S(2)}) copy-start(f32[1,12,512,1]{2,1,3,0:T(8,128)S(1)} %get-tuple-element.1204) | copy-start | bytes 73732
  76.0 36.1 %copy-start.79 = (f32[1,512,1]{1,2,0:T(1,128)}, f32[1,512,1]{1,2,0:T(1,128)S(1)}, u32[]{:S(2)}) copy-start(f32[1,512,1]{1,2,0:T(1,128)S(1)} %get-tuple-element.1183) | copy-start | bytes 6148
  77.1 34.9 %collective-permute-start = (bf16[768]{0:T(1024)(128)(2,1)S(1)}, bf16[768]{0:T(1024)(128)(2,1)S(1)}, u32[]{:S(2)}, u32[]{:S(2)}) collective-permute-start(bf16[768]{0:T(1024)(128)(2,1)S(1)} %fusion.298), channel_id=1, source_target_pairs={{0,16},{1,17},{2,18},{3,19},{4,20},{5,21},{6,22},{7,23},{8,24},{9,... | collective-permute-start | bytes 4616 | tf_op jit(solution)/shard_map/ppermute | solution.py:17
  167.3 2.6 collective-permute-start.1
  197.2 48.1 %copy-start.56 = (f32[16,1,1920]{2,1,0:T(1,128)S(1)}, f32[16,1,1920]{2,1,0:T(1,128)}, u32[]{:S(2)}) copy-start(f32[16,1,1920]{2,1,0:T(1,128)} %convert_element_type.568) | copy-start | bytes 368644
  197.2 48.1 %copy-start.70 = (f32[768]{0:T(1024)S(1)}, f32[768]{0:T(1024)}, u32[]{:S(2)}) copy-start(f32[768]{0:T(1024)} %slice_reduce_fusion.31) | copy-start | bytes 9220
  197.2 48.1 %copy-start.71 = (f32[768]{0:T(1024)S(1)}, f32[768]{0:T(1024)}, u32[]{:S(2)}) copy-start(f32[768]{0:T(1024)} %get-tuple-element.1420) | copy-start | bytes 9220
  198.8 118.7 %copy-start.12 = (f32[128,768]{1,0:T(8,128)}, f32[128,768]{1,0:T(8,128)S(1)}, u32[]{:S(2)}) copy-start(f32[128,768]{1,0:T(8,128)S(1)} %get-tuple-element.1448) | copy-start | bytes 1179652
  198.8 118.7 %copy-start.88 = (f32[128]{0:T(128)}, f32[128]{0:T(128)S(1)}, u32[]{:S(2)}) copy-start(f32[128]{0:T(128)S(1)} %broadcast_multiply_fusion.20) | copy-start | bytes 1540
  199.0 118.5 %copy-start.89 = (f32[128]{0:T(128)}, f32[128]{0:T(128)S(1)}, u32[]{:S(2)}) copy-start(f32[128]{0:T(128)S(1)} %add_rsqrt_fusion.6) | copy-start | bytes 1540
  245.3 25.4 %copy-start.16 = (s32[128]{0:T(128)S(1)}, s32[128]{0:T(128)}, u32[]{:S(2)}) copy-start(s32[128]{0:T(128)} %get-tuple-element.1534) | copy-start | bytes 1540
  281.2 20.3 %copy-start.15 = (s32[128]{0:T(128)S(1)}, s32[128]{0:T(128)}, u32[]{:S(2)}) copy-start(s32[128]{0:T(128)} %get-tuple-element.1533) | copy-start | bytes 1540
  354.8 1363.2 %all-reduce.4.cloned.1.call-start = ((), (), s32[]{:S(2)}) async-start(), calls=%async_computation.13 | async-start | bytes 5898240 | tf_op jit(solution)/shard_map/psum | solution.py:361
  1215.9 507.0 %reduce-scatter.15.cloned.1.call-start = ((), (), s32[]{:S(2)}) async-start(), calls=%async_computation.11 | async-start | bytes 2506752 | tf_op jit(solution)/shard_map/reduce_scatter | solution.py:357
  1247.0 475.9 %reduce-scatter.9.cloned.1.call-start = ((), (), s32[]{:S(2)}) async-start(), calls=%async_computation.8 | async-start | bytes 2506752 | tf_op jit(solution)/shard_map/reduce_scatter | solution.py:354
  1295.2 100.0 %copy-start.3 = (f32[512,768]{1,0:T(8,128)S(1)}, f32[512,768]{1,0:T(8,128)}, u32[]{:S(2)}) copy-start(f32[512,768]{1,0:T(8,128)} %copy-done.2) | copy-start | bytes 4718596
  1318.3 76.8 %collective-permute-start.2 = (bf16[768]{0:T(1024)(128)(2,1)S(1)}, bf16[768]{0:T(1024)(128)(2,1)S(1)}, u32[]{:S(2)}, u32[]{:S(2)}) collective-permute-start(bf16[768]{0:T(1024)(128)(2,1)S(1)} %fusion.296), channel_id=1, source_target_pairs={{16,0},{17,1},{18,2},{19,3},{20,4},{21,5},{22,6},{23,7},{24,8},{25... | collective-permute-start | bytes 4616 | tf_op jit(solution)/shard_map/ppermute | solution.py:17
  1454.8 24.9 %copy-start.51 = (bf16[12,64,512]{2,1,0:T(8,128)(2,1)}, bf16[12,64,512]{2,1,0:T(8,128)(2,1)S(1)}, u32[]{:S(2)}) copy-start(bf16[12,64,512]{2,1,0:T(8,128)(2,1)S(1)} %fusion.166) | copy-start | bytes 2359300 | tf_op jit(solution)/shard_map/cond
  1490.0 5.5 collective-permute-start.3
  1551.8 25.1 %copy-start.52 = (bf16[12,64,512]{2,1,0:T(8,128)(2,1)}, bf16[12,64,512]{2,1,0:T(8,128)(2,1)S(1)}, u32[]{:S(2)}) copy-start(bf16[12,64,512]{2,1,0:T(8,128)(2,1)S(1)} %fusion.229) | copy-start | bytes 2359300 | tf_op jit(solution)/shard_map/cond
  1589.3 156.1 %reduce-scatter.7.cloned.1.call-start = ((), (), s32[]{:S(2)}) async-start(), calls=%async_computation.7 | async-start | bytes 7520256 | tf_op jit(solution)/shard_map/reduce_scatter | solution.py:353
  1600.9 260.1 %reduce-scatter.11.cloned.1.call-start = ((), (), s32[]{:S(2)}) async-start(), calls=%async_computation.9 | async-start | bytes 10027008 | tf_op jit(solution)/shard_map/reduce_scatter | solution.py:355
  1616.3 361.1 %reduce-scatter.13.cloned.1.call-start = ((), (), s32[]{:S(2)}) async-start(), calls=%async_computation.10 | async-start | bytes 10027008 | tf_op jit(solution)/shard_map/reduce_scatter | solution.py:356
  (94 other events, 559.4 us)
Sparse Core Ops, SparseCore 0:
  9.7 235.6 all-gather.2
  355.0 856.3 reduce-scatter.16
  1216.0 80.6 all-reduce.3
  1301.4 62.9 reduce-scatter.14
  1589.5 61.8 reduce-scatter.8
  1656.3 89.0 reduce-scatter.6
  1750.1 110.8 reduce-scatter.10
  1866.3 111.0 reduce-scatter.12
where the time goes:
time: 2000 us; the launch traced here: 1990 us
  waiting for transfers between devices  1180 us (59%)
  matrix products  298 us (15%)
  other arithmetic  199 us (10%)
  local copies, waits for them, and re-layouts  177 us (9%)
  blocking collectives  89.8 us (4%)
    reduce_scatter x1, waiting for transfers between devices, on_device(): lax.psum_scatter(outer_sum(score_grad, head_low), 'dp', scatter_dimension...  802 us
    reduce_scatter x1, waiting for transfers between devices, on_device(): lax.psum_scatter(grad_mats[3], 'dp', scatter_dimension=0, tiled=True)  116 us
    reduce_scatter x1, waiting for transfers between devices, on_device(): lax.psum_scatter(grad_mats[2], 'dp', scatter_dimension=0, tiled=True)  116 us
    dot_general x10, matrix products, outer_sum(): lax.dot_general(left, right, (((0,), (0,)), ((), ())), preferred_element_...  95.6 us
    dot_general x12, matrix products, matmul(): return jnp.dot(left, right, preferred_element_type=jnp.float32)  90 us
    ppermute x4, waiting for transfers between devices, passed_along(): return lax.ppermute(block, axis, route)  79.7 us
    psum x1, blocking collectives, on_device(): lax.psum((gain_total, bias_total, grad_shift, word_shift_grad, loss_part)...  61 us
    dynamic_update_slice x32, local copies, waits for them, and re-layouts, on_device(): lax.dynamic_update_index_in_dim(buffer, value, store, 0)  58.8 us
  transfers between devices with their start and end apart: 12, of which 7 were waited for; matrix products, arithmetic and copies ran while one was open for 28% of the time, Pallas kernels for 0%

commit v1 on v0

v1 whole, which is shorter than its diff:
```python
import functools

import jax
import jax.numpy as jnp
from jax import lax
from jax.experimental import pallas as pl
from jax.experimental.pallas import tpu as pltpu
from jax.sharding import PartitionSpec as P

HEADS = 12
EPS = 1e-12
ROOT_HALF = 0.7071067811865476
INV_ROOT_TAU = 0.3989422804014327
HIDDEN = -1000000000.0
LANES = 128
VMEM = 56 * 1024 * 1024
F32 = jnp.float32
BF16 = jnp.bfloat16


def product(left, right, left_dim, right_dim):
    return lax.dot_general(
        left, right, (((left_dim,), (right_dim,)), ((), ())), preferred_element_type=F32
    )


def matmul(left, right):
    return product(left, right, 1, 0)


def outer_sum(left, right):
    return product(left, right, 0, 0)


def back_mul(left, right):
    return product(left, right, 1, 1)


def passed_along(block, axis, distance):
    devices = range(lax.axis_size(axis))
    route = [(i - distance, i) for i in devices if i - distance in devices]
    return lax.ppermute(block, axis, route)


def swapped(block, bit):
    devices = range(lax.axis_size("dp"))
    return lax.ppermute(block, "dp", [(i, i ^ bit) for i in devices])


def bits_of(order):
    return [1 << i for i in range(order.bit_length() - 1)]


def gather_all(block):
    place = lax.axis_index("dp")
    shape = block.shape
    block = block[None]
    for bit in reversed(bits_of(lax.axis_size("dp"))):
        other = swapped(block, bit)
        low = (place & bit) == 0
        pair = [jnp.where(low, block, other), jnp.where(low, other, block)]
        block = jnp.stack(pair, axis=1).reshape((-1,) + shape)
    return block.reshape((-1,) + shape[1:])


def gather_near(block):
    near = lax.axis_size("dp") // 2
    parts = [block] + [swapped(block, mask) for mask in range(2, near, 2)]
    block = jnp.stack(parts)
    return jnp.stack([block, swapped(block, 1)], axis=1).reshape((near,) + parts[0].shape)


def scatter_near(blocks):
    blocks = blocks.reshape((-1, 2) + blocks.shape[1:])
    got = swapped(blocks[:, 1], 1)
    blocks = (blocks[:, 0].astype(F32) + got.astype(F32)).astype(BF16)
    total = blocks[0].astype(F32)
    for i in range(1, blocks.shape[0]):
        total = total + swapped(blocks[i], 2 * i).astype(F32)
    return total


def normalise(resid):
    centre = resid - jnp.mean(resid, axis=-1, keepdims=True)
    scale_inv = lax.rsqrt(jnp.mean(centre * centre, axis=-1, keepdims=True) + EPS)
    return centre * scale_inv, scale_inv


def norm_back(scaled, normed, scale_inv):
    first_mean = jnp.mean(scaled, axis=-1, keepdims=True)
    second_mean = jnp.mean(scaled * normed, axis=-1, keepdims=True)
    return scale_inv * (scaled - first_mean - normed * second_mean)


def gelu_and_slope(value):
    gate = 0.5 * (1.0 + lax.erf(value * ROOT_HALF))
    return value * gate, gate + value * jnp.exp(-0.5 * value * value) * INV_ROOT_TAU


def attend_kernel(lengths, q_ref, k_ref, v_ref, out_ref, log_ref, *, head_dim):
    length = lengths[pl.program_id(0)]
    rows, lanes = q_ref.shape
    q = q_ref[...] * (head_dim**-0.5)
    k = k_ref[...]
    v_t = v_ref[...].T
    head_of = lax.broadcasted_iota(jnp.int32, (rows, lanes), 1) // head_dim
    visible = lax.broadcasted_iota(jnp.int32, (rows, rows), 0) < length
    parts = []
    for head in range(lanes // head_dim):
        scores = back_mul(k, jnp.where(head_of == head, q, jnp.zeros_like(q)))
        scores = jnp.where(visible, scores, HIDDEN)
        peak = jnp.max(scores, axis=0, keepdims=True)
        powers = jnp.exp(scores - peak)
        total = jnp.sum(powers, axis=0, keepdims=True)
        piece = matmul(v_t[head * head_dim : (head + 1) * head_dim], powers.astype(BF16))
        parts.append(piece / total)
        log_ref[0, head : head + 1, :] = peak + jnp.log(total)
    out_ref[...] = jnp.concatenate(parts, axis=0).T.astype(BF16)


def attend(qkv, lengths, count):
    rows = qkv.shape[0] // count
    width = qkv.shape[1] // 3
    pairs = width // LANES
    head_dim = width // HEADS
    block = lambda part: pl.BlockSpec((rows, LANES), lambda b, p, _: (b, part * pairs + p))
    return pl.pallas_call(
        functools.partial(attend_kernel, head_dim=head_dim),
        grid_spec=pltpu.PrefetchScalarGridSpec(
            num_scalar_prefetch=1,
            grid=(count, pairs),
            in_specs=[block(0), block(1), block(2)],
            out_specs=[
                pl.BlockSpec((rows, LANES), lambda b, p, _: (b, p)),
                pl.BlockSpec((1, LANES // head_dim, rows), lambda b, p, _: (b * pairs + p, 0, 0)),
            ],
        ),
        out_shape=[
            jax.ShapeDtypeStruct((count * rows, width), BF16),
            jax.ShapeDtypeStruct((count * pairs, LANES // head_dim, rows), F32),
        ],
        compiler_params=pltpu.CompilerParams(vmem_limit_bytes=VMEM),
        name="attend",
    )(lengths, qkv, qkv, qkv)


def attend_back_kernel(lengths, q_ref, k_ref, v_ref, grad_ref, log_ref, *refs, head_dim, passage):
    out_ref = refs[-1]
    length = lengths[passage]
    rows, lanes = q_ref.shape
    scale = head_dim**-0.5
    q = q_ref[...] * scale
    k = k_ref[...]
    v = v_ref[...]
    grad = grad_ref[...]
    head_of = lax.broadcasted_iota(jnp.int32, (rows, lanes), 1) // head_dim
    visible = lax.broadcasted_iota(jnp.int32, (rows, rows), 0) < length
    totals = [jnp.zeros((rows, lanes), F32)] * 3
    for head in range(lanes // head_dim):
        mine = head_of == head
        scores = back_mul(k, jnp.where(mine, q, jnp.zeros_like(q)))
        share = jnp.where(visible, jnp.exp(scores - log_ref[0, head : head + 1, :]), 0.0)
        share_grad = back_mul(jnp.where(mine, v, jnp.zeros_like(v)), grad)
        inner = jnp.sum(share * share_grad, axis=0, keepdims=True)
        score_grad = (share * (share_grad - inner)).astype(BF16)
        parts = (
            outer_sum(score_grad, k) * scale,
            matmul(score_grad, q),
            matmul(share.astype(BF16), grad),
        )
        totals = [jnp.where(mine, part, total) for part, total in zip(parts, totals)]
    for i, total in enumerate(totals):
        out_ref[i] = total.astype(BF16)


def attend_back(qkv, grad, logs, lengths, passage, done=()):
    count = lengths.shape[0]
    rows = qkv.shape[0] // count
    width = qkv.shape[1] // 3
    pairs = width // LANES
    head_dim = width // HEADS
    block = lambda part: pl.BlockSpec((rows, LANES), lambda p, _: (passage, part * pairs + p))
    return pl.pallas_call(
        functools.partial(attend_back_kernel, head_dim=head_dim, passage=passage),
        grid_spec=pltpu.PrefetchScalarGridSpec(
            num_scalar_prefetch=1,
            grid=(pairs,),
            in_specs=[
                block(0),
                block(1),
                block(2),
                block(0),
                pl.BlockSpec((1, LANES // head_dim, rows), lambda p, _: (passage * pairs + p, 0, 0)),
            ]
            + [pl.BlockSpec(memory_space=pl.ANY)] * len(done),
            out_specs=pl.BlockSpec((3, rows, LANES), lambda p, _: (0, passage, p)),
        ),
        out_shape=jax.ShapeDtypeStruct((3, count * rows, width), BF16),
        input_output_aliases={6: 0} if done else {},
        compiler_params=pltpu.CompilerParams(vmem_limit_bytes=VMEM),
        name="attend_back",
    )(lengths, qkv, qkv, qkv, grad, logs, *done)


def tail_kernel(
    ctx_ref, x_ref, mixer_ref, expand_ref, contract_ref, gain_ref, bias_ref, shift_ref,
    y_ref, normed_one_ref, scale_one_ref, first_ref, active_ref, slope_ref, normed_two_ref, scale_two_ref,
    *, chunk,
):
    mixed = matmul(ctx_ref[...], mixer_ref[...]) + bias_ref[2:3]
    normed, scale = normalise(x_ref[...].astype(F32) + mixed)
    first = normed * gain_ref[0:1] + bias_ref[3:4]
    first_low = first.astype(BF16)
    normed_one_ref[...] = normed.astype(BF16)
    scale_one_ref[...] = jnp.broadcast_to(scale, scale_one_ref.shape)
    first_ref[...] = first_low
    total = first + bias_ref[4:5]
    for start in range(0, expand_ref.shape[1], chunk):
        part = slice(start, start + chunk)
        hidden = matmul(first_low, expand_ref[:, part]) + shift_ref[0:1, part]
        active, slope = gelu_and_slope(hidden)
        active = active.astype(BF16)
        active_ref[:, part] = active
        slope_ref[:, part] = slope.astype(BF16)
        total = total + matmul(active, contract_ref[part, :])
    normed, scale = normalise(total)
    normed_two_ref[...] = normed.astype(BF16)
    scale_two_ref[...] = jnp.broadcast_to(scale, scale_two_ref.shape)
    y_ref[...] = (normed * gain_ref[1:2] + bias_ref[5:6]).astype(BF16)


def whole(array):
    return pl.BlockSpec(array.shape, lambda *_: (0,) * array.ndim, pipeline_mode=pl.Buffered(1))


def layer_tail(ctx, x, mats, gain, bias, shift, step=256, chunk=3072):
    rows, width = x.shape
    hidden = shift.shape[1]
    step = min(step, rows)
    by_row = lambda n: pl.BlockSpec((step, n), lambda i: (i, 0))
    shape = lambda n, kind: jax.ShapeDtypeStruct((rows, n), kind)
    widths = [(width, BF16), (width, BF16), (LANES, F32), (width, BF16), (hidden, BF16), (hidden, BF16), (width, BF16), (LANES, F32)]
    return pl.pallas_call(
        functools.partial(tail_kernel, chunk=min(chunk, hidden)),
        grid=(rows // step,),
        in_specs=[by_row(width), by_row(width)] + [whole(m) for m in mats + (gain, bias, shift)],
        out_specs=[by_row(n) for n, _ in widths],
        out_shape=[shape(n, kind) for n, kind in widths],
        compiler_params=pltpu.CompilerParams(vmem_limit_bytes=VMEM),
        name="layer_tail",
    )(ctx, x, *mats, gain, bias, shift)


def tail_back_kernel(
    grad_ref, normed_two_ref, scale_two_ref, slope_ref, normed_one_ref, scale_one_ref,
    mixer_ref, expand_ref, contract_ref, gain_ref,
    branch_ref, hidden_ref, one_ref, mixed_ref, ctx_ref, sums_ref, shift_sum_ref,
    *, chunk,
):
    @pl.when(pl.program_id(0) == 0)
    def _():
        sums_ref[...] = jnp.zeros_like(sums_ref)
        shift_sum_ref[...] = jnp.zeros_like(shift_sum_ref)

    def add_sum(row, value):
        sums_ref[row : row + 1] += jnp.sum(value, axis=0, keepdims=True)

    grad = grad_ref[...]
    normed = normed_two_ref[...].astype(F32)
    add_sum(0, grad * normed)
    add_sum(1, grad)
    total = norm_back(grad * gain_ref[1:2], normed, scale_two_ref[:, 0:1])
    branch = total.astype(BF16)
    branch_ref[...] = branch
    add_sum(2, branch.astype(F32))
    for start in range(0, expand_ref.shape[1], chunk):
        part = slice(start, start + chunk)
        hidden = back_mul(branch, contract_ref[part, :]) * slope_ref[:, part].astype(F32)
        hidden = hidden.astype(BF16)
        hidden_ref[:, part] = hidden
        shift_sum_ref[0:1, part] += jnp.sum(hidden.astype(F32), axis=0, keepdims=True)
        total = total + back_mul(hidden, expand_ref[:, part])
    normed = normed_one_ref[...].astype(F32)
    add_sum(3, total * normed)
    add_sum(4, total)
    total = norm_back(total * gain_ref[0:1], normed, scale_one_ref[:, 0:1])
    one_ref[...] = total
    mixed = total.astype(BF16)
    mixed_ref[...] = mixed
    add_sum(5, mixed.astype(F32))
    ctx_ref[...] = back_mul(mixed, mixer_ref[...]).astype(BF16)


def tail_back(grad, kept, mats, gain, step=256, chunk=3072):
    rows, width = grad.shape
    hidden = mats[1].shape[1]
    step = min(step, rows)
    by_row = lambda n: pl.BlockSpec((step, n), lambda i: (i, 0))
    shape = lambda n, kind: jax.ShapeDtypeStruct((rows, n), kind)
    widths = [(width, BF16), (hidden, BF16), (width, F32), (width, BF16), (width, BF16)]
    return pl.pallas_call(
        functools.partial(tail_back_kernel, chunk=min(chunk, hidden)),
        grid=(rows // step,),
        in_specs=[by_row(array.shape[1]) for array in (grad,) + kept] + [whole(m) for m in mats + (gain,)],
        out_specs=[by_row(n) for n, _ in widths]
        + [pl.BlockSpec((8, width), lambda i: (0, 0)), pl.BlockSpec((1, hidden), lambda i: (0, 0))],
        out_shape=[shape(n, kind) for n, kind in widths]
        + [jax.ShapeDtypeStruct((8, width), F32), jax.ShapeDtypeStruct((1, hidden), F32)],
        compiler_params=pltpu.CompilerParams(vmem_limit_bytes=VMEM),
        name="tail_back",
    )(grad, *kept, *mats, gain)


PACK = 16


def first_block(rows, width, passage):
    return pl.BlockSpec((PACK, width), lambda *_: (passage * rows // PACK, 0))


def packed(refs):
    rows = [ref[...].astype(F32)[0:1] for ref in refs]
    place = lax.broadcasted_iota(jnp.int32, (PACK, rows[0].shape[1]), 0)
    total = jnp.zeros((PACK, rows[0].shape[1]), F32)
    for i, row in enumerate(rows):
        total = jnp.where(place == i, row, total)
    return total


def per_head(row, head_dim):
    shape = (PACK, row.shape[1])
    mine = lax.broadcasted_iota(jnp.int32, shape, 1) // head_dim == lax.broadcasted_iota(jnp.int32, shape, 0)
    return jnp.where(mine, row, 0.0)


def heads_joined(block, head_dim):
    mine = lax.broadcasted_iota(jnp.int32, block.shape, 1) // head_dim == lax.broadcasted_iota(jnp.int32, block.shape, 0)
    return jnp.sum(jnp.where(mine, block, 0.0), axis=0, keepdims=True)


def first_share(query, keys, length):
    scores = back_mul(query, keys)
    visible = lax.broadcasted_iota(jnp.int32, scores.shape, 1) < length
    scores = jnp.where(visible, scores, HIDDEN)
    powers = jnp.exp(scores - jnp.max(scores, axis=1, keepdims=True))
    return powers / jnp.sum(powers, axis=1, keepdims=True)


def cls_kernel(lengths, *refs, count, rows, head_dim, chunk):
    x_refs, (qkv_ref, mixer_ref, expand_ref, contract_ref, gain_ref, bias_ref, shift_ref, out_ref) = (
        refs[:count],
        refs[count:],
    )
    width = out_ref.shape[1]
    x = packed(x_refs)
    place = lax.broadcasted_iota(jnp.int32, (PACK, width), 0)
    ctx = jnp.zeros((PACK, width), F32)
    for b in range(count):
        base = b * rows
        query = qkv_ref[base : base + PACK, 0:width].astype(F32)[0:1] * head_dim**-0.5
        query = per_head(query, head_dim).astype(BF16)
        share = first_share(query, qkv_ref[base : base + rows, width : 2 * width], lengths[b])
        mixed = matmul(share.astype(BF16), qkv_ref[base : base + rows, 2 * width : 3 * width])
        ctx = jnp.where(place == b, heads_joined(mixed, head_dim), ctx)
    mixed = matmul(ctx.astype(BF16), mixer_ref[...]) + bias_ref[2:3]
    first = normalise(x + mixed)[0] * gain_ref[0:1] + bias_ref[3:4]
    first_low = first.astype(BF16)
    total = first + bias_ref[4:5]
    for start in range(0, expand_ref.shape[1], chunk):
        part = slice(start, start + chunk)
        active, _ = gelu_and_slope(matmul(first_low, expand_ref[:, part]) + shift_ref[0:1, part])
        total = total + matmul(active.astype(BF16), contract_ref[part, :])
    out_ref[...] = (normalise(total)[0] * gain_ref[1:2] + bias_ref[5:6]).astype(BF16)


def cls_forward(x, qkv, lengths, mats, gain, bias, shift):
    count = lengths.shape[0]
    rows, width = x.shape[0] // count, x.shape[1]
    rest = (qkv,) + mats + (gain, bias, shift)
    return pl.pallas_call(
        functools.partial(cls_kernel, count=count, rows=rows, head_dim=width // HEADS, chunk=768),
        grid_spec=pltpu.PrefetchScalarGridSpec(
            num_scalar_prefetch=1,
            grid=(1,),
            in_specs=[first_block(rows, width, b) for b in range(count)] + [whole(r) for r in rest],
            out_specs=pl.BlockSpec((PACK, width), lambda *_: (0, 0)),
        ),
        out_shape=jax.ShapeDtypeStruct((PACK, width), BF16),
        compiler_params=pltpu.CompilerParams(vmem_limit_bytes=VMEM),
        name="cls_forward",
    )(lengths, *[x] * count, *rest)


def place_kernel(decoder, cls_ref, x_ref, qkv_ref, joint_ref, shift_ref, x_out, qkv_out, new_ref):
    step = pl.program_id(0)

    @pl.when(step == 0)
    def _():
        new_ref[...] = (matmul(cls_ref[...], joint_ref[...]) + shift_ref[...]).astype(BF16).astype(F32)

    def put(old, new, out):
        spot = lax.broadcasted_iota(jnp.int32, new.shape, 0)
        row = jnp.sum(jnp.where(spot == step, new, 0.0), axis=0, keepdims=True)
        here = (spot == 0) & (decoder[0] == 1)
        out[...] = jnp.where(here, row, old.astype(F32)).astype(BF16)

    put(x_ref[...], cls_ref[...].astype(F32), x_out)
    put(qkv_ref[...], new_ref[...], qkv_out)


def place_first(decoder, cls, x, qkv, joint, shift, count):
    rows, width = x.shape[0] // count, x.shape[1]
    block = lambda n: pl.BlockSpec((PACK, n), lambda b, _: (b * rows // PACK, 0))
    return pl.pallas_call(
        place_kernel,
        grid_spec=pltpu.PrefetchScalarGridSpec(
            num_scalar_prefetch=1,
            grid=(count,),
            in_specs=[whole(cls), block(width), block(3 * width), whole(joint), whole(shift)],
            out_specs=[block(width), block(3 * width)],
            scratch_shapes=[pltpu.VMEM((PACK, 3 * width), F32)],
        ),
        out_shape=[jax.ShapeDtypeStruct(x.shape, BF16), jax.ShapeDtypeStruct(qkv.shape, BF16)],
        input_output_aliases={2: 0, 3: 1},
        compiler_params=pltpu.CompilerParams(vmem_limit_bytes=VMEM),
        name="place_first",
    )(decoder, cls, x, qkv, joint, shift)


def cls_grad_kernel(*refs, count):
    part_refs, one_refs, (joint_ref, out_ref) = refs[:count], refs[count : 2 * count], refs[2 * count :]
    width = out_ref.shape[1]
    total = packed(one_refs)
    for i in range(3):
        grad = packed([ref.at[i] for ref in part_refs]).astype(BF16)
        total = total + back_mul(grad, joint_ref[:, i * width : (i + 1) * width])
    out_ref[...] = total.astype(BF16)


def cls_back(parts, one, joint, count):
    rows, width = one.shape[0] // count, one.shape[1]
    part = lambda b: pl.BlockSpec((3, PACK, width), lambda *_: (0, b * rows // PACK, 0))
    return pl.pallas_call(
        functools.partial(cls_grad_kernel, count=count),
        grid=(1,),
        in_specs=[part(b) for b in range(count)]
        + [first_block(rows, width, b) for b in range(count)]
        + [whole(joint)],
        out_specs=pl.BlockSpec((PACK, width), lambda *_: (0, 0)),
        out_shape=jax.ShapeDtypeStruct((PACK, width), BF16),
        compiler_params=pltpu.CompilerParams(vmem_limit_bytes=VMEM),
        name="cls_back",
    )(*[parts] * count, *[one] * count, joint)


def first_back_kernel(lengths, grad_ref, *refs, count, rows, head_dim, chunk):
    kept = [packed(refs[i * count : (i + 1) * count]) for i in range(5)]
    normed_two, scale_two, slope, normed_one, scale_one = kept
    scale_two, scale_one = scale_two[:, 0:1], scale_one[:, 0:1]
    mixer_ref, expand_ref, contract_ref, gain_ref, qkv_ref, parts_ref = refs[5 * count : 5 * count + 6]
    branch_ref, hidden_ref, mixed_ref, one_ref, sums_ref, shift_sum_ref, out_ref, part_sums_ref = refs[5 * count + 6 :]
    width = grad_ref.shape[1]
    grad = grad_ref[...].astype(F32)
    sums_ref[...] = jnp.zeros_like(sums_ref)

    def add_sum(row, value):
        sums_ref[row : row + 1] = jnp.sum(value, axis=0, keepdims=True)

    add_sum(0, grad * normed_two)
    add_sum(1, grad)
    total = norm_back(grad * gain_ref[1:2], normed_two, scale_two)
    branch = total.astype(BF16)
    branch_ref[...] = branch
    add_sum(2, branch.astype(F32))
    for start in range(0, expand_ref.shape[1], chunk):
        part = slice(start, start + chunk)
        hidden = (back_mul(branch, contract_ref[part, :]) * slope[:, part]).astype(BF16)
        hidden_ref[:, part] = hidden
        shift_sum_ref[0:1, part] = jnp.sum(hidden.astype(F32), axis=0, keepdims=True)
        total = total + back_mul(hidden, expand_ref[:, part])
    add_sum(3, total * normed_one)
    add_sum(4, total)
    total = norm_back(total * gain_ref[0:1], normed_one, scale_one)
    one_ref[...] = total
    mixed = total.astype(BF16)
    mixed_ref[...] = mixed
    add_sum(5, mixed.astype(F32))
    ctx = back_mul(mixed, mixer_ref[...]).astype(BF16).astype(F32)
    for b in range(count):
        span = slice(b * rows, (b + 1) * rows)
        keys, values = qkv_ref[span, width : 2 * width], qkv_ref[span, 2 * width : 3 * width]
        query = qkv_ref[b * rows : b * rows + PACK, 0:width].astype(F32)[0:1] * head_dim**-0.5
        query = per_head(query, head_dim).astype(BF16)
        share = first_share(query, keys, lengths[b])
        ctx_heads = per_head(ctx[b : b + 1], head_dim).astype(BF16)
        share_grad = back_mul(ctx_heads, values)
        inner = jnp.sum(share * share_grad, axis=1, keepdims=True)
        score = (share * (share_grad - inner)).astype(BF16)
        query_grad = heads_joined(matmul(score, keys), head_dim) * head_dim**-0.5
        head_rows = parts_ref[0, b * rows : b * rows + PACK].astype(F32)
        top = lax.broadcasted_iota(jnp.int32, head_rows.shape, 0) == 0
        out_ref[0, span] = parts_ref[0, span]
        out_ref[0, b * rows : b * rows + PACK] = jnp.where(top, head_rows + query_grad, head_rows).astype(BF16)
        out_ref[1, span] = (parts_ref[1, span].astype(F32) + outer_sum(score, query)).astype(BF16)
        out_ref[2, span] = (parts_ref[2, span].astype(F32) + outer_sum(share.astype(BF16), ctx_heads)).astype(BF16)
    part_sums_ref[...] = jnp.zeros_like(part_sums_ref)
    for i in (0, 2):
        part_sums_ref[i : i + 1] = jnp.sum(out_ref[i].astype(F32), axis=0, keepdims=True)


def first_back(grad, kept, mats, gain, qkv, parts, lengths):
    count = lengths.shape[0]
    rows, width = qkv.shape[0] // count, grad.shape[1]
    hidden = mats[1].shape[1]
    blocks = [first_block(rows, array.shape[1], b) for array in kept for b in range(count)]
    rest = mats + (gain, qkv, parts)
    small = lambda n, kind, r=PACK: (pl.BlockSpec((r, n), lambda *_: (0, 0)), jax.ShapeDtypeStruct((r, n), kind))
    outs = [small(width, BF16), small(hidden, BF16), small(width, BF16), small(width, F32), small(width, F32, 8), small(hidden, F32, 1)]
    outs.append((whole(parts), jax.ShapeDtypeStruct(parts.shape, BF16)))
    outs.append(small(width, F32, 8))
    return pl.pallas_call(
        functools.partial(first_back_kernel, count=count, rows=rows, head_dim=width // HEADS, chunk=768),
        grid_spec=pltpu.PrefetchScalarGridSpec(
            num_scalar_prefetch=1,
            grid=(1,),
            in_specs=[whole(grad)] + blocks + [whole(r) for r in rest],
            out_specs=[spec for spec, _ in outs],
        ),
        out_shape=[shape for _, shape in outs],
        compiler_params=pltpu.CompilerParams(vmem_limit_bytes=VMEM),
        name="first_back",
    )(lengths, grad, *[array for array in kept for _ in range(count)], *rest)


def project_kernel(x_ref, joint_ref, shift_ref, out_ref):
    out_ref[...] = (matmul(x_ref[...], joint_ref[...]) + shift_ref[...]).astype(BF16)


def project(x, joint, shift):
    rows, width = x.shape
    step = min(256, rows)
    return pl.pallas_call(
        project_kernel,
        grid=(rows // step,),
        in_specs=[pl.BlockSpec((step, width), lambda i: (i, 0)), whole(joint), whole(shift)],
        out_specs=pl.BlockSpec((step, joint.shape[1]), lambda i: (i, 0)),
        out_shape=jax.ShapeDtypeStruct((rows, joint.shape[1]), BF16),
        compiler_params=pltpu.CompilerParams(vmem_limit_bytes=VMEM),
        name="project",
    )(x, joint, shift)


def input_grad_kernel(decoder, parts_ref, one_ref, first_ref, joint_ref, out_ref, *, step, rows):
    i = pl.program_id(0)
    width = out_ref.shape[1]

    total = one_ref[...]
    for j in range(3):
        total = total + back_mul(parts_ref[j], joint_ref[:, j * width : (j + 1) * width])
    out_ref[...] = total

    @pl.when(lax.rem(i * step, rows) == 0)
    def _():
        spot = lax.broadcasted_iota(jnp.int32, first_ref.shape, 0)
        row = jnp.sum(jnp.where(spot == i * step // rows, first_ref[...], 0.0), axis=0, keepdims=True)
        head = total[0:8]
        keep = jnp.where(decoder[0] == 1, 0.0, 1.0)
        top = lax.broadcasted_iota(jnp.int32, head.shape, 0) == 0
        out_ref[0:8] = jnp.where(top, (head + row) * keep, head)


def input_gradient(decoder, parts, one, one_first, joint, count):
    total_rows, width = one.shape
    rows = total_rows // count
    step = min(256, rows)
    return pl.pallas_call(
        functools.partial(input_grad_kernel, step=step, rows=rows),
        grid_spec=pltpu.PrefetchScalarGridSpec(
            num_scalar_prefetch=1,
            grid=(total_rows // step,),
            in_specs=[
                pl.BlockSpec((3, step, width), lambda i, _: (0, i, 0)),
                pl.BlockSpec((step, width), lambda i, _: (i, 0)),
                whole(one_first),
                whole(joint),
            ],
            out_specs=pl.BlockSpec((step, width), lambda i, _: (i, 0)),
        ),
        out_shape=jax.ShapeDtypeStruct(one.shape, F32),
        compiler_params=pltpu.CompilerParams(vmem_limit_bytes=VMEM),
        name="input_gradient",
    )(decoder, parts, one, one_first, joint)


def weight_grad_kernel(place, left_ref, right_ref, *refs):
    keep_ref, send_ref = refs[-2:]
    own, rows, _ = keep_ref.shape
    total = outer_sum(left_ref[...], right_ref[0]).astype(BF16)
    odd = lax.rem(place[0], 2) == 1
    for i in range(own):
        pair = [total[(2 * i + j) * rows : (2 * i + j + 1) * rows] for j in range(2)]
        keep_ref[i] = jnp.where(odd, pair[1], pair[0])
        send_ref[i] = jnp.where(odd, pair[0], pair[1])


def weight_grads(place, *pairs, tile=768):
    groups = lax.axis_size("dp")
    pairs = [(left, right if right.ndim == 3 else right[None]) for left, right in pairs]
    width = min(right.shape[2] for _, right in pairs)
    sizes = [left.shape[1] // groups for left, _ in pairs]
    heights = [size * right.shape[0] * right.shape[2] // width for size, (_, right) in zip(sizes, pairs)]
    if any(size % 16 for size in sizes):
        blocks = []
        for size, (left, right) in zip(sizes, pairs):
            total = jnp.concatenate([outer_sum(left, r) for r in right], axis=1).astype(BF16)
            total = total.reshape(groups, size, -1, width).transpose(0, 2, 1, 3)
            blocks.append(total.reshape(groups // 2, 2, -1, width))
        blocks = jnp.concatenate(blocks, axis=2)
        odd = lax.rem(place, 2)
        return tuple(lax.dynamic_index_in_dim(blocks, i, 1, False) for i in (odd, 1 - odd))
    shape = jax.ShapeDtypeStruct((groups // 2, sum(heights), width), BF16)
    done = []
    for i, (size, (left, right)) in enumerate(zip(sizes, pairs)):
        rows, height = left.shape
        cuts = right.shape[2] // width
        first = sum(heights[:i]) // size
        spec = pl.BlockSpec((tile // size // 2, size, width), lambda j, i, _, first=first: (i, first + j, 0))
        done = pl.pallas_call(
            weight_grad_kernel,
            grid_spec=pltpu.PrefetchScalarGridSpec(
                num_scalar_prefetch=1,
                grid=(right.shape[0] * cuts, height // tile),
                in_specs=[
                    pl.BlockSpec((rows, tile), lambda j, i, _: (0, i)),
                    pl.BlockSpec((1, rows, width), lambda j, i, _, cuts=cuts: (j // cuts, 0, j % cuts)),
                ]
                + [pl.BlockSpec(memory_space=pl.ANY)] * len(done),
                out_specs=[spec, spec],
            ),
            out_shape=[shape, shape],
            input_output_aliases={3: 0, 4: 1} if done else {},
            compiler_params=pltpu.CompilerParams(vmem_limit_bytes=VMEM),
            name="weight_grad",
        )(place.reshape(1), left, right, *done)
    return tuple(done)


def unstacked(total, shapes):
    parts = []
    start = 0
    for rows, columns in shapes:
        height = rows * columns // total.shape[1]
        part = total[start : start + height].reshape(-1, rows, total.shape[1])
        parts.append(part.transpose(1, 0, 2).reshape(rows, columns))
        start += height
    return parts


def add_split_kernel(mine, keep_a, got_a, keep_b, got_b, keep_ref, send_ref):
    keep_ref[...] = (keep_a[...].astype(F32) + got_a[...].astype(F32)).astype(BF16)
    send_ref[...] = (keep_b[...].astype(F32) + got_b[...].astype(F32)).astype(BF16)


def add_split(keep, got, axis, mine):
    rows, width = keep.shape[-2:]
    if rows % 16:
        total = (keep.astype(F32) + got.astype(F32)).astype(BF16)
        return tuple(lax.dynamic_index_in_dim(total, i, axis, False) for i in (mine, 1 - mine))
    rest = keep.shape[:axis] + keep.shape[axis + 1 : -2]
    before = 2**axis
    after = 2 ** (len(rest) - axis)
    shaped = [array.reshape(before, 2, after, rows, width) for array in (keep, got)]
    block = lambda other: pl.BlockSpec(
        (before, None, after, rows, min(width, 768)), lambda j, m: (0, (1 - m[0]) if other else m[0], 0, 0, j)
    )
    out = pl.BlockSpec((before, after, rows, min(width, 768)), lambda j, m: (0, 0, 0, j))
    shape = jax.ShapeDtypeStruct((before, after, rows, width), BF16)
    keep, send = pl.pallas_call(
        add_split_kernel,
        grid_spec=pltpu.PrefetchScalarGridSpec(
            num_scalar_prefetch=1,
            grid=(width // min(width, 768),),
            in_specs=[block(False), block(False), block(True), block(True)],
            out_specs=[out, out],
        ),
        out_shape=[shape, shape],
        compiler_params=pltpu.CompilerParams(vmem_limit_bytes=VMEM),
        name="add_split",
    )(mine.reshape(1), *shaped, *shaped)
    return keep.reshape(rest + (rows, width)), send.reshape(rest + (rows, width))


def first_hop(pair):
    keep, send = pair
    axes = tuple(reversed(bits_of(lax.axis_size("dp"))))[:-1]
    shape = (2,) * len(axes) + keep.shape[1:]
    return keep.reshape(shape), swapped(send, 1).reshape(shape), axes


def added(state, bit):
    keep, got, axes = state
    axis = axes.index(bit)
    mine = jnp.where((lax.axis_index("dp") & bit) == 0, 0, 1)
    return (*add_split(keep, got, axis, mine), axes[:axis] + axes[axis + 1 :])


def sent(halves, bit):
    keep, send, axes = halves
    return keep, swapped(send, bit), axes


def rest_of(state, order):
    for bit in order:
        state = sent(added(state, bit), bit)
    return state[0].astype(F32) + state[1].astype(F32)


def tied(*values):
    return lax.optimization_barrier(values)


def as_row(column):
    return jnp.broadcast_to(column, (column.shape[0], LANES)).T[0:1]


def as_column(row):
    return jnp.broadcast_to(row, (LANES, row.shape[1])).T[:, 0:1]


def word_cuts(slice_rows):
    size = 768
    return [
        (i, slice(start, min(start + size, slice_rows)), slice(i * slice_rows + start, i * slice_rows + min(start + size, slice_rows)))
        for i in range(2)
        for start in range(0, slice_rows, size)
    ]


def join(section, mine_ref, other_ref, out_ref):
    @pl.when(pl.program_id(0) == 0)
    def _():
        half = mine_ref.shape[0]
        swap = section == 1
        mine, other = mine_ref[...], other_ref[...]
        out_ref[:half] = jnp.where(swap, other, mine)
        out_ref[half:] = jnp.where(swap, mine, other)


def word_kernel(place, head_ref, own_ref, mine_ref, other_ref, shift_ref, peak_ref, total_ref, own_logit_ref, far_logit_ref, scores_ref, far_ref, *, steps):
    join(place[1], mine_ref, other_ref, far_ref)
    group, picks, _ = head_ref.shape
    width = own_ref.shape[1]
    rows = group * picks
    head = head_ref[:, :, 0:width].reshape(rows, width)
    peak = jnp.full((rows, 1), -jnp.inf, F32)
    cuts = word_cuts(own_ref.shape[0])
    for table, part, columns in cuts:
        scores = back_mul(head, (own_ref, far_ref)[table][part]) + shift_ref[0:1, columns]
        scores_ref[:, columns] = scores
        peak = jnp.maximum(peak, jnp.max(scores, axis=1, keepdims=True))
    total = jnp.zeros_like(peak)
    for _, _, columns in cuts:
        total = total + jnp.sum(jnp.exp(scores_ref[:, columns] - peak), axis=1, keepdims=True)
    for g in range(group):
        part = slice(g * picks, (g + 1) * picks)
        peak_ref[g] = as_row(peak[part])
        total_ref[g] = as_row(total[part])

    @pl.when(pl.program_id(0) < steps)
    def _():
        for g in range(group):
            part = slice(g * picks, (g + 1) * picks)
            spot = jnp.bitwise_xor(lax.rem(place[0], group), g)
            own_logit_ref[spot] = scores_ref[part, : own_ref.shape[0]].astype(BF16)
            far_logit_ref[spot] = scores_ref[part, own_ref.shape[0] :].astype(BF16)


def word_scores(place, head, own, mine, other, shift, group=4):
    near, picks, padded = head.shape
    vocab = shift.shape[1]
    quarter = near // 2
    steps = quarter // group
    row = pl.BlockSpec((group, 1, picks), lambda k, _: (k, 0, 0))
    row_shape = jax.ShapeDtypeStruct((near, 1, picks), F32)
    spot = lambda k, p: (jnp.bitwise_xor(lax.rem(p[0], quarter) // group, jnp.minimum(k, steps - 1)), 0, 0)
    return pl.pallas_call(
        functools.partial(word_kernel, steps=steps),
        grid_spec=pltpu.PrefetchScalarGridSpec(
            num_scalar_prefetch=1,
            grid=(near // group,),
            in_specs=[pl.BlockSpec((group, picks, padded), lambda k, _: (k, 0, 0))]
            + [whole(array) for array in (own, mine, other, shift)],
            out_specs=[row, row] + [pl.BlockSpec((group, picks, vocab // 2), spot)] * 2,
            scratch_shapes=[pltpu.VMEM((group * picks, vocab), F32), pltpu.VMEM(own.shape, BF16)],
        ),
        out_shape=[row_shape] * 2 + [jax.ShapeDtypeStruct((quarter, picks, vocab // 2), BF16)] * 2,
        compiler_params=pltpu.CompilerParams(vmem_limit_bytes=VMEM),
        name="word_scores",
    )(place, head, own, mine, other, shift)


def side_kernel(place, head_ref, own_mine, own_other, far_mine, far_other, shift_ref, logit_ref, own_ref, far_ref):
    join(place[1], own_mine, own_other, own_ref)
    join(place[1], far_mine, far_other, far_ref)
    group, picks, _ = head_ref.shape
    width = own_ref.shape[1]
    head = head_ref[:, :, 0:width].reshape(group * picks, width)
    for table, part, columns in word_cuts(own_ref.shape[0]):
        scores = back_mul(head, (own_ref, far_ref)[table][part]) + shift_ref[0:1, columns]
        scores = scores.astype(BF16)
        for g in range(group):
            spot = jnp.bitwise_xor(lax.rem(place[0], group), g)
            logit_ref[spot, :, columns] = scores[g * picks : (g + 1) * picks]


def side_scores(place, head, own, far, shift, group=4):
    tables = own + far
    near, picks, padded = head.shape
    vocab = shift.shape[1]
    quarter = near // 2
    spot = lambda k, p: (jnp.bitwise_xor(lax.rem(p[0], quarter) // group, k), 0, 0)
    return pl.pallas_call(
        side_kernel,
        grid_spec=pltpu.PrefetchScalarGridSpec(
            num_scalar_prefetch=1,
            grid=(quarter // group,),
            in_specs=[pl.BlockSpec((group, picks, padded), lambda k, _: (k, 0, 0))]
            + [whole(array) for array in tables + (shift,)],
            out_specs=pl.BlockSpec((group, picks, vocab), spot),
            scratch_shapes=[pltpu.VMEM((vocab // 2, own[0].shape[1]), BF16)] * 2,
        ),
        out_shape=jax.ShapeDtypeStruct((quarter, picks, vocab), BF16),
        compiler_params=pltpu.CompilerParams(vmem_limit_bytes=VMEM),
        name="side_scores",
    )(place, head, *tables, shift)


def word_back_kernel(first, head_ref, log_ref, own_ref, mine_ref, other_ref, shift_ref, grad_ref, out_ref, sums_ref, hit_ref, far_ref, *, masked):
    join(first[2], mine_ref, other_ref, far_ref)

    @pl.when(pl.program_id(0) == 0)
    def _():
        sums_ref[...] = jnp.zeros_like(sums_ref)

    group, picks, width = out_ref.shape
    rows = group * picks
    label = head_ref[:, :, width:].reshape(rows, -1).astype(F32)
    label = (label[:, 0:1] * 256.0 + label[:, 1:2]).astype(jnp.int32)
    logs = jnp.concatenate([as_column(log_ref[g]) for g in range(group)])
    head = head_ref[:, :, 0:width].reshape(rows, width)
    total = jnp.zeros((rows, width), F32)
    hit = jnp.zeros((rows, 1), F32)
    for table, part, columns in word_cuts(own_ref.shape[0]):
        words = (own_ref, far_ref)[table][part]
        scores = back_mul(head, words) + shift_ref[0:1, columns]
        share = jnp.exp(scores - logs)
        mine = lax.broadcasted_iota(jnp.int32, share.shape, 1) == label - (first[table] + part.start)
        hit = hit + jnp.sum(jnp.where(mine, scores, 0.0), axis=1, keepdims=True)
        grad = (jnp.where(mine, share - 1.0, share) * (1.0 / masked)).astype(BF16)
        grad_ref[:, :, columns] = grad.reshape(group, picks, -1)
        sums_ref[0:1, columns] += jnp.sum(grad.astype(F32), axis=0, keepdims=True)
        total = total + matmul(grad, words)
    out_ref[...] = total.astype(BF16).reshape(group, picks, width)
    for g in range(group):
        hit_ref[g] = as_row(hit[g * picks : (g + 1) * picks])


def word_back(first, head, logs, own, mine, other, shift, masked, group=4):
    near, picks, padded = head.shape
    width = own.shape[1]
    vocab = shift.shape[1]
    block = lambda n: pl.BlockSpec((group, picks, n), lambda k, _: (k, 0, 0))
    row = pl.BlockSpec((group, 1, picks), lambda k, _: (k, 0, 0))
    return pl.pallas_call(
        functools.partial(word_back_kernel, masked=masked),
        grid_spec=pltpu.PrefetchScalarGridSpec(
            num_scalar_prefetch=1,
            grid=(near // group,),
            in_specs=[block(padded), row] + [whole(array) for array in (own, mine, other, shift)],
            out_specs=[block(vocab), block(width), pl.BlockSpec((1, vocab), lambda k, _: (0, 0)), row],
            scratch_shapes=[pltpu.VMEM(own.shape, BF16)],
        ),
        out_shape=[
            jax.ShapeDtypeStruct((near, picks, vocab), BF16),
            jax.ShapeDtypeStruct((near, picks, width), BF16),
            jax.ShapeDtypeStruct((1, vocab), F32),
            jax.ShapeDtypeStruct((near, 1, picks), F32),
        ],
        compiler_params=pltpu.CompilerParams(vmem_limit_bytes=VMEM),
        name="word_back",
    )(first, head, logs, own, mine, other, shift)


def assemble_kernel(place, own_ref, far_ref, side_ref, side_far_ref, out_ref, *, quarter):
    for i, ref in enumerate((own_ref, side_ref, far_ref, side_far_ref)):

        @pl.when(jnp.bitwise_xor(place[0] // quarter, pl.program_id(0)) == i)
        def _():
            out_ref[...] = ref[0]


def assembled(place, own, far, side):
    quarter, picks, slice_rows = own.shape
    if slice_rows % LANES:
        parts = jnp.stack([own, side[:, :, :slice_rows], far, side[:, :, slice_rows:]])
        parts = jnp.take(parts, jnp.bitwise_xor(jnp.arange(4), place // quarter), axis=0)
        return parts.transpose(2, 0, 1, 3).reshape(picks, 4 * quarter * slice_rows)

    def spec(flip, column):
        def index(b, j, p):
            turn = jnp.bitwise_xor(p[0] // quarter, flip)
            return jnp.where(b == turn, j, jnp.where(b < turn, 0, quarter - 1)), 0, column

        return pl.BlockSpec((1, picks, slice_rows), index)

    return pl.pallas_call(
        functools.partial(assemble_kernel, quarter=quarter),
        grid_spec=pltpu.PrefetchScalarGridSpec(
            num_scalar_prefetch=1,
            grid=(4, quarter),
            in_specs=[spec(0, 0), spec(2, 0), spec(1, 0), spec(3, 1)],
            out_specs=pl.BlockSpec((picks, slice_rows), lambda b, j, _: (0, b * quarter + j)),
        ),
        out_shape=jax.ShapeDtypeStruct((picks, 4 * quarter * slice_rows), BF16),
        compiler_params=pltpu.CompilerParams(vmem_limit_bytes=VMEM),
        name="assemble",
    )(place.reshape(1), own, far, side, side)


def on_device(
    embedded,
    lengths,
    positions,
    labels,
    joint_weight,
    mixer_weight,
    expand_weight,
    contract_weight,
    head_weight,
    gains,
    biases,
    expand_bias,
    word_table,
    word_bias,
):
    section = lax.axis_index("section")
    place = lax.axis_index("dp")
    groups = lax.axis_size("dp")
    decoder = section == 1
    count, rows, width = embedded.shape[1:]
    total_rows = count * rows
    head_dim = width // HEADS
    masked = positions.shape[-1]
    picks = count * masked
    joint = joint_weight[0]
    mats = (mixer_weight[0], expand_weight[0], contract_weight[0])
    head_matrix = head_weight[0]
    gain = gains[0]
    bias = biases[0]
    shift = expand_bias
    slice_rows = word_table.shape[0]

    flag = section.astype(jnp.int32).reshape(1)
    place32 = place.astype(jnp.int32)
    units = shift.shape[1]
    own = width // groups
    near, quarter = groups // 2, groups // 4
    half = slice_rows // 2
    bits = bits_of(groups)
    order = bits[1:]
    joint_order = bits[-2:-1] + bits[1:-2] + bits[-1:]
    across = lambda array: lax.ppermute(array, "section", [(0, 1), (1, 0)])
    pick_half = lambda array, which: lax.dynamic_slice_in_dim(array, which * half, half)

    def joined(mine, other):
        return jnp.where(decoder, jnp.concatenate([other, mine]), jnp.concatenate([mine, other]))

    my_half = pick_half(word_table, section)
    far_mine = swapped(my_half, near)
    side_half = swapped(my_half, quarter)

    x = embedded[0].reshape(total_rows, width)
    joint_shift = jnp.concatenate([bias[0], jnp.zeros((width,), F32), bias[1]])[None]
    qkv = project(x, joint, joint_shift)
    cls_out = cls_forward(x, qkv, lengths, mats, gain, bias, shift)
    cls_in = passed_along(cls_out, "section", 1)
    x, qkv = place_first(flag, cls_in, x, qkv, joint, joint_shift, count)
    ctx, logs = attend(qkv, lengths, count)
    ctx, side_half = tied(ctx, side_half)
    far_shift = swapped(word_bias, near)
    side_shift = swapped(word_bias, quarter)
    y, normed_one, scale_one, first_low, active, slope, normed_two, scale_two = layer_tail(
        ctx, x, mats, gain, bias, shift
    )
    y, far_mine, far_shift, side_shift = tied(y, far_mine, far_shift, side_shift)
    far_other = across(far_mine)
    side_far_shift = swapped(far_shift, quarter)

    chosen = positions[0][:, :, None] == jnp.arange(rows)[None, None, :]
    picked = jnp.einsum(
        "bml,blw->bmw", chosen.astype(BF16), y.reshape(count, rows, width), preferred_element_type=F32
    )
    picked_low = picked.astype(BF16).reshape(picks, width)
    dense = matmul(picked_low, head_matrix) + bias[6]
    dense_active, dense_slope = gelu_and_slope(dense)
    normed_head, scale_head = normalise(dense_active)
    head_low = (normed_head * gain[2] + bias[7]).astype(BF16)
    answers = labels[0].reshape(-1, 1)
    answers = jnp.concatenate([answers // 256, answers % 256, jnp.zeros((picks, LANES - 2), jnp.int32)], axis=1)
    head_all = gather_near(jnp.concatenate([head_low, answers.astype(BF16)], axis=1))
    head_all, far_other, side_far_shift, side_half = tied(head_all, far_other, side_far_shift, side_half)
    side_half_other = across(side_half)
    word_shift = jnp.concatenate([word_bias, far_shift]).astype(F32)[None]
    side_word_shift = jnp.concatenate([side_shift, side_far_shift]).astype(F32)[None]
    where_to = jnp.stack([place32, section.astype(jnp.int32)])
    peak, total, *logits = word_scores(where_to, head_all, word_table, far_mine, far_other, word_shift)
    grid = (2,) * (len(bits) - 1)
    peak, total = (array.reshape(grid + (picks,)) for array in (peak, total))
    for axis, bit in enumerate(reversed(bits[:-1])):
        other_peak, other_total = jnp.flip(swapped(jnp.stack([peak, total]), bit), axis + 1)
        top = jnp.maximum(peak, other_peak)
        total = total * jnp.exp(peak - top) + other_total * jnp.exp(other_peak - top)
        peak = top
    log_total = (peak + jnp.log(total)).reshape(near, 1, picks)
    log_total, far_mine, *logits = tied(log_total, far_mine, *logits)
    side_far_half = swapped(far_mine, quarter)
    exchanged = lambda part: lax.all_to_all(
        part, "dp", 0, 0, axis_index_groups=[list(range(i, i + quarter)) for i in range(0, groups, quarter)]
    )
    logits_own = exchanged(logits[0])
    first = (jnp.stack([place, jnp.bitwise_xor(place, near)]) * slice_rows).astype(jnp.int32)
    first = jnp.concatenate([first, flag])
    score_grad, head_back, word_sums, hits = word_back(
        first, head_all, log_total, word_table, far_mine, far_other, word_shift, masked
    )
    head_back, logits_own, side_half_other, side_far_half = tied(
        head_back, logits_own, side_half_other, side_far_half
    )
    side_far_other = across(side_far_half)
    loss_part = jnp.sum(log_total[0]) - jnp.sum(hits)
    head_grad = scatter_near(head_back)

    score_grad = score_grad.reshape(near * picks, 2 * slice_rows)
    head_rows = head_all[:, :, :width].reshape(near * picks, width)
    own_grad, far_grad = (
        outer_sum(score_grad[:, i * slice_rows : (i + 1) * slice_rows], head_rows).astype(BF16) for i in range(2)
    )
    head_grad, own_grad, far_grad, logits_far = tied(head_grad, own_grad, far_grad, logits[1])
    logits_far = exchanged(logits_far)
    far_got = across(pick_half(far_grad, 1 - section))

    gain_head = jnp.sum(head_grad * normed_head, 0)
    shift_head = jnp.sum(head_grad, 0)
    dense_grad = (norm_back(head_grad * gain[2], normed_head, scale_head) * dense_slope).astype(BF16)
    dense_shift = jnp.sum(dense_grad, axis=0, dtype=F32)
    picked_grad = back_mul(dense_grad, head_matrix).reshape(count, masked, width)
    grad = jnp.einsum(
        "bml,bmw->blw", chosen.astype(F32), picked_grad, precision=lax.Precision.HIGHEST
    ).reshape(total_rows, width)

    kept = (normed_two, scale_two, slope, normed_one, scale_one)
    branch, hidden, one, mixed, ctx_grad, sums, shift_sum = tail_back(grad, kept, mats, gain)
    hidden, branch, side_far_other, side_half_other, logits_far = tied(
        hidden, branch, side_far_other, side_half_other, logits_far
    )
    logits_side = side_scores(
        where_to, head_all, (side_half, side_half_other), (side_far_half, side_far_other), side_word_shift
    )
    branch, logits_side = tied(branch, logits_side)
    logits_side = exchanged(logits_side)
    one_pair = weight_grads(place32, (active, branch), (ctx, mixed))
    hidden, one_pair, far_got = tied(hidden, one_pair, far_got)
    one_state = first_hop(one_pair)
    far_half = (pick_half(far_grad, section).astype(F32) + far_got.astype(F32)).astype(BF16)
    far_quarters = [far_half[i * half // 4 : (i + 1) * half // 4] for i in range(4)]
    far_quarters[0] = swapped(far_quarters[0], near)
    two_pair = weight_grads(place32, (first_low, hidden), (picked_low, dense_grad))
    ctx_grad, two_pair = tied(ctx_grad, two_pair)
    two_state = first_hop(two_pair)
    halves = added(one_state, order[0])
    ctx_grad, halves_now, far_quarters[0], far_quarters[1] = tied(
        ctx_grad, halves[:2], far_quarters[0], far_quarters[1]
    )
    one_state = sent((*halves_now, halves[2]), order[0])
    far_quarters[1] = swapped(far_quarters[1], near)
    parts = attend_back(qkv, ctx_grad, logs, lengths, 0)
    halves = added(two_state, order[0])
    parts, halves_now, far_quarters[1], far_quarters[2] = tied(
        parts, halves[:2], far_quarters[1], far_quarters[2]
    )
    two_state = sent((*halves_now, halves[2]), order[0])
    far_quarters[2] = swapped(far_quarters[2], near)
    own_got = across(pick_half(own_grad, 1 - section))
    for passage in range(1, count):
        parts = attend_back(qkv, ctx_grad, logs, lengths, passage, (parts,))
    halves = added(one_state, order[1])
    parts, halves_now, logits_side, far_quarters[2], far_quarters[3] = tied(
        parts, halves[:2], logits_side, far_quarters[2], far_quarters[3]
    )
    one_state = sent((*halves_now, halves[2]), order[1])
    cls_grad = passed_along(cls_back(parts, one, joint, count), "section", -1)
    far_quarters[3] = swapped(far_quarters[3], near)

    branch_f, hidden_f, mixed_f, one_f, sums_f, shift_f, parts, part_sums = first_back(
        cls_grad, kept, mats, gain, qkv, parts, lengths
    )
    halves = added(two_state, order[1])
    parts, halves_now, far_quarters[3], own_got = tied(parts, halves[:2], far_quarters[3], own_got)
    two_state = sent((*halves_now, halves[2]), order[1])
    joint_pair = weight_grads(place32, (x, parts))
    parts, joint_pair = tied(parts, joint_pair)
    joint_state = first_hop(joint_pair)
    own_half = pick_half(own_grad, section).astype(F32) + own_got.astype(F32)
    own_half = (own_half + jnp.concatenate(far_quarters).astype(F32)).astype(BF16)
    table_total = joined(own_half, across(own_half)).astype(F32)
    word_total = word_sums[0, :slice_rows] + swapped(word_sums[0, slice_rows:], near)
    word_total = word_total + across(word_total)
    halves = added(one_state, order[2])
    parts, halves_now = tied(parts, halves[:2])
    one_state = sent((*halves_now, halves[2]), order[2])
    halves = added(joint_state, joint_order[0])
    parts, halves_now, *logits = tied(parts, halves[:2], logits_own, logits_far, logits_side)
    joint_state = sent((*halves_now, halves[2]), joint_order[0])
    input_grad = input_gradient(flag, parts, one, one_f, joint, count)
    joint_sum = unstacked(rest_of(joint_state, joint_order[1:]), [(own, 3 * width)])[0]
    contract_sum, mixer_sum = unstacked(rest_of(one_state, order[3:]), [(units // groups, width), (own, width)])
    expand_sum, head_sum = unstacked(rest_of(two_state, order[2:]), [(own, units), (own, width)])

    def firsts(array):
        return jnp.concatenate([array[b * rows : b * rows + 1] for b in range(count)])

    mine = jnp.concatenate(
        [firsts(active), firsts(first_low), firsts(ctx), branch_f[:count], hidden_f[:count], mixed_f[:count]],
        axis=1,
    )
    sums = sums + sums_f
    small = jnp.concatenate(
        [
            jnp.stack([sums[3], sums[0], gain_head]),
            jnp.stack(
                [part_sums[0], part_sums[2], sums[5], sums[4], sums[2], sums[1], dense_shift, shift_head]
            ),
            (shift_sum + shift_f).reshape(-1, width),
            jnp.broadcast_to(loss_part, (1, width)),
        ]
    )
    small_high = lax.reduce_precision(small, 8, 7)
    small_low = (small - small_high).astype(BF16)
    small_high = small_high.astype(BF16)
    mine = mine.reshape(-1, width)
    counts = [mine.shape[0], small.shape[0], small.shape[0]]
    rows_all = gather_all(jnp.concatenate([mine, small_high, small_low]))
    rows_all = rows_all.reshape(groups, -1, width)
    small = jnp.sum(rows_all[:, counts[0] :].astype(F32), axis=0)
    small = small[: counts[1]] + small[counts[1] :]
    rows_all = rows_all[:, : counts[0]].reshape(groups * count, -1)
    cuts = [units, width, width, width, units, width]
    starts = [sum(cuts[:i]) for i in range(len(cuts))]
    active_a, first_a, ctx_a, branch_a, hidden_a, mixed_a = (
        rows_all[:, s : s + n] for s, n in zip(starts, cuts)
    )

    def own_columns(array):
        size = array.shape[1] // groups
        return lax.dynamic_slice_in_dim(array, place * size, size, 1)

    contract_sum = contract_sum + outer_sum(own_columns(active_a), branch_a)
    expand_sum = expand_sum + outer_sum(own_columns(first_a), hidden_a)
    mixer_sum = mixer_sum + outer_sum(own_columns(ctx_a), mixed_a)

    logits_out = assembled(place32, *logits)
    loss = (small[-1, 0] / (picks * groups)).reshape(1)
    return (
        loss,
        logits_out.reshape(1, count, masked, -1),
        input_grad.reshape(1, count, rows, width),
        joint_sum[None],
        mixer_sum[None],
        expand_sum[None],
        contract_sum[None],
        head_sum[None],
        small[None, :3],
        small[None, 3:11],
        small[11:-1].reshape(1, -1),
        table_total,
        word_total,
    )


def solution(mesh):
    in_specs = (
        P("section", "dp", None, None),
        P("dp"),
        P("section", "dp", None),
        P("section", "dp", None),
        P("section", None, None),
        P("section", None, None),
        P("section", None, None),
        P("section", None, None),
        P("section", None, None),
        P("section", None, None),
        P("section", None, None),
        P("section", None),
        P("dp", None),
        P("dp"),
    )
    out_specs = (
        P("section"),
        P("section", "dp", None, None),
        P("section", "dp", None, None),
        P("section", "dp", None),
        P("section", "dp", None),
        P("section", "dp", None),
        P("section", "dp", None),
        P("section", "dp", None),
        P("section", None, None),
        P("section", None, None),
        P("section", None),
        P("dp", None),
        P("dp"),
    )
    return jax.shard_map(
        on_device, mesh=mesh, in_specs=in_specs, out_specs=out_specs, check_vma=False
    )
```

time: 2000 us -> 565 us (0.28)
  waiting for transfers between devices: 1180 us -> 126 us
  matrix products: 298 us -> 22.1 us
  Pallas kernels: 0 us -> 267 us
  other arithmetic: 199 us -> 32.6 us
  local copies, waits for them, and re-layouts: 177 us -> 35.8 us
  blocking collectives: 89.8 us -> 0 us
  starting transfers between devices: 5.79 us -> 66.2 us
    reduce_scatter x6 -> x0, waiting for transfers between devices: 1060 us -> none  [the longest x1 802 us: on_device(): lax.psum_scatter(outer_sum(score_grad, head_low), 'dp', scatter_dimension...]
    dot_general x46 -> x9, matrix products: 298 us -> 22.1 us  [the longest x7 17.1 us: product(): lax.dot_general(left, right, (((left_dim,), (right_dim,)), ((), ())), pre...]
    pallas_call x0 -> x29, Pallas kernels: none -> 267 us  [the longest x5 33.6 us: weight_grads(): pl.pallas_call(weight_grad_kernel, grid_spec=pltpu.PrefetchScalarGridSpec...]
    ppermute x0 -> x45, waiting for transfers between devices: none -> 125 us  [the longest x38 101 us: swapped(): return lax.ppermute(block, 'dp', [(i, i ^ bit) for i in devices])]
    ppermute x4 -> x2, waiting for transfers between devices: 79.7 us -> 1.76 us  [passed_along(): return lax.ppermute(block, axis, route)]
    psum x2 -> x0, blocking collectives: 65.9 us -> none  [the longest x1 61 us: on_device(): lax.psum((gain_total, bias_total, grad_shift, word_shift_grad, loss_part)...]
    dynamic_update_slice x35 -> x0, local copies, waits for them, and re-layouts: 64 us -> none  [the longest x32 58.8 us: on_device(): lax.dynamic_update_index_in_dim(buffer, value, store, 0)]
    ppermute x0 -> x45, starting transfers between devices: none -> 47.3 us  [the longest x38 39.4 us: swapped(): return lax.ppermute(block, 'dp', [(i, i ^ bit) for i in devices])]
  transfers between devices with their start and end apart: 12 -> 50, of which waited for: 7 -> 23; matrix products, arithmetic and copies ran while one was open for 28% -> 12% of each run, Pallas kernels for 0% -> 45%
where the time goes in v1:
time: 565 us; the launch traced here: 555 us
  Pallas kernels  267 us (47%)
  waiting for transfers between devices  126 us (22%)
  starting transfers between devices  66.2 us (12%)
  local copies, waits for them, and re-layouts  35.8 us (6%)
  other arithmetic  32.6 us (6%)
  matrix products  22.1 us (4%)
    ppermute x38, waiting for transfers between devices, swapped(): return lax.ppermute(block, 'dp', [(i, i ^ bit) for i in devices])  101 us
    ppermute x38, starting transfers between devices, swapped(): return lax.ppermute(block, 'dp', [(i, i ^ bit) for i in devices])  39.4 us
    pallas_call x5, Pallas kernels, weight_grads(): pl.pallas_call(weight_grad_kernel, grid_spec=pltpu.PrefetchScalarGridSpec...  33.6 us
    pallas_call x2, Pallas kernels, attend_back(): pl.pallas_call(functools.partial(attend_back_kernel, head_dim=head_dim, p...  31.9 us
    pallas_call x9, Pallas kernels, add_split(): pl.pallas_call(add_split_kernel, grid_spec=pltpu.PrefetchScalarGridSpec(n...  28.1 us
    ppermute x7, waiting for transfers between devices, on_device(): across = lambda array: lax.ppermute(array, 'section', [(0, 1), (1, 0)])  23.5 us
    pallas_call x1, Pallas kernels, tail_back(): pl.pallas_call(functools.partial(tail_back_kernel, chunk=min(chunk, hidde...  22.9 us
    pallas_call x1, Pallas kernels, layer_tail(): pl.pallas_call(functools.partial(tail_kernel, chunk=min(chunk, hidden)),...  22.5 us
  transfers between devices with their start and end apart: 50, of which 23 were waited for; matrix products, arithmetic and copies ran while one was open for 12% of the time, Pallas kernels for 45%

profile of v1, /device:TPU:0, one launch (start us, length us, event | category | flops | bytes accessed | tf_op | source)
XLA Modules:
  0.0 555.1 jit_solution(12495138611771729459)
XLA Ops:
  12.4 7.8 %project.1.refs_2_.qkv_ref = bf16[1024,2304]{1,0:T(8,128)(2,1)} custom-call(bf16[1024,768]{1,0:T(8,128)(2,1)} %bitcast.189, bf16[768,2304]{1,0:T(8,128)(2,1)} %bitcast.201, f32[1,2304]{1,0:T(1,128)} %broadcast_in_dim.50.shift_ref), custom_call_target="tpu_custom_call" | custom-call | tf_op jit(solution)/shard_map/project/pallas_call | solution.py:542
  20.2 10.4 %cls_forward.1 = bf16[16,768]{1,0:T(8,128)(2,1)} custom-call(s32[2]{0:T(128)} %lengths.9, bf16[1024,768]{1,0:T(8,128)(2,1)} %bitcast.190, bf16[1024,768]{1,0:T(8,128)(2,1)} %bitcast.191, bf16[1024,2304]{1,0:T(8,128)(2,1)} %project.1.refs_2_.qkv_ref, bf16[768,768]{1,0:T(8,128)(2,1)} %bitcast.213, bf16[768,3072]{1,0:T(8,128)(2,1)} %bitcast.193, ...), custom_call_target="tpu_custom_call" | custom-call | tf_op jit(solution)/shard_map/cls_forward/pallas_call | solution.py:380
  40.1 18.3 %attend.1 = (bf16[1024,768]{1,0:T(8,128)(2,1)}, f32[12,2,512]{2,1,0:T(2,128)}) custom-call(s32[2]{0:T(128)} %lengths.9, bf16[1024,2304]{1,0:T(8,128)(2,1)} %get-tuple-element.145.q_ref.k_ref.v_ref.refs_14_, bf16[1024,2304]{1,0:T(8,128)(2,1)} %get-tuple-element.145.q_ref.k_ref.v_ref.refs_14_, bf16[1024,2304]{1,0:T(8,128)(2,1)} %get-tuple-element.145.q_ref.k_ref.v_ref.refs_14_), custom_call_target="tpu_custom_call" | custom-call | tf_op jit(solution)/shard_map/attend/pallas_call | solution.py:127
  58.4 13.6 %collective-permute-done.1.own_mine = bf16[960,768]{1,0:T(8,128)(2,1)} collective-permute-done((bf16[960,768]{1,0:T(8,128)(2,1)S(1)}, bf16[960,768]{1,0:T(8,128)(2,1)}, u32[]{:S(2)}, u32[]{:S(2)}) %collective-permute-start.1) | collective-permute-done | bytes 1474592 | tf_op jit(solution)/shard_map/ppermute | solution.py:47
  72.0 22.5 %layer_tail.1 = (bf16[1024,768]{1,0:T(8,128)(2,1)}, bf16[1024,768]{1,0:T(8,128)(2,1)}, f32[1024,128]{1,0:T(8,128)}, bf16[1024,768]{1,0:T(8,128)(2,1)}, bf16[1024...) custom-call(bf16[1024,768]{1,0:T(8,128)(2,1)} %get-tuple-element.147.ctx_ref.le, ...), custom_call_target="tpu_custom_call" | custom-call | tf_op jit(solution)/shard_map/layer_tail/pallas_call | solution.py:243
  119.3 12.1 %collective-permute-done.9.other_ref = bf16[960,768]{1,0:T(8,128)(2,1)S(1)} collective-permute-done((bf16[960,768]{1,0:T(8,128)(2,1)}, bf16[960,768]{1,0:T(8,128)(2,1)S(1)}, u32[]{:S(2)}, u32[]{:S(2)}) %collective-permute-start.9) | collective-permute-done | bytes 1474592 | tf_op jit(solution)/shard_map/ppermute | solution.py:972
  132.5 16.0 %word_scores.1 = (f32[8,1,128]{2,1,0:T(1,128)}, f32[8,1,128]{2,1,0:T(1,128)}, bf16[4,128,1920]{2,1,0:T(8,128)(2,1)}, bf16[4,128,1920]{2,1,0:T(8,128)(2,1)}) custom-call(s32[2]{0:T(128)} %pad_add_fusion.1.place, bf16[8,128,896]{2,1,0:T(8,128)(2,1)} %bitcast.205, bf16[1920,768]{1,0:T(8,128)(2,1)} %own_ref.3, bf16[960,768]{1,0:T(8,128)(2,1)} %collective-permute-done.2.mine_ref, ...), custom_call_target="tpu_custom_call" | custom-call | tf_op jit(solution)/shard_map/word_scores/pallas_call | solution.py:786
  165.3 22.1 %word_back.1 = (bf16[8,128,3840]{2,1,0:T(8,128)(2,1)}, bf16[8,128,768]{2,1,0:T(8,128)(2,1)}, f32[1,3840]{1,0:T(1,128)}, f32[8,1,128]{2,1,0:T(1,128)}) custom-call(s32[3]{0:T(128)} %pad_add_fusion.first, bf16[8,128,896]{2,1,0:T(8,128)(2,1)} %bitcast.206, f32[8,1,128]{2,1,0:T(1,128)} %bitcast.281, bf16[1920,768]{1,0:T(8,128)(2,1)} %own_ref.3, ...), custom_call_target="tpu_custom_call" | custom-call | tf_op jit(solution)/shard_map/word_back/pallas_call | solution.py:874
  187.5 4.9 collective-permute-done.14.own_other
  197.2 7.2 %fusion.8 = bf16[1920,768]{1,0:T(8,128)(2,1)} fusion(bf16[1024,768]{1,0:T(8,128)(2,1)S(1)} %bitcast.258, bf16[1024,3840]{1,0:T(8,128)(2,1)} %bitcast.292), kind=kOutput, calls=%fused_computation.7 | convolution fusion | flops 3021373440 | bytes 8454144 | tf_op jit(solution)/shard_map/dot_general | solution.py:22
  209.3 5.0 fusion.5
  231.7 22.9 %tail_back.1 = (bf16[1024,768]{1,0:T(8,128)(2,1)}, bf16[1024,3072]{1,0:T(8,128)(2,1)}, f32[1024,768]{1,0:T(8,128)}, bf16[1024,768]{1,0:T(8,128)(2,1)}, bf16[1024...) custom-call(f32[1024,768]{1,0:T(8,128)} %bitcast.217, ...), custom_call_target="tpu_custom_call" | custom-call | tf_op jit(solution)/shard_map/tail_back/pallas_call | solution.py:301
  254.7 9.1 %side_scores.1 = bf16[4,128,3840]{2,1,0:T(8,128)(2,1)} custom-call(s32[2]{0:T(128)} %pad_add_fusion.1.place, bf16[8,128,896]{2,1,0:T(8,128)(2,1)} %bitcast.207, bf16[960,768]{1,0:T(8,128)(2,1)} %collective-permute-done.1.own_mine, bf16[960,768]{1,0:T(8,128)(2,1)} %collective-permute-done.14.own_other, bf16[960,768]{1,0:T(8,128)(2,1)} %collective-permute-done.15.far_mine, ...), custom_call_target="tpu_custom_call" | custom-call | tf_op jit(solution)/shard_map/side_scores/pallas_call | solution.py:822
  263.7 9.2 %weight_grad.5 = (bf16[8,240,768]{2,1,0:T(8,128)(2,1)}, bf16[8,240,768]{2,1,0:T(8,128)(2,1)}) custom-call(s32[1]{0:T(128)} %bitcast.11.place, bf16[1024,3072]{1,0:T(8,128)(2,1)} %get-tuple-element.149.left_ref, bf16[1,1024,768]{2,1,0:T(8,128)(2,1)} %bitcast.263), custom_call_target="tpu_custom_call" | custom-call | tf_op jit(solution)/shard_map/weight_grad/pallas_call | solution.py:628
  280.1 9.7 %weight_grad.7 = (bf16[8,240,768]{2,1,0:T(8,128)(2,1)}, bf16[8,240,768]{2,1,0:T(8,128)(2,1)}) custom-call(s32[1]{0:T(128)} %bitcast.11.place, bf16[1024,768]{1,0:T(8,128)(2,1)} %get-tuple-element.150.left_ref, bf16[1,1024,3072]{2,1,0:T(8,128)(2,1)} %bitcast.223), custom_call_target="tpu_custom_call" | custom-call | tf_op jit(solution)/shard_map/weight_grad/pallas_call | solution.py:628
  292.9 4.8 all-to-all-start.2
  302.1 4.6 add_split.9
  306.7 13.6 %collective-permute-done.23 = bf16[240,768]{1,0:T(8,128)(2,1)S(1)} collective-permute-done((bf16[240,768]{1,0:T(8,128)(2,1)S(1)}, bf16[240,768]{1,0:T(8,128)(2,1)S(1)}, u32[]{:S(2)}, u32[]{:S(2)}) %collective-permute-start.23) | collective-permute-done | bytes 368672 | tf_op jit(solution)/shard_map/ppermute | solution.py:47
  323.7 4.7 add_split.10
  328.4 16.0 %attend_back.2.refs_0_ = bf16[3,1024,768]{2,1,0:T(8,128)(2,1)} custom-call(s32[2]{0:T(128)} %lengths.9, bf16[1024,2304]{1,0:T(8,128)(2,1)} %get-tuple-element.145.q_ref.k_ref.v_ref.refs_14_, bf16[1024,2304]{1,0:T(8,128)(2,1)} %get-tuple-element.145.q_ref.k_ref.v_ref.refs_14_, bf16[1024,2304]{1,0:T(8,128)(2,1)} %get-tuple-element.145.q_ref.k_ref.v_ref.refs_14_, ...), custom_call_target="tpu_custom_call" | custom-call | tf_op jit(solution)/shard_map/attend_back/pallas_call | solution.py:183
  351.3 15.9 %attend_back.3.refs_0_.refs_1_.refs_15_ = bf16[3,1024,768]{2,1,0:T(8,128)(2,1)} custom-call(s32[2]{0:T(128)} %lengths.9, bf16[1024,2304]{1,0:T(8,128)(2,1)} %get-tuple-element.145.q_ref.k_ref.v_ref.refs_14_, bf16[1024,2304]{1,0:T(8,128)(2,1)} %get-tuple-element.145.q_ref.k_ref.v_ref.refs_14_, ...), custom_call_target="tpu_custom_call", output_to_operand_aliasing={{}: (6, {})} | custom-call | tf_op jit(solution)/shard_map/attend_back/pallas_call | solution.py:183
  367.3 7.3 %collective-permute-done.26 = bf16[2,2,240,768]{3,2,1,0:T(8,128)(2,1)S(1)} collective-permute-done((bf16[2,2,240,768]{3,2,1,0:T(8,128)(2,1)}, bf16[2,2,240,768]{3,2,1,0:T(8,128)(2,1)S(1)}, u32[]{:S(2)}, u32[]{:S(2)}) %collective-permute-start.26) | collective-permute-done | bytes 1474592 | tf_op jit(solution)/shard_map/ppermute | solution.py:47
  389.6 15.4 %first_back.1 = (bf16[16,768]{1,0:T(8,128)(2,1)}, bf16[16,3072]{1,0:T(8,128)(2,1)}, bf16[16,768]{1,0:T(8,128)(2,1)}, f32[16,768]{1,0:T(8,128)}, f32[8,768]{1,0:T...) custom-call(s32[2]{0:T(128)} %lengths.9, bf16[16,768]{1,0:T(8,128)(2,1)} %copy-done.24, ...), custom_call_target="tpu_custom_call" | custom-call | tf_op jit(solution)/shard_map/first_back/pallas_call | solution.py:521
  411.3 4.7 collective-permute-done.29
  428.8 4.6 collective-permute-done.34
  433.4 7.8 %weight_grad.9 = (bf16[8,144,768]{2,1,0:T(8,128)(2,1)}, bf16[8,144,768]{2,1,0:T(8,128)(2,1)}) custom-call(s32[1]{0:T(128)} %bitcast.11.place, bf16[1024,768]{1,0:T(8,128)(2,1)} %get-tuple-element.148.x_ref.left_ref, bf16[3,1024,768]{2,1,0:T(8,128)(2,1)} %get-tuple-element.257.right_ref.parts_ref), custom_call_target="tpu_custom_call" | custom-call | tf_op jit(solution)/shard_map/weight_grad/pallas_call | solution.py:628
  449.9 10.7 %collective-permute-done.45 = f32[1920]{0:T(1024)S(1)} collective-permute-done((f32[1920]{0:T(1024)S(1)}, f32[1920]{0:T(1024)S(1)}, u32[]{:S(2)}, u32[]{:S(2)}) %collective-permute-start.45) | collective-permute-done | bytes 7712 | tf_op jit(solution)/shard_map/ppermute | solution.py:47
  491.8 15.5 %collective-permute-done.38 = bf16[2,2,144,768]{3,2,1,0:T(8,128)(2,1)S(1)} collective-permute-done((bf16[2,2,144,768]{3,2,1,0:T(8,128)(2,1)}, bf16[2,2,144,768]{3,2,1,0:T(8,128)(2,1)S(1)}, u32[]{:S(2)}, u32[]{:S(2)}) %collective-permute-start.38) | collective-permute-done | bytes 884768 | tf_op jit(solution)/shard_map/ppermute | solution.py:47
  515.1 5.9 %collective-permute-done.39 = bf16[2,144,768]{2,1,0:T(8,128)(2,1)S(1)} collective-permute-done((bf16[2,144,768]{2,1,0:T(8,128)(2,1)}, bf16[2,144,768]{2,1,0:T(8,128)(2,1)S(1)}, u32[]{:S(2)}, u32[]{:S(2)}) %collective-permute-start.39) | collective-permute-done | bytes 442400 | tf_op jit(solution)/shard_map/ppermute | solution.py:47
  525.8 4.8 fusion.11
  530.6 8.8 %input_gradient.1 = f32[1024,768]{1,0:T(8,128)} custom-call(s32[1]{0:T(128)} %bitcast.decoder, bf16[3,1024,768]{2,1,0:T(8,128)(2,1)} %get-tuple-element.257.right_ref.parts_ref, f32[1024,768]{1,0:T(8,128)} %get-tuple-element.221.refs_2_.refs_3_.one_ref, f32[16,768]{1,0:T(8,128)} %get-tuple-element.258.first_ref, bf16[768,2304]{1,0:T(8,128)(2,1)} %bitcast.204), custom_call_target="tpu_custom_call" | custom-call | tf_op jit(solution)/shard_map/input_gradient/pallas_call | solution.py:576
  539.4 12.9 %assemble.1 = bf16[128,30720]{1,0:T(8,128)(2,1)} custom-call(s32[1]{0:T(128)} %bitcast.11.place, bf16[4,128,1920]{2,1,0:T(8,128)(2,1)} %all-to-all-done.own_ref, bf16[4,128,1920]{2,1,0:T(8,128)(2,1)} %all-to-all-done.1.far_ref, bf16[4,128,3840]{2,1,0:T(8,128)(2,1)} %all-to-all-done.2.side_ref.side_far_ref, ...), custom_call_target="tpu_custom_call" | custom-call | tf_op jit(solution)/shard_map/assemble/pallas_call | solution.py:916
  (295 shorter events, 201.3 us)
Async XLA Ops:
  5.0 67.0 %collective-permute-start.1 = (bf16[960,768]{1,0:T(8,128)(2,1)S(1)}, bf16[960,768]{1,0:T(8,128)(2,1)}, u32[]{:S(2)}, u32[]{:S(2)}) collective-permute-start(bf16[960,768]{1,0:T(8,128)(2,1)S(1)} %constant_dynamic-slice_fusion.2), channel_id=1, source_target_pairs={{0,4},{1,5},{2,6},{3,7},{4,0},{5,1},{6,2},{7,3},{8,12},{9,13},{10,... | collective-permute-start | bytes 4423688 | tf_op jit(solution)/shard_map/ppermute | solution.py:47
  8.1 86.4 %collective-permute-start.2 = (bf16[960,768]{1,0:T(8,128)(2,1)S(1)}, bf16[960,768]{1,0:T(8,128)(2,1)}, u32[]{:S(2)}, u32[]{:S(2)}) collective-permute-start(bf16[960,768]{1,0:T(8,128)(2,1)S(1)} %constant_dynamic-slice_fusion.2), channel_id=1, source_target_pairs={{0,8},{1,9},{2,10},{3,11},{4,12},{5,13},{6,14},{7,15},{8,0},{9,1},... | collective-permute-start | bytes 4423688 | tf_op jit(solution)/shard_map/ppermute | solution.py:47
  10.7 83.8 %collective-permute-start.3 = (bf16[1920]{0:T(1024)(128)(2,1)S(1)}, bf16[1920]{0:T(1024)(128)(2,1)S(1)}, u32[]{:S(2)}, u32[]{:S(2)}) collective-permute-start(bf16[1920]{0:T(1024)(128)(2,1)S(1)} %copy-done.30), channel_id=1, source_target_pairs={{0,8},{1,9},{2,10},{3,11},{4,12},{5,13},{6,14},{7,15},{8,0},{9,1},... | collective-permute-start | bytes 11528 | tf_op jit(solution)/shard_map/ppermute | solution.py:47
  11.0 83.5 %collective-permute-start.4 = (bf16[1920]{0:T(1024)(128)(2,1)S(1)}, bf16[1920]{0:T(1024)(128)(2,1)S(1)}, u32[]{:S(2)}, u32[]{:S(2)}) collective-permute-start(bf16[1920]{0:T(1024)(128)(2,1)S(1)} %copy-done.30), channel_id=1, source_target_pairs={{0,4},{1,5},{2,6},{3,7},{4,0},{5,1},{6,2},{7,3},{8,12},{9,13},{10,... | collective-permute-start | bytes 11528 | tf_op jit(solution)/shard_map/ppermute | solution.py:47
  97.7 33.7 %collective-permute-start.9 = (bf16[960,768]{1,0:T(8,128)(2,1)}, bf16[960,768]{1,0:T(8,128)(2,1)S(1)}, u32[]{:S(2)}, u32[]{:S(2)}) collective-permute-start(bf16[960,768]{1,0:T(8,128)(2,1)} %collective-permute-done.2.mine_ref), channel_id=1, source_target_pairs={{0,16},{16,0},{1,17},{17,1},{2,18},{18,2},{3,19},{19,3},{4,20},{20... | collective-permute-start | bytes 4423688 | tf_op jit(solution)/shard_map/ppermute | solution.py:972
  157.4 35.0 %collective-permute-start.14 = (bf16[960,768]{1,0:T(8,128)(2,1)}, bf16[960,768]{1,0:T(8,128)(2,1)}, u32[]{:S(2)}, u32[]{:S(2)}) collective-permute-start(bf16[960,768]{1,0:T(8,128)(2,1)} %collective-permute-done.1.own_mine), channel_id=1, source_target_pairs={{0,16},{16,0},{1,17},{17,1},{2,18},{18,2},{3,19},{19,3},{4,20},{20... | collective-permute-start | bytes 4423688 | tf_op jit(solution)/shard_map/ppermute | solution.py:972
  160.2 34.7 %collective-permute-start.15 = (bf16[960,768]{1,0:T(8,128)(2,1)}, bf16[960,768]{1,0:T(8,128)(2,1)}, u32[]{:S(2)}, u32[]{:S(2)}) collective-permute-start(bf16[960,768]{1,0:T(8,128)(2,1)} %collective-permute-done.2.mine_ref), channel_id=1, source_target_pairs={{0,4},{1,5},{2,6},{3,7},{4,0},{5,1},{6,2},{7,3},{8,12},{9,13},{10,... | collective-permute-start | bytes 4423688 | tf_op jit(solution)/shard_map/ppermute | solution.py:47
  160.2 34.7 %all-to-all-start = ((bf16[4,128,1920]{2,1,0:T(8,128)(2,1)}), bf16[4,128,1920]{2,1,0:T(8,128)(2,1)}, u32[]{:S(2)}, u32[]{:S(2)}) async-start(bf16[4,128,1920]{2,1,0:T(8,128)(2,1)} %get-tuple-element.165), calls=%async_computation | async-start | bytes 3932160 | tf_op jit(solution)/shard_map/all_to_all | solution.py:1027
  214.3 40.4 %collective-permute-start.20 = (bf16[960,768]{1,0:T(8,128)(2,1)}, bf16[960,768]{1,0:T(8,128)(2,1)}, u32[]{:S(2)}, u32[]{:S(2)}) collective-permute-start(bf16[960,768]{1,0:T(8,128)(2,1)} %collective-permute-done.15.far_mine), channel_id=1, source_target_pairs={{0,16},{16,0},{1,17},{17,1},{2,18},{18,2},{3,19},{19,3},{4,20},{20... | collective-permute-start | bytes 4423688 | tf_op jit(solution)/shard_map/ppermute | solution.py:972
  218.6 36.0 %all-to-all-start.1 = ((bf16[4,128,1920]{2,1,0:T(8,128)(2,1)}), bf16[4,128,1920]{2,1,0:T(8,128)(2,1)}, u32[]{:S(2)}, u32[]{:S(2)}) async-start(bf16[4,128,1920]{2,1,0:T(8,128)(2,1)} %get-tuple-element.181), calls=%async_computation.1 | async-start | bytes 3932160 | tf_op jit(solution)/shard_map/all_to_all | solution.py:1027
  225.8 54.3 %collective-permute-start.21 = (bf16[960,768]{1,0:T(8,128)(2,1)}, bf16[960,768]{1,0:T(8,128)(2,1)}, u32[]{:S(2)}, u32[]{:S(2)}) collective-permute-start(bf16[960,768]{1,0:T(8,128)(2,1)} %constant_dynamic-slice_fusion.1), channel_id=1, source_target_pairs={{0,16},{16,0},{1,17},{17,1},{2,18},{18,2},{3,19},{19,3},{4,20},{20... | collective-permute-start | bytes 4423688 | tf_op jit(solution)/shard_map/ppermute | solution.py:972
  280.1 22.0 %collective-permute-start.22 = (bf16[8,240,768]{2,1,0:T(8,128)(2,1)}, bf16[8,240,768]{2,1,0:T(8,128)(2,1)}, u32[]{:S(2)}, u32[]{:S(2)}) collective-permute-start(bf16[8,240,768]{2,1,0:T(8,128)(2,1)} %get-tuple-element.202), channel_id=1, source_target_pairs={{0,1},{1,0},{2,3},{3,2},{4,5},{5,4},{6,7},{7,6},{8,9},{9,8},{10,11... | collective-permute-start | bytes 8847368 | tf_op jit(solution)/shard_map/ppermute | solution.py:47
  292.4 31.3 %collective-permute-start.24 = (bf16[8,240,768]{2,1,0:T(8,128)(2,1)}, bf16[8,240,768]{2,1,0:T(8,128)(2,1)}, u32[]{:S(2)}, u32[]{:S(2)}) collective-permute-start(bf16[8,240,768]{2,1,0:T(8,128)(2,1)} %get-tuple-element.209), channel_id=1, source_target_pairs={{0,1},{1,0},{2,3},{3,2},{4,5},{5,4},{6,7},{7,6},{8,9},{9,8},{10,11... | collective-permute-start | bytes 8847368 | tf_op jit(solution)/shard_map/ppermute | solution.py:47
  292.9 86.0 %all-to-all-start.2 = ((bf16[4,128,3840]{2,1,0:T(8,128)(2,1)}), bf16[4,128,3840]{2,1,0:T(8,128)(2,1)}, u32[]{:S(2)}, u32[]{:S(2)}) async-start(bf16[4,128,3840]{2,1,0:T(8,128)(2,1)} %side_scores.1), calls=%async_computation.2 | async-start | bytes 7864320 | tf_op jit(solution)/shard_map/all_to_all | solution.py:1027
  300.7 19.6 %collective-permute-start.23 = (bf16[240,768]{1,0:T(8,128)(2,1)S(1)}, bf16[240,768]{1,0:T(8,128)(2,1)S(1)}, u32[]{:S(2)}, u32[]{:S(2)}) collective-permute-start(bf16[240,768]{1,0:T(8,128)(2,1)S(1)} %get-tuple-element.302), channel_id=1, source_target_pairs={{0,8},{1,9},{2,10},{3,11},{4,12},{5,13},{6,14},{7,15},{8,0},{9,1},... | collective-permute-start | bytes 1105928 | tf_op jit(solution)/shard_map/ppermute | solution.py:47
  320.3 54.3 %collective-permute-start.26 = (bf16[2,2,240,768]{3,2,1,0:T(8,128)(2,1)}, bf16[2,2,240,768]{3,2,1,0:T(8,128)(2,1)S(1)}, u32[]{:S(2)}, u32[]{:S(2)}) collective-permute-start(bf16[2,2,240,768]{3,2,1,0:T(8,128)(2,1)} %bitcast.296), channel_id=1, source_target_pairs={{0,2},{1,3},{2,0},{3,1},{4,6},{5,7},{6,4},{7,5},{8,10},{9,11},{10,... | collective-permute-start | bytes 4423688 | tf_op jit(solution)/shard_map/ppermute | solution.py:47
  322.8 21.6 %collective-permute-start.25 = (bf16[240,768]{1,0:T(8,128)(2,1)S(1)}, bf16[240,768]{1,0:T(8,128)(2,1)S(1)}, u32[]{:S(2)}, u32[]{:S(2)}) collective-permute-start(bf16[240,768]{1,0:T(8,128)(2,1)S(1)} %get-tuple-element.212), channel_id=1, source_target_pairs={{0,8},{1,9},{2,10},{3,11},{4,12},{5,13},{6,14},{7,15},{8,0},{9,1},... | collective-permute-start | bytes 1105928 | tf_op jit(solution)/shard_map/ppermute | solution.py:47
  344.4 34.4 %collective-permute-start.27 = (bf16[240,768]{1,0:T(8,128)(2,1)S(1)}, bf16[240,768]{1,0:T(8,128)(2,1)S(1)}, u32[]{:S(2)}, u32[]{:S(2)}) collective-permute-start(bf16[240,768]{1,0:T(8,128)(2,1)S(1)} %get-tuple-element.219), channel_id=1, source_target_pairs={{0,8},{1,9},{2,10},{3,11},{4,12},{5,13},{6,14},{7,15},{8,0},{9,1},... | collective-permute-start | bytes 1105928 | tf_op jit(solution)/shard_map/ppermute | solution.py:47
  385.4 43.4 %collective-permute-start.35 = (bf16[960,768]{1,0:T(8,128)(2,1)}, bf16[960,768]{1,0:T(8,128)(2,1)}, u32[]{:S(2)}, u32[]{:S(2)}) collective-permute-start(bf16[960,768]{1,0:T(8,128)(2,1)} %constant_dynamic-slice_fusion), channel_id=1, source_target_pairs={{0,16},{16,0},{1,17},{17,1},{2,18},{18,2},{3,19},{19,3},{4,20},{20... | collective-permute-start | bytes 4423688 | tf_op jit(solution)/shard_map/ppermute | solution.py:972
  388.0 36.5 %collective-permute-start.33 = (bf16[2,2,240,768]{3,2,1,0:T(8,128)(2,1)}, bf16[2,2,240,768]{3,2,1,0:T(8,128)(2,1)S(1)}, u32[]{:S(2)}, u32[]{:S(2)}) collective-permute-start(bf16[2,2,240,768]{3,2,1,0:T(8,128)(2,1)} %bitcast.52), channel_id=1, source_target_pairs={{0,2},{1,3},{2,0},{3,1},{4,6},{5,7},{6,4},{7,5},{8,10},{9,11},{10,... | collective-permute-start | bytes 4423688 | tf_op jit(solution)/shard_map/ppermute | solution.py:47
  416.2 17.2 %collective-permute-start.34 = (bf16[240,768]{1,0:T(8,128)(2,1)}, bf16[240,768]{1,0:T(8,128)(2,1)}, u32[]{:S(2)}, u32[]{:S(2)}) collective-permute-start(bf16[240,768]{1,0:T(8,128)(2,1)} %get-tuple-element.236), channel_id=1, source_target_pairs={{0,8},{1,9},{2,10},{3,11},{4,12},{5,13},{6,14},{7,15},{8,0},{9,1},... | collective-permute-start | bytes 1105928 | tf_op jit(solution)/shard_map/ppermute | solution.py:47
  422.9 18.4 %collective-permute-start.31 = (bf16[4,56,768]{2,1,0:T(8,128)(2,1)S(1)}, bf16[4,56,768]{2,1,0:T(8,128)(2,1)}, u32[]{:S(2)}, u32[]{:S(2)}) collective-permute-start(bf16[4,56,768]{2,1,0:T(8,128)(2,1)S(1)} %bitcast.264), channel_id=1, source_target_pairs={{0,2},{1,3},{2,0},{3,1},{4,6},{5,7},{6,4},{7,5},{8,10},{9,11},{10,... | collective-permute-start | bytes 1032200 | tf_op jit(solution)/shard_map/ppermute | solution.py:47
  424.0 22.8 %collective-permute-start.36 = (bf16[2,240,768]{2,1,0:T(8,128)(2,1)}, bf16[2,240,768]{2,1,0:T(8,128)(2,1)}, u32[]{:S(2)}, u32[]{:S(2)}) collective-permute-start(bf16[2,240,768]{2,1,0:T(8,128)(2,1)} %bitcast.297), channel_id=1, source_target_pairs={{0,4},{1,5},{2,6},{3,7},{4,0},{5,1},{6,2},{7,3},{8,12},{9,13},{10,... | collective-permute-start | bytes 2211848 | tf_op jit(solution)/shard_map/ppermute | solution.py:47
  441.2 27.3 %collective-permute-start.42 = (bf16[2,240,768]{2,1,0:T(8,128)(2,1)}, bf16[2,240,768]{2,1,0:T(8,128)(2,1)S(1)}, u32[]{:S(2)}, u32[]{:S(2)}) collective-permute-start(bf16[2,240,768]{2,1,0:T(8,128)(2,1)} %bitcast.76), channel_id=1, source_target_pairs={{0,4},{1,5},{2,6},{3,7},{4,0},{5,1},{6,2},{7,3},{8,12},{9,13},{10,... | collective-permute-start | bytes 2211848 | tf_op jit(solution)/shard_map/ppermute | solution.py:47
  441.2 40.7 %collective-permute-start.37 = (bf16[8,144,768]{2,1,0:T(8,128)(2,1)}, bf16[8,144,768]{2,1,0:T(8,128)(2,1)S(1)}, u32[]{:S(2)}, u32[]{:S(2)}) collective-permute-start(bf16[8,144,768]{2,1,0:T(8,128)(2,1)} %get-tuple-element.248), channel_id=1, source_target_pairs={{0,1},{1,0},{2,3},{3,2},{4,5},{5,4},{6,7},{7,6},{8,9},{9,8},{10,11... | collective-permute-start | bytes 5308424 | tf_op jit(solution)/shard_map/ppermute | solution.py:47
  443.3 33.7 %collective-permute-start.32 = (bf16[8,56,768]{2,1,0:T(8,128)(2,1)}, bf16[8,56,768]{2,1,0:T(8,128)(2,1)}, u32[]{:S(2)}, u32[]{:S(2)}) collective-permute-start(bf16[8,56,768]{2,1,0:T(8,128)(2,1)} %bitcast.68), channel_id=1, source_target_pairs={{0,1},{1,0},{2,3},{3,2},{4,5},{5,4},{6,7},{7,6},{8,9},{9,8},{10,11... | collective-permute-start | bytes 2064392 | tf_op jit(solution)/shard_map/ppermute | solution.py:47
  443.9 16.7 %collective-permute-start.45 = (f32[1920]{0:T(1024)S(1)}, f32[1920]{0:T(1024)S(1)}, u32[]{:S(2)}, u32[]{:S(2)}) collective-permute-start(f32[1920]{0:T(1024)S(1)} %get-tuple-element.285), channel_id=1, source_target_pairs={{0,8},{1,9},{2,10},{3,11},{4,12},{5,13},{6,14},{7,15},{8,0},{9,1},... | collective-permute-start | bytes 23048 | tf_op jit(solution)/shard_map/ppermute | solution.py:47
  449.1 25.9 %collective-permute-start.41 = (bf16[240,768]{1,0:T(8,128)(2,1)}, bf16[240,768]{1,0:T(8,128)(2,1)}, u32[]{:S(2)}, u32[]{:S(2)}) collective-permute-start(bf16[240,768]{1,0:T(8,128)(2,1)} %bitcast.300), channel_id=1, source_target_pairs={{0,8},{1,9},{2,10},{3,11},{4,12},{5,13},{6,14},{7,15},{8,0},{9,1},... | collective-permute-start | bytes 1105928 | tf_op jit(solution)/shard_map/ppermute | solution.py:47
  468.5 57.2 %collective-permute-start.44 = (bf16[960,768]{1,0:T(8,128)(2,1)}, bf16[960,768]{1,0:T(8,128)(2,1)}, u32[]{:S(2)}, u32[]{:S(2)}) collective-permute-start(bf16[960,768]{1,0:T(8,128)(2,1)} %add_convert_fusion), channel_id=1, source_target_pairs={{0,16},{16,0},{1,17},{17,1},{2,18},{18,2},{3,19},{19,3},{4,20},{20... | collective-permute-start | bytes 4423688 | tf_op jit(solution)/shard_map/ppermute | solution.py:972
  471.7 40.4 %collective-permute-start.43 = (bf16[240,768]{1,0:T(8,128)(2,1)}, bf16[240,768]{1,0:T(8,128)(2,1)}, u32[]{:S(2)}, u32[]{:S(2)}) collective-permute-start(bf16[240,768]{1,0:T(8,128)(2,1)} %bitcast.299), channel_id=1, source_target_pairs={{0,8},{1,9},{2,10},{3,11},{4,12},{5,13},{6,14},{7,15},{8,0},{9,1},... | collective-permute-start | bytes 1105928 | tf_op jit(solution)/shard_map/ppermute | solution.py:47
  486.6 20.7 %collective-permute-start.38 = (bf16[2,2,144,768]{3,2,1,0:T(8,128)(2,1)}, bf16[2,2,144,768]{3,2,1,0:T(8,128)(2,1)S(1)}, u32[]{:S(2)}, u32[]{:S(2)}) collective-permute-start(bf16[2,2,144,768]{3,2,1,0:T(8,128)(2,1)} %get-tuple-element.260), channel_id=1, source_target_pairs={{0,4},{1,5},{2,6},{3,7},{4,0},{5,1},{6,2},{7,3},{8,12},{9,13},{10,... | collective-permute-start | bytes 2654216 | tf_op jit(solution)/shard_map/ppermute | solution.py:47
  523.9 28.5 %collective-permute-start.40 = (bf16[144,768]{1,0:T(8,128)(2,1)}, bf16[144,768]{1,0:T(8,128)(2,1)S(1)}, u32[]{:S(2)}, u32[]{:S(2)}) collective-permute-start(bf16[144,768]{1,0:T(8,128)(2,1)} %bitcast.301), channel_id=1, source_target_pairs={{0,8},{1,9},{2,10},{3,11},{4,12},{5,13},{6,14},{7,15},{8,0},{9,1},... | collective-permute-start | bytes 663560 | tf_op jit(solution)/shard_map/ppermute | solution.py:47
  (54 other events, 527.7 us)

commit v2 on v1

--- a/solution.py
+++ b/solution.py
@@ -13,7 +13,7 @@
 INV_ROOT_TAU = 0.3989422804014327
 HIDDEN = -1000000000.0
 LANES = 128
-VMEM = 56 * 1024 * 1024
+MIB = 1024 * 1024
 F32 = jnp.float32
 BF16 = jnp.bfloat16
 
@@ -51,23 +51,23 @@
     return [1 << i for i in range(order.bit_length() - 1)]
 
 
-def gather_all(block):
-    place = lax.axis_index("dp")
-    shape = block.shape
-    block = block[None]
-    for bit in reversed(bits_of(lax.axis_size("dp"))):
-        other = swapped(block, bit)
-        low = (place & bit) == 0
-        pair = [jnp.where(low, block, other), jnp.where(low, other, block)]
-        block = jnp.stack(pair, axis=1).reshape((-1,) + shape)
-    return block.reshape((-1,) + shape[1:])
-
-
-def gather_near(block):
-    near = lax.axis_size("dp") // 2
-    parts = [block] + [swapped(block, mask) for mask in range(2, near, 2)]
-    block = jnp.stack(parts)
-    return jnp.stack([block, swapped(block, 1)], axis=1).reshape((near,) + parts[0].shape)
+def tied(*values):
+    return lax.optimization_barrier(values)
+
+
+def side_by_side(blocks, other, bit):
+    low = (lax.axis_index("dp") & bit) == 0
+    pair = [jnp.where(low, blocks, other), jnp.where(low, other, blocks)]
+    return jnp.stack(pair, axis=1).reshape((-1,) + blocks.shape[1:])
+
+
+def gather_chips(block):
+    return [block] + [swapped(block, mask) for mask in range(2, lax.axis_size("dp") // 2, 2)]
+
+
+def gather_cores(blocks):
+    blocks = jnp.stack(blocks)
+    return jnp.stack([blocks, swapped(blocks, 1)], axis=1).reshape((-1,) + blocks.shape[1:])
 
 
 def scatter_near(blocks):
@@ -139,14 +139,13 @@
             jax.ShapeDtypeStruct((count * rows, width), BF16),
             jax.ShapeDtypeStruct((count * pairs, LANES // head_dim, rows), F32),
         ],
-        compiler_params=pltpu.CompilerParams(vmem_limit_bytes=VMEM),
+        compiler_params=pltpu.CompilerParams(vmem_limit_bytes=48 * MIB),
         name="attend",
     )(lengths, qkv, qkv, qkv)
 
 
-def attend_back_kernel(lengths, q_ref, k_ref, v_ref, grad_ref, log_ref, *refs, head_dim, passage):
-    out_ref = refs[-1]
-    length = lengths[passage]
+def attend_back_kernel(lengths, q_ref, k_ref, v_ref, grad_ref, log_ref, out_ref, *, head_dim):
+    length = lengths[pl.program_id(0)]
     rows, lanes = q_ref.shape
     scale = head_dim**-0.5
     q = q_ref[...] * scale
@@ -173,33 +172,31 @@
         out_ref[i] = total.astype(BF16)
 
 
-def attend_back(qkv, grad, logs, lengths, passage, done=()):
+def attend_back(qkv, grad, logs, lengths):
     count = lengths.shape[0]
     rows = qkv.shape[0] // count
     width = qkv.shape[1] // 3
     pairs = width // LANES
     head_dim = width // HEADS
-    block = lambda part: pl.BlockSpec((rows, LANES), lambda p, _: (passage, part * pairs + p))
-    return pl.pallas_call(
-        functools.partial(attend_back_kernel, head_dim=head_dim, passage=passage),
+    block = lambda part: pl.BlockSpec((rows, LANES), lambda b, p, _: (b, part * pairs + p))
+    return pl.pallas_call(
+        functools.partial(attend_back_kernel, head_dim=head_dim),
         grid_spec=pltpu.PrefetchScalarGridSpec(
             num_scalar_prefetch=1,
-            grid=(pairs,),
+            grid=(count, pairs),
             in_specs=[
                 block(0),
                 block(1),
                 block(2),
                 block(0),
-                pl.BlockSpec((1, LANES // head_dim, rows), lambda p, _: (passage * pairs + p, 0, 0)),
-            ]
-            + [pl.BlockSpec(memory_space=pl.ANY)] * len(done),
-            out_specs=pl.BlockSpec((3, rows, LANES), lambda p, _: (0, passage, p)),
+                pl.BlockSpec((1, LANES // head_dim, rows), lambda b, p, _: (b * pairs + p, 0, 0)),
+            ],
+            out_specs=pl.BlockSpec((3, rows, LANES), lambda b, p, _: (0, b, p)),
         ),
         out_shape=jax.ShapeDtypeStruct((3, count * rows, width), BF16),
-        input_output_aliases={6: 0} if done else {},
-        compiler_params=pltpu.CompilerParams(vmem_limit_bytes=VMEM),
+        compiler_params=pltpu.CompilerParams(vmem_limit_bytes=48 * MIB),
         name="attend_back",
-    )(lengths, qkv, qkv, qkv, grad, logs, *done)
+    )(lengths, qkv, qkv, qkv, grad, logs)
 
 
 def tail_kernel(
@@ -246,7 +243,7 @@
         in_specs=[by_row(width), by_row(width)] + [whole(m) for m in mats + (gain, bias, shift)],
         out_specs=[by_row(n) for n, _ in widths],
         out_shape=[shape(n, kind) for n, kind in widths],
-        compiler_params=pltpu.CompilerParams(vmem_limit_bytes=VMEM),
+        compiler_params=pltpu.CompilerParams(vmem_limit_bytes=48 * MIB),
         name="layer_tail",
     )(ctx, x, *mats, gain, bias, shift)
 
@@ -306,7 +303,7 @@
         + [pl.BlockSpec((8, width), lambda i: (0, 0)), pl.BlockSpec((1, hidden), lambda i: (0, 0))],
         out_shape=[shape(n, kind) for n, kind in widths]
         + [jax.ShapeDtypeStruct((8, width), F32), jax.ShapeDtypeStruct((1, hidden), F32)],
-        compiler_params=pltpu.CompilerParams(vmem_limit_bytes=VMEM),
+        compiler_params=pltpu.CompilerParams(vmem_limit_bytes=48 * MIB),
         name="tail_back",
     )(grad, *kept, *mats, gain)
 
@@ -386,7 +383,7 @@
             out_specs=pl.BlockSpec((PACK, width), lambda *_: (0, 0)),
         ),
         out_shape=jax.ShapeDtypeStruct((PACK, width), BF16),
-        compiler_params=pltpu.CompilerParams(vmem_limit_bytes=VMEM),
+        compiler_params=pltpu.CompilerParams(vmem_limit_bytes=26 * MIB),
         name="cls_forward",
     )(lengths, *[x] * count, *rest)
 
@@ -422,7 +419,7 @@
         ),
         out_shape=[jax.ShapeDtypeStruct(x.shape, BF16), jax.ShapeDtypeStruct(qkv.shape, BF16)],
         input_output_aliases={2: 0, 3: 1},
-        compiler_params=pltpu.CompilerParams(vmem_limit_bytes=VMEM),
+        compiler_params=pltpu.CompilerParams(vmem_limit_bytes=8 * MIB),
         name="place_first",
     )(decoder, cls, x, qkv, joint, shift)
 
@@ -448,7 +445,7 @@
         + [whole(joint)],
         out_specs=pl.BlockSpec((PACK, width), lambda *_: (0, 0)),
         out_shape=jax.ShapeDtypeStruct((PACK, width), BF16),
-        compiler_params=pltpu.CompilerParams(vmem_limit_bytes=VMEM),
+        compiler_params=pltpu.CompilerParams(vmem_limit_bytes=48 * MIB),
         name="cls_back",
     )(*[parts] * count, *[one] * count, joint)
 
@@ -527,7 +524,7 @@
             out_specs=[spec for spec, _ in outs],
         ),
         out_shape=[shape for _, shape in outs],
-        compiler_params=pltpu.CompilerParams(vmem_limit_bytes=VMEM),
+        compiler_params=pltpu.CompilerParams(vmem_limit_bytes=32 * MIB),
         name="first_back",
     )(lengths, grad, *[array for array in kept for _ in range(count)], *rest)
 
@@ -545,7 +542,7 @@
         in_specs=[pl.BlockSpec((step, width), lambda i: (i, 0)), whole(joint), whole(shift)],
         out_specs=pl.BlockSpec((step, joint.shape[1]), lambda i: (i, 0)),
         out_shape=jax.ShapeDtypeStruct((rows, joint.shape[1]), BF16),
-        compiler_params=pltpu.CompilerParams(vmem_limit_bytes=VMEM),
+        compiler_params=pltpu.CompilerParams(vmem_limit_bytes=16 * MIB),
         name="project",
     )(x, joint, shift)
 
@@ -587,7 +584,7 @@
             out_specs=pl.BlockSpec((step, width), lambda i, _: (i, 0)),
         ),
         out_shape=jax.ShapeDtypeStruct(one.shape, F32),
-        compiler_params=pltpu.CompilerParams(vmem_limit_bytes=VMEM),
+        compiler_params=pltpu.CompilerParams(vmem_limit_bytes=48 * MIB),
         name="input_gradient",
     )(decoder, parts, one, one_first, joint)
 
@@ -639,7 +636,7 @@
             ),
             out_shape=[shape, shape],
             input_output_aliases={3: 0, 4: 1} if done else {},
-            compiler_params=pltpu.CompilerParams(vmem_limit_bytes=VMEM),
+            compiler_params=pltpu.CompilerParams(vmem_limit_bytes=48 * MIB),
             name="weight_grad",
         )(place.reshape(1), left, right, *done)
     return tuple(done)
@@ -684,7 +681,7 @@
             out_specs=[out, out],
         ),
         out_shape=[shape, shape],
-        compiler_params=pltpu.CompilerParams(vmem_limit_bytes=VMEM),
+        compiler_params=pltpu.CompilerParams(vmem_limit_bytes=48 * MIB),
         name="add_split",
     )(mine.reshape(1), *shaped, *shaped)
     return keep.reshape(rest + (rows, width)), send.reshape(rest + (rows, width))
@@ -713,10 +710,6 @@
     for bit in order:
         state = sent(added(state, bit), bit)
     return state[0].astype(F32) + state[1].astype(F32)
-
-
-def tied(*values):
-    return lax.optimization_barrier(values)
 
 
 def as_row(column):
@@ -740,14 +733,12 @@
     @pl.when(pl.program_id(0) == 0)
     def _():
         half = mine_ref.shape[0]
-        swap = section == 1
-        mine, other = mine_ref[...], other_ref[...]
-        out_ref[:half] = jnp.where(swap, other, mine)
-        out_ref[half:] = jnp.where(swap, mine, other)
-
-
-def word_kernel(place, head_ref, own_ref, mine_ref, other_ref, shift_ref, peak_ref, total_ref, own_logit_ref, far_logit_ref, scores_ref, far_ref, *, steps):
-    join(place[1], mine_ref, other_ref, far_ref)
+        out_ref[pl.ds(pl.multiple_of(section * half, 16), half)] = mine_ref[...]
+        out_ref[pl.ds(pl.multiple_of((1 - section) * half, 16), half)] = other_ref[...]
+
+
+def word_kernel(section, head_ref, own_ref, mine_ref, other_ref, shift_ref, peak_ref, total_ref, scores_ref, far_ref):
+    join(section[0], mine_ref, other_ref, far_ref)
     group, picks, _ = head_ref.shape
     width = own_ref.shape[1]
     rows = group * picks
@@ -766,86 +757,84 @@
         peak_ref[g] = as_row(peak[part])
         total_ref[g] = as_row(total[part])
 
-    @pl.when(pl.program_id(0) < steps)
-    def _():
-        for g in range(group):
-            part = slice(g * picks, (g + 1) * picks)
-            spot = jnp.bitwise_xor(lax.rem(place[0], group), g)
-            own_logit_ref[spot] = scores_ref[part, : own_ref.shape[0]].astype(BF16)
-            far_logit_ref[spot] = scores_ref[part, own_ref.shape[0] :].astype(BF16)
-
-
-def word_scores(place, head, own, mine, other, shift, group=4):
+
+def word_scores(section, head, own, mine, other, shift, group=4):
     near, picks, padded = head.shape
     vocab = shift.shape[1]
-    quarter = near // 2
-    steps = quarter // group
     row = pl.BlockSpec((group, 1, picks), lambda k, _: (k, 0, 0))
     row_shape = jax.ShapeDtypeStruct((near, 1, picks), F32)
-    spot = lambda k, p: (jnp.bitwise_xor(lax.rem(p[0], quarter) // group, jnp.minimum(k, steps - 1)), 0, 0)
-    return pl.pallas_call(
-        functools.partial(word_kernel, steps=steps),
+    return pl.pallas_call(
+        word_kernel,
         grid_spec=pltpu.PrefetchScalarGridSpec(
             num_scalar_prefetch=1,
             grid=(near // group,),
             in_specs=[pl.BlockSpec((group, picks, padded), lambda k, _: (k, 0, 0))]
             + [whole(array) for array in (own, mine, other, shift)],
-            out_specs=[row, row] + [pl.BlockSpec((group, picks, vocab // 2), spot)] * 2,
+            out_specs=[row, row],
             scratch_shapes=[pltpu.VMEM((group * picks, vocab), F32), pltpu.VMEM(own.shape, BF16)],
         ),
-        out_shape=[row_shape] * 2 + [jax.ShapeDtypeStruct((quarter, picks, vocab // 2), BF16)] * 2,
-        compiler_params=pltpu.CompilerParams(vmem_limit_bytes=VMEM),
+        out_shape=[row_shape] * 2,
+        compiler_params=pltpu.CompilerParams(vmem_limit_bytes=48 * MIB),
         name="word_scores",
-    )(place, head, own, mine, other, shift)
-
-
-def side_kernel(place, head_ref, own_mine, own_other, far_mine, far_other, shift_ref, logit_ref, own_ref, far_ref):
-    join(place[1], own_mine, own_other, own_ref)
-    join(place[1], far_mine, far_other, far_ref)
+    )(section, head, own, mine, other, shift)
+
+
+def logit_kernel(place, head_ref, *refs, wholes):
+    pairs = len(wholes)
+    tables = refs[: sum(1 if w else 2 for w in wholes)]
+    shift_ref, logit_ref, *joined = refs[len(tables) :]
     group, picks, _ = head_ref.shape
-    width = own_ref.shape[1]
+    width = tables[0].shape[1]
     head = head_ref[:, :, 0:width].reshape(group * picks, width)
-    for table, part, columns in word_cuts(own_ref.shape[0]):
-        scores = back_mul(head, (own_ref, far_ref)[table][part]) + shift_ref[0:1, columns]
-        scores = scores.astype(BF16)
+    slice_rows = shift_ref.shape[1] // pairs
+    for i, is_whole in enumerate(wholes):
+        table_ref, *tables = tables
+        if not is_whole:
+            mine_ref, (other_ref, *tables) = table_ref, tables
+            table_ref, *joined = joined
+            join(place[1], mine_ref, other_ref, table_ref)
+        columns = slice(i * slice_rows, (i + 1) * slice_rows)
+        scores = (back_mul(head, table_ref[...]) + shift_ref[0:1, columns]).astype(BF16)
         for g in range(group):
             spot = jnp.bitwise_xor(lax.rem(place[0], group), g)
             logit_ref[spot, :, columns] = scores[g * picks : (g + 1) * picks]
 
 
-def side_scores(place, head, own, far, shift, group=4):
-    tables = own + far
+def word_logits(place, head, tables, shift, group=4):
     near, picks, padded = head.shape
     vocab = shift.shape[1]
+    slice_rows = vocab // len(tables)
     quarter = near // 2
+    wholes = tuple(len(table) == 1 for table in tables)
+    arrays = [array for table in tables for array in table]
     spot = lambda k, p: (jnp.bitwise_xor(lax.rem(p[0], quarter) // group, k), 0, 0)
     return pl.pallas_call(
-        side_kernel,
+        functools.partial(logit_kernel, wholes=wholes),
         grid_spec=pltpu.PrefetchScalarGridSpec(
             num_scalar_prefetch=1,
             grid=(quarter // group,),
             in_specs=[pl.BlockSpec((group, picks, padded), lambda k, _: (k, 0, 0))]
-            + [whole(array) for array in tables + (shift,)],
+            + [whole(array) for array in arrays + [shift]],
             out_specs=pl.BlockSpec((group, picks, vocab), spot),
-            scratch_shapes=[pltpu.VMEM((vocab // 2, own[0].shape[1]), BF16)] * 2,
+            scratch_shapes=[pltpu.VMEM((slice_rows, arrays[0].shape[1]), BF16)] * (len(tables) - sum(wholes)),
         ),
         out_shape=jax.ShapeDtypeStruct((quarter, picks, vocab), BF16),
-        compiler_params=pltpu.CompilerParams(vmem_limit_bytes=VMEM),
-        name="side_scores",
-    )(place, head, *tables, shift)
-
-
-def word_back_kernel(first, head_ref, log_ref, own_ref, mine_ref, other_ref, shift_ref, grad_ref, out_ref, sums_ref, hit_ref, far_ref, *, masked):
+        compiler_params=pltpu.CompilerParams(vmem_limit_bytes=48 * MIB),
+        name="word_logits",
+    )(place, head, *arrays, shift)
+
+
+def labels_of(head_ref, width):
+    label = head_ref[:, :, width:].astype(F32)
+    label = label.reshape(-1, label.shape[2])
+    return (label[:, 0:1] * 256.0 + label[:, 1:2]).astype(jnp.int32)
+
+
+def word_back_kernel(first, head_ref, log_ref, own_ref, mine_ref, other_ref, shift_ref, grad_ref, out_ref, hit_ref, far_ref, *, masked):
     join(first[2], mine_ref, other_ref, far_ref)
-
-    @pl.when(pl.program_id(0) == 0)
-    def _():
-        sums_ref[...] = jnp.zeros_like(sums_ref)
-
     group, picks, width = out_ref.shape
     rows = group * picks
-    label = head_ref[:, :, width:].reshape(rows, -1).astype(F32)
-    label = (label[:, 0:1] * 256.0 + label[:, 1:2]).astype(jnp.int32)
+    label = labels_of(head_ref, width)
     logs = jnp.concatenate([as_column(log_ref[g]) for g in range(group)])
     head = head_ref[:, :, 0:width].reshape(rows, width)
     total = jnp.zeros((rows, width), F32)
@@ -857,8 +846,8 @@
         mine = lax.broadcasted_iota(jnp.int32, share.shape, 1) == label - (first[table] + part.start)
         hit = hit + jnp.sum(jnp.where(mine, scores, 0.0), axis=1, keepdims=True)
         grad = (jnp.where(mine, share - 1.0, share) * (1.0 / masked)).astype(BF16)
-        grad_ref[:, :, columns] = grad.reshape(group, picks, -1)
-        sums_ref[0:1, columns] += jnp.sum(grad.astype(F32), axis=0, keepdims=True)
+        if table == 0:
+            grad_ref[:, :, columns] = grad.reshape(group, picks, -1)
         total = total + matmul(grad, words)
     out_ref[...] = total.astype(BF16).reshape(group, picks, width)
     for g in range(group):
@@ -877,39 +866,94 @@
             num_scalar_prefetch=1,
             grid=(near // group,),
             in_specs=[block(padded), row] + [whole(array) for array in (own, mine, other, shift)],
-            out_specs=[block(vocab), block(width), pl.BlockSpec((1, vocab), lambda k, _: (0, 0)), row],
+            out_specs=[block(vocab // 2), block(width), row],
             scratch_shapes=[pltpu.VMEM(own.shape, BF16)],
         ),
         out_shape=[
-            jax.ShapeDtypeStruct((near, picks, vocab), BF16),
+            jax.ShapeDtypeStruct((near, picks, vocab // 2), BF16),
             jax.ShapeDtypeStruct((near, picks, width), BF16),
-            jax.ShapeDtypeStruct((1, vocab), F32),
             jax.ShapeDtypeStruct((near, 1, picks), F32),
         ],
-        compiler_params=pltpu.CompilerParams(vmem_limit_bytes=VMEM),
+        compiler_params=pltpu.CompilerParams(vmem_limit_bytes=48 * MIB),
         name="word_back",
     )(first, head, logs, own, mine, other, shift)
 
 
-def assemble_kernel(place, own_ref, far_ref, side_ref, side_far_ref, out_ref, *, quarter):
-    for i, ref in enumerate((own_ref, side_ref, far_ref, side_far_ref)):
-
-        @pl.when(jnp.bitwise_xor(place[0] // quarter, pl.program_id(0)) == i)
+def table_kernel(first, grad_ref, head_ref, other_ref, log_ref, own_ref, shift_ref, out_ref, sums_ref, total_ref, *, masked):
+    @pl.when(pl.program_id(0) == 0)
+    def _():
+        total_ref[...] = jnp.zeros_like(total_ref)
+        sums_ref[...] = jnp.zeros_like(sums_ref)
+
+    group, picks, slice_rows = grad_ref.shape
+    rows = group * picks
+    width = own_ref.shape[1]
+    label = labels_of(other_ref, width)
+    logs = jnp.concatenate([as_column(log_ref[g]) for g in range(group)])
+    head = head_ref[:, :, 0:width].reshape(rows, width)
+    other = other_ref[:, :, 0:width].reshape(rows, width)
+    for table, part, columns in word_cuts(slice_rows):
+        if table == 0:
+            share = jnp.exp(back_mul(other, own_ref[part]) + shift_ref[0:1, columns] - logs)
+            mine = lax.broadcasted_iota(jnp.int32, share.shape, 1) == label - (first[0] + part.start)
+            other_grad = (jnp.where(mine, share - 1.0, share) * (1.0 / masked)).astype(BF16)
+            grad = grad_ref[:, :, part].reshape(rows, -1)
+            sums_ref[0:1, part] += jnp.sum(grad.astype(F32) + other_grad.astype(F32), axis=0, keepdims=True)
+            total_ref[part] += outer_sum(grad, head) + outer_sum(other_grad, other)
+
+    @pl.when(pl.program_id(0) == pl.num_programs(0) - 1)
+    def _():
+        out_ref[...] = total_ref[...].astype(BF16)
+
+
+def table_gradient(first, grad, head, other, logs, own, shift, masked, group=4):
+    near, picks, slice_rows = grad.shape
+    padded, width = head.shape[2], own.shape[1]
+    block = lambda n: pl.BlockSpec((group, picks, n), lambda k, _: (k, 0, 0))
+    row = pl.BlockSpec((group, 1, picks), lambda k, _: (k, 0, 0))
+    return pl.pallas_call(
+        functools.partial(table_kernel, masked=masked),
+        grid_spec=pltpu.PrefetchScalarGridSpec(
+            num_scalar_prefetch=1,
+            grid=(near // group,),
+            in_specs=[block(slice_rows), block(padded), block(padded), row, whole(own), whole(shift)],
+            out_specs=[pl.BlockSpec(own.shape, lambda k, _: (0, 0)), pl.BlockSpec((1, slice_rows), lambda k, _: (0, 0))],
+            scratch_shapes=[pltpu.VMEM(own.shape, F32)],
+        ),
+        out_shape=[jax.ShapeDtypeStruct(own.shape, BF16), jax.ShapeDtypeStruct((1, slice_rows), F32)],
+        compiler_params=pltpu.CompilerParams(vmem_limit_bytes=48 * MIB),
+        name="table_gradient",
+    )(first, grad, head, other, logs, own, shift)
+
+
+def assemble_kernel(place, near_ref, side_ref, out_ref, *, quarter):
+    turn = jnp.bitwise_xor(place[0] // quarter, pl.program_id(0))
+    for i, ref in enumerate((near_ref, side_ref)):
+
+        @pl.when(turn % 2 == i)
         def _():
             out_ref[...] = ref[0]
 
 
-def assembled(place, own, far, side):
-    quarter, picks, slice_rows = own.shape
+def assembled(place, nears, sides):
+    quarter, picks, vocab = nears.shape
+    slice_rows = vocab // 2
     if slice_rows % LANES:
-        parts = jnp.stack([own, side[:, :, :slice_rows], far, side[:, :, slice_rows:]])
-        parts = jnp.take(parts, jnp.bitwise_xor(jnp.arange(4), place // quarter), axis=0)
-        return parts.transpose(2, 0, 1, 3).reshape(picks, 4 * quarter * slice_rows)
-
-    def spec(flip, column):
+        parts = jnp.stack([array.reshape(quarter, picks, 2, slice_rows) for array in (nears, sides)], axis=3)
+        parts = parts.reshape(quarter, picks, 4, slice_rows)
+        parts = jnp.take(parts, jnp.bitwise_xor(jnp.arange(4), place // quarter), axis=2)
+        return parts.transpose(1, 2, 0, 3).reshape(picks, 2 * quarter * vocab)
+
+    def spec(side):
         def index(b, j, p):
-            turn = jnp.bitwise_xor(p[0] // quarter, flip)
-            return jnp.where(b == turn, j, jnp.where(b < turn, 0, quarter - 1)), 0, column
+            turn = jnp.bitwise_xor(p[0] // quarter, b)
+            last = jnp.bitwise_xor(p[0] // quarter, jnp.bitwise_xor(b, 1)) // 2
+            first_of_pair = lax.rem(b, 2) == 0
+            return (
+                jnp.where(lax.rem(turn, 2) == side, j, jnp.where(first_of_pair, 0, quarter - 1)),
+                0,
+                jnp.where(lax.rem(turn, 2) == side, turn // 2, last),
+            )
 
         return pl.BlockSpec((1, picks, slice_rows), index)
 
@@ -918,13 +962,13 @@
         grid_spec=pltpu.PrefetchScalarGridSpec(
             num_scalar_prefetch=1,
             grid=(4, quarter),
-            in_specs=[spec(0, 0), spec(2, 0), spec(1, 0), spec(3, 1)],
+            in_specs=[spec(0), spec(1)],
             out_specs=pl.BlockSpec((picks, slice_rows), lambda b, j, _: (0, b * quarter + j)),
         ),
-        out_shape=jax.ShapeDtypeStruct((picks, 4 * quarter * slice_rows), BF16),
-        compiler_params=pltpu.CompilerParams(vmem_limit_bytes=VMEM),
+        out_shape=jax.ShapeDtypeStruct((picks, 2 * quarter * vocab), BF16),
+        compiler_params=pltpu.CompilerParams(vmem_limit_bytes=48 * MIB),
         name="assemble",
-    )(place.reshape(1), own, far, side, side)
+    )(place.reshape(1), nears, sides)
 
 
 def on_device(
@@ -967,16 +1011,12 @@
     near, quarter = groups // 2, groups // 4
     half = slice_rows // 2
     bits = bits_of(groups)
-    order = bits[1:]
-    joint_order = bits[-2:-1] + bits[1:-2] + bits[-1:]
+    order = bits[-2:-1] + bits[1:-2] + bits[-1:]
+    turned = bits[1:]
     across = lambda array: lax.ppermute(array, "section", [(0, 1), (1, 0)])
-    pick_half = lambda array, which: lax.dynamic_slice_in_dim(array, which * half, half)
-
-    def joined(mine, other):
-        return jnp.where(decoder, jnp.concatenate([other, mine]), jnp.concatenate([mine, other]))
-
-    my_half = pick_half(word_table, section)
-    far_mine = swapped(my_half, near)
+
+    my_half = lax.dynamic_slice_in_dim(word_table, section * half, half)
+    far_one, far_two = (swapped(piece, near) for piece in (my_half[: half // 2], my_half[half // 2 :]))
     side_half = swapped(my_half, quarter)
 
     x = embedded[0].reshape(total_rows, width)
@@ -986,14 +1026,18 @@
     cls_in = passed_along(cls_out, "section", 1)
     x, qkv = place_first(flag, cls_in, x, qkv, joint, joint_shift, count)
     ctx, logs = attend(qkv, lengths, count)
-    ctx, side_half = tied(ctx, side_half)
+    ctx, far_one = tied(ctx, far_one)
+    far_one_other = across(far_one)
     far_shift = swapped(word_bias, near)
     side_shift = swapped(word_bias, quarter)
     y, normed_one, scale_one, first_low, active, slope, normed_two, scale_two = layer_tail(
         ctx, x, mats, gain, bias, shift
     )
-    y, far_mine, far_shift, side_shift = tied(y, far_mine, far_shift, side_shift)
-    far_other = across(far_mine)
+    y, far_one_other, far_two, far_shift, side_shift, side_half = tied(
+        y, far_one_other, far_two, far_shift, side_shift, side_half
+    )
+    far_two_other = across(far_two)
+    far_mine = jnp.concatenate([far_one, far_two])
     side_far_shift = swapped(far_shift, quarter)
 
     chosen = positions[0][:, :, None] == jnp.arange(rows)[None, None, :]
@@ -1007,13 +1051,20 @@
     head_low = (normed_head * gain[2] + bias[7]).astype(BF16)
     answers = labels[0].reshape(-1, 1)
     answers = jnp.concatenate([answers // 256, answers % 256, jnp.zeros((picks, LANES - 2), jnp.int32)], axis=1)
-    head_all = gather_near(jnp.concatenate([head_low, answers.astype(BF16)], axis=1))
-    head_all, far_other, side_far_shift, side_half = tied(head_all, far_other, side_far_shift, side_half)
-    side_half_other = across(side_half)
+    head_low = jnp.concatenate([head_low, answers.astype(BF16)], axis=1)
+    head_all, head_low, far_two_other, side_far_shift = tied(
+        gather_chips(head_low), head_low, far_two_other, side_far_shift
+    )
+    head_all = gather_cores(head_all)
+    head_other = swapped(head_low, near)
+    far_other = jnp.concatenate([far_one_other, far_two_other])
     word_shift = jnp.concatenate([word_bias, far_shift]).astype(F32)[None]
     side_word_shift = jnp.concatenate([side_shift, side_far_shift]).astype(F32)[None]
     where_to = jnp.stack([place32, section.astype(jnp.int32)])
-    peak, total, *logits = word_scores(where_to, head_all, word_table, far_mine, far_other, word_shift)
+    head_all, side_half = tied(head_all, side_half)
+    side_half_other = across(side_half)
+    peak, total = word_scores(flag, head_all, word_table, far_mine, far_other, word_shift)
+    peak, head_other = tied(peak, head_other)
     grid = (2,) * (len(bits) - 1)
     peak, total = (array.reshape(grid + (picks,)) for array in (peak, total))
     for axis, bit in enumerate(reversed(bits[:-1])):
@@ -1022,32 +1073,29 @@
         total = total * jnp.exp(peak - top) + other_total * jnp.exp(other_peak - top)
         peak = top
     log_total = (peak + jnp.log(total)).reshape(near, 1, picks)
-    log_total, far_mine, *logits = tied(log_total, far_mine, *logits)
+    log_other = swapped(log_total, near)
+    head_other = gather_chips(head_other)
+    first = (jnp.stack([place, jnp.bitwise_xor(place, near)]) * slice_rows).astype(jnp.int32)
+    first = jnp.concatenate([first, flag])
+    score_grad, head_back, hits = word_back(
+        first, head_all, log_total, word_table, far_mine, far_other, word_shift, masked
+    )
+    head_back, side_half_other, head_other, log_other = tied(head_back, side_half_other, head_other, log_other)
+    head_other = gather_cores(head_other)
+    loss_part = jnp.sum(log_total[0]) - jnp.sum(hits)
+    head_grad = scatter_near(head_back)
+    table_grad, word_sums = table_gradient(
+        first, score_grad, head_all, head_other, log_other, word_table, word_shift, masked
+    )
+    head_grad, table_grad, word_sums, far_mine = tied(head_grad, table_grad, word_sums, far_mine)
+    word_other = across(word_sums)
     side_far_half = swapped(far_mine, quarter)
     exchanged = lambda part: lax.all_to_all(
         part, "dp", 0, 0, axis_index_groups=[list(range(i, i + quarter)) for i in range(0, groups, quarter)]
     )
-    logits_own = exchanged(logits[0])
-    first = (jnp.stack([place, jnp.bitwise_xor(place, near)]) * slice_rows).astype(jnp.int32)
-    first = jnp.concatenate([first, flag])
-    score_grad, head_back, word_sums, hits = word_back(
-        first, head_all, log_total, word_table, far_mine, far_other, word_shift, masked
-    )
-    head_back, logits_own, side_half_other, side_far_half = tied(
-        head_back, logits_own, side_half_other, side_far_half
-    )
-    side_far_other = across(side_far_half)
-    loss_part = jnp.sum(log_total[0]) - jnp.sum(hits)
-    head_grad = scatter_near(head_back)
-
-    score_grad = score_grad.reshape(near * picks, 2 * slice_rows)
-    head_rows = head_all[:, :, :width].reshape(near * picks, width)
-    own_grad, far_grad = (
-        outer_sum(score_grad[:, i * slice_rows : (i + 1) * slice_rows], head_rows).astype(BF16) for i in range(2)
-    )
-    head_grad, own_grad, far_grad, logits_far = tied(head_grad, own_grad, far_grad, logits[1])
-    logits_far = exchanged(logits_far)
-    far_got = across(pick_half(far_grad, 1 - section))
+    logits_near = word_logits(where_to, head_all, ((word_table,), (far_mine, far_other)), word_shift)
+    head_grad, logits_near = tied(head_grad, logits_near)
+    logits_near = exchanged(logits_near)
 
     gain_head = jnp.sum(head_grad * normed_head, 0)
     shift_head = jnp.sum(head_grad, 0)
@@ -1060,71 +1108,35 @@
 
     kept = (normed_two, scale_two, slope, normed_one, scale_one)
     branch, hidden, one, mixed, ctx_grad, sums, shift_sum = tail_back(grad, kept, mats, gain)
-    hidden, branch, side_far_other, side_half_other, logits_far = tied(
-        hidden, branch, side_far_other, side_half_other, logits_far
-    )
-    logits_side = side_scores(
-        where_to, head_all, (side_half, side_half_other), (side_far_half, side_far_other), side_word_shift
-    )
-    branch, logits_side = tied(branch, logits_side)
+    hidden, branch, side_far_half, word_other = tied(hidden, branch, side_far_half, word_other)
+    side_far_other = across(side_far_half)
+    one_pair = weight_grads(place32, (active, branch), (ctx, mixed))
+    hidden, one_pair = tied(hidden, one_pair)
+    one_state = first_hop(one_pair)
+    two_pair = weight_grads(place32, (first_low, hidden), (picked_low, dense_grad))
+    ctx_grad, two_pair, logits_near = tied(ctx_grad, two_pair, logits_near)
+    two_state = first_hop(two_pair)
+    one_halves, two_halves = added(one_state, order[0]), added(two_state, turned[0])
+    ctx_grad, one_now, two_now = tied(ctx_grad, one_halves[:2], two_halves[:2])
+    one_state, two_state = sent((*one_now, one_halves[2]), order[0]), sent((*two_now, two_halves[2]), turned[0])
+    parts = attend_back(qkv, ctx_grad, logs, lengths)
+    one_halves, two_halves = added(one_state, order[1]), added(two_state, turned[1])
+    parts, one_now, two_now, side_far_other = tied(parts, one_halves[:2], two_halves[:2], side_far_other)
+    logits_side = word_logits(
+        where_to, head_all, ((side_half, side_half_other), (side_far_half, side_far_other)), side_word_shift
+    )
+    one_state, two_state = sent((*one_now, one_halves[2]), order[1]), sent((*two_now, two_halves[2]), turned[1])
     logits_side = exchanged(logits_side)
-    one_pair = weight_grads(place32, (active, branch), (ctx, mixed))
-    hidden, one_pair, far_got = tied(hidden, one_pair, far_got)
-    one_state = first_hop(one_pair)
-    far_half = (pick_half(far_grad, section).astype(F32) + far_got.astype(F32)).astype(BF16)
-    far_quarters = [far_half[i * half // 4 : (i + 1) * half // 4] for i in range(4)]
-    far_quarters[0] = swapped(far_quarters[0], near)
-    two_pair = weight_grads(place32, (first_low, hidden), (picked_low, dense_grad))
-    ctx_grad, two_pair = tied(ctx_grad, two_pair)
-    two_state = first_hop(two_pair)
-    halves = added(one_state, order[0])
-    ctx_grad, halves_now, far_quarters[0], far_quarters[1] = tied(
-        ctx_grad, halves[:2], far_quarters[0], far_quarters[1]
-    )
-    one_state = sent((*halves_now, halves[2]), order[0])
-    far_quarters[1] = swapped(far_quarters[1], near)
-    parts = attend_back(qkv, ctx_grad, logs, lengths, 0)
-    halves = added(two_state, order[0])
-    parts, halves_now, far_quarters[1], far_quarters[2] = tied(
-        parts, halves[:2], far_quarters[1], far_quarters[2]
-    )
-    two_state = sent((*halves_now, halves[2]), order[0])
-    far_quarters[2] = swapped(far_quarters[2], near)
-    own_got = across(pick_half(own_grad, 1 - section))
-    for passage in range(1, count):
-        parts = attend_back(qkv, ctx_grad, logs, lengths, passage, (parts,))
-    halves = added(one_state, order[1])
-    parts, halves_now, logits_side, far_quarters[2], far_quarters[3] = tied(
-        parts, halves[:2], logits_side, far_quarters[2], far_quarters[3]
-    )
-    one_state = sent((*halves_now, halves[2]), order[1])
     cls_grad = passed_along(cls_back(parts, one, joint, count), "section", -1)
-    far_quarters[3] = swapped(far_quarters[3], near)
+    cls_grad, table_grad = tied(cls_grad, table_grad)
+    table_top = across(table_grad[:half])
 
     branch_f, hidden_f, mixed_f, one_f, sums_f, shift_f, parts, part_sums = first_back(
         cls_grad, kept, mats, gain, qkv, parts, lengths
     )
-    halves = added(two_state, order[1])
-    parts, halves_now, far_quarters[3], own_got = tied(parts, halves[:2], far_quarters[3], own_got)
-    two_state = sent((*halves_now, halves[2]), order[1])
-    joint_pair = weight_grads(place32, (x, parts))
-    parts, joint_pair = tied(parts, joint_pair)
-    joint_state = first_hop(joint_pair)
-    own_half = pick_half(own_grad, section).astype(F32) + own_got.astype(F32)
-    own_half = (own_half + jnp.concatenate(far_quarters).astype(F32)).astype(BF16)
-    table_total = joined(own_half, across(own_half)).astype(F32)
-    word_total = word_sums[0, :slice_rows] + swapped(word_sums[0, slice_rows:], near)
-    word_total = word_total + across(word_total)
-    halves = added(one_state, order[2])
-    parts, halves_now = tied(parts, halves[:2])
-    one_state = sent((*halves_now, halves[2]), order[2])
-    halves = added(joint_state, joint_order[0])
-    parts, halves_now, *logits = tied(parts, halves[:2], logits_own, logits_far, logits_side)
-    joint_state = sent((*halves_now, halves[2]), joint_order[0])
-    input_grad = input_gradient(flag, parts, one, one_f, joint, count)
-    joint_sum = unstacked(rest_of(joint_state, joint_order[1:]), [(own, 3 * width)])[0]
-    contract_sum, mixer_sum = unstacked(rest_of(one_state, order[3:]), [(units // groups, width), (own, width)])
-    expand_sum, head_sum = unstacked(rest_of(two_state, order[2:]), [(own, units), (own, width)])
+    two_halves = added(two_state, turned[2])
+    parts, two_now = tied(parts, two_halves[:2])
+    two_state = sent((*two_now, two_halves[2]), turned[2])
 
     def firsts(array):
         return jnp.concatenate([array[b * rows : b * rows + 1] for b in range(count)])
@@ -1149,11 +1161,50 @@
     small_high = small_high.astype(BF16)
     mine = mine.reshape(-1, width)
     counts = [mine.shape[0], small.shape[0], small.shape[0]]
-    rows_all = gather_all(jnp.concatenate([mine, small_high, small_low]))
-    rows_all = rows_all.reshape(groups, -1, width)
+    gathered = jnp.concatenate([mine, small_high, small_low])[None]
+    arriving = swapped(gathered, near)
+    joint_pair = weight_grads(place32, (x, parts))
+    parts, joint_pair, arriving, logits_side = tied(parts, joint_pair, arriving, logits_side)
+    joint_state = first_hop(joint_pair)
+    gathered = side_by_side(gathered, arriving, near)
+    arriving = swapped(gathered, quarter)
+    joint_halves = added(joint_state, order[0])
+    parts, joint_now, arriving = tied(parts, joint_halves[:2], arriving)
+    joint_state = sent((*joint_now, joint_halves[2]), order[0])
+    bit = quarter
+    for below in reversed(bits[:-2]):
+        gathered = side_by_side(gathered, arriving, bit)
+        arriving = swapped(gathered, below)
+        bit = below
+        if bit == 2:
+            input_grad = input_gradient(flag, parts, one, one_f, joint, count)
+            input_grad, logits_near, logits_side = tied(input_grad, logits_near, logits_side)
+            logits_out = assembled(place32, logits_near, logits_side)
+            logits_out, arriving = tied(logits_out, arriving)
+    logits_out, one_got, table_top = tied(logits_out, one_state[1], table_top)
+    table_rest = across(table_grad[half:])
+    one_halves = added((one_state[0], one_got, one_state[2]), order[2])
+    logits_out, one_now = tied(logits_out, one_halves[:2])
+    one_state = sent((*one_now, one_halves[2]), order[2])
+    joint_keep, joint_got, logits_out, input_grad, two_got = tied(
+        *joint_state[:2], logits_out, input_grad, two_state[1]
+    )
+    two_state = two_state[0], two_got, two_state[2]
+    joint_state = sent(added((joint_keep, joint_got, joint_state[2]), order[1]), order[1])
+    expand_sum, head_sum = unstacked(rest_of(two_state, turned[3:]), [(own, units), (own, width)])
+    joint_keep, joint_got, expand_sum, head_sum = tied(*joint_state[:2], expand_sum, head_sum)
+    joint_keep, joint_send, axes = added((joint_keep, joint_got, joint_state[2]), order[2])
+    joint_got = swapped(joint_send, order[2])
+    joint_keep, arriving, one_got, table_rest = tied(joint_keep, arriving, one_state[1], table_rest)
+    table_total = table_grad.astype(F32) + jnp.concatenate([table_top, table_rest]).astype(F32)
+    one_state = one_state[0], one_got, one_state[2]
+    contract_sum, mixer_sum = unstacked(rest_of(one_state, order[3:]), [(units // groups, width), (own, width)])
+    joint_sum = unstacked(rest_of((joint_keep, joint_got, axes), order[3:]), [(own, 3 * width)])[0]
+    rows_all = side_by_side(gathered, arriving, 1)
     small = jnp.sum(rows_all[:, counts[0] :].astype(F32), axis=0)
     small = small[: counts[1]] + small[counts[1] :]
     rows_all = rows_all[:, : counts[0]].reshape(groups * count, -1)
+    word_total = word_sums[0] + word_other[0]
     cuts = [units, width, width, width, units, width]
     starts = [sum(cuts[:i]) for i in range(len(cuts))]
     active_a, first_a, ctx_a, branch_a, hidden_a, mixed_a = (
@@ -1168,7 +1219,6 @@
     expand_sum = expand_sum + outer_sum(own_columns(first_a), hidden_a)
     mixer_sum = mixer_sum + outer_sum(own_columns(ctx_a), mixed_a)
 
-    logits_out = assembled(place32, *logits)
     loss = (small[-1, 0] / (picks * groups)).reshape(1)
     return (
         loss,

time: 565 us -> 445 us (0.79)
  waiting for transfers between devices: 126 us -> 56.6 us
  Pallas kernels: 267 us -> 234 us
  local copies, waits for them, and re-layouts: 35.8 us -> 51.4 us
  matrix products: 22.1 us -> 7.69 us
  other arithmetic: 32.6 us -> 20.7 us
    ppermute x38 -> x40, waiting for transfers between devices: 101 us -> 35.3 us  [swapped(): return lax.ppermute(block, 'dp', [(i, i ^ bit) for i in devices])]
    pallas_call x9, Pallas kernels: 28.1 us -> 7.02 us  [add_split(): pl.pallas_call(add_split_kernel, grid_spec=pltpu.PrefetchScalarGridSpec(n...]
    pallas_call x4 -> x5, Pallas kernels: 57 us -> 75.2 us  [the longest x1 29.5 us: attend_back(): pl.pallas_call(functools.partial(attend_back_kernel, head_dim=head_dim),...]
    unnamed x78 -> x226, local copies, waits for them, and re-layouts: 15.2 us -> 32.4 us
    dot_general x7 -> x5, matrix products: 17.1 us -> 4.06 us  [product(): lax.dot_general(left, right, (((left_dim,), (right_dim,)), ((), ())), pre...]
    convert_element_type x3 -> x0, other arithmetic: 10.7 us -> none  [the longest x1 4.81 us: on_device(): table_total = joined(own_half, across(own_half)).astype(F32)]
    pallas_call x1, Pallas kernels: 10.4 us -> 4.08 us  [cls_forward(): pl.pallas_call(functools.partial(cls_kernel, count=count, rows=rows, head...]
    all_to_all x3 -> x2, starting transfers between devices: 13.7 us -> 10.2 us  [on_device(): lax.all_to_all(part, 'dp', 0, 0, axis_index_groups=[list(range(i, i + qua...]
  transfers between devices with their start and end apart: 50 -> 51, of which waited for: 23 -> 18; matrix products, arithmetic and copies ran while one was open for 12% -> 9% of each run, Pallas kernels for 45% -> 49%
where the time goes in v2:
time: 445 us; the launch traced here: 440 us
  Pallas kernels  234 us (53%)
  starting transfers between devices  63.8 us (14%)
  waiting for transfers between devices  56.6 us (13%)
  local copies, waits for them, and re-layouts  51.4 us (12%)
  other arithmetic  20.7 us (5%)
  matrix products  7.69 us (2%)
  between operations  5.71 us (1%)
    ppermute x40, starting transfers between devices, swapped(): return lax.ppermute(block, 'dp', [(i, i ^ bit) for i in devices])  39.3 us
    ppermute x40, waiting for transfers between devices, swapped(): return lax.ppermute(block, 'dp', [(i, i ^ bit) for i in devices])  35.3 us
    unnamed x226, local copies, waits for them, and re-layouts  32.4 us
    pallas_call x1, Pallas kernels, attend_back(): pl.pallas_call(functools.partial(attend_back_kernel, head_dim=head_dim),...  29.5 us
    pallas_call x5, Pallas kernels, weight_grads(): pl.pallas_call(weight_grad_kernel, grid_spec=pltpu.PrefetchScalarGridSpec...  28 us
    pallas_call x1, Pallas kernels, tail_back(): pl.pallas_call(functools.partial(tail_back_kernel, chunk=min(chunk, hidde...  22.7 us
    pallas_call x1, Pallas kernels, layer_tail(): pl.pallas_call(functools.partial(tail_kernel, chunk=min(chunk, hidden)),...  22 us
    ppermute x7, waiting for transfers between devices, on_device(): across = lambda array: lax.ppermute(array, 'section', [(0, 1), (1, 0)])  18.6 us
  transfers between devices with their start and end apart: 51, of which 18 were waited for; matrix products, arithmetic and copies ran while one was open for 9% of the time, Pallas kernels for 49%

profile of v2, /device:TPU:0, one launch (start us, length us, event | category | flops | bytes accessed | tf_op | source)
XLA Modules:
  0.0 439.8 jit_solution(15561998896032710717)
XLA Ops:
  4.7 4.0 collective-permute-start.1
  13.1 4.4 %project.1.refs_2_.qkv_ref = bf16[1024,2304]{1,0:T(8,128)(2,1)S(1)} custom-call(bf16[1024,768]{1,0:T(8,128)(2,1)S(1)} %bitcast.186, bf16[768,2304]{1,0:T(8,128)(2,1)S(1)} %bitcast.207, f32[1,2304]{1,0:T(1,128)S(1)} %broadcast_in_dim.53.shift_ref), custom_call_target="tpu_custom_call" | custom-call | tf_op jit(solution)/shard_map/project/pallas_call | solution.py:539
  17.6 4.1 cls_forward.1
  21.7 3.6 collective-permute-start
  29.5 17.6 %attend.1 = (bf16[1024,768]{1,0:T(8,128)(2,1)S(1)}, f32[12,2,512]{2,1,0:T(2,128)S(1)}) custom-call(s32[2]{0:T(128)S(1)} %copy-done.62, bf16[1024,2304]{1,0:T(8,128)(2,1)} %copy-done.2, bf16[1024,2304]{1,0:T(8,128)(2,1)} %copy-done.2, bf16[1024,2304]{1,0:T(8,128)(2,1)} %copy-done.2), custom_call_target="tpu_custom_call" | custom-call | tf_op jit(solution)/shard_map/attend/pallas_call | solution.py:127
  53.7 22.0 %layer_tail.1 = (bf16[1024,768]{1,0:T(8,128)(2,1)S(1)}, bf16[1024,768]{1,0:T(8,128)(2,1)S(1)}, f32[1024,128]{1,0:T(8,128)S(1)}, bf16[1024,768]{1,0:T(8,128)(2,1)...) custom-call(bf16[1024,768]{1,0:T(8,128)(2,1)} %copy-done.30, ...), custom_call_target="tpu_custom_call" | custom-call | tf_op jit(solution)/shard_map/layer_tail/pallas_call | solution.py:240
  84.0 7.7 %collective-permute-done.11 = bf16[1920]{0:T(1024)(128)(2,1)S(1)} collective-permute-done((bf16[1920]{0:T(1024)(128)(2,1)S(1)}, bf16[1920]{0:T(1024)(128)(2,1)S(1)}, u32[]{:S(2)}, u32[]{:S(2)}) %collective-permute-start.11) | collective-permute-done | bytes 3872 | tf_op jit(solution)/shard_map/ppermute | solution.py:47
  98.7 11.4 %word_scores.1 = (f32[8,1,128]{2,1,0:T(1,128)S(1)}, f32[8,1,128]{2,1,0:T(1,128)S(1)}) custom-call(s32[1]{0:T(128)} %bitcast.decoder.section, bf16[8,128,896]{2,1,0:T(8,128)(2,1)S(1)} %bitcast.200, bf16[1920,768]{1,0:T(8,128)(2,1)} %refs_0_.1, bf16[960,768]{1,0:T(8,128)(2,1)S(1)} %constant_dynamic-update-slice_fusion.mine_ref.refs_1_, ...), custom_call_target="tpu_custom_call" | custom-call | tf_op jit(solution)/shard_map/word_scores/pallas_call | solution.py:766
  117.9 2.7 collective-permute-start.20
  126.8 18.4 %word_back.1 = (bf16[8,128,1920]{2,1,0:T(8,128)(2,1)}, bf16[8,128,768]{2,1,0:T(8,128)(2,1)S(1)}, f32[8,1,128]{2,1,0:T(1,128)S(1)}) custom-call(s32[3]{0:T(128)S(1)} %pad_add_fusion.first, bf16[8,128,896]{2,1,0:T(8,128)(2,1)} %bitcast.201, f32[8,1,128]{2,1,0:T(1,128)S(1)} %bitcast.271, bf16[1920,768]{1,0:T(8,128)(2,1)} %refs_0_.1, ...), custom_call_target="tpu_custom_call" | custom-call | tf_op jit(solution)/shard_map/word_back/pallas_call | solution.py:863
  154.3 17.9 %table_gradient.1 = (bf16[1920,768]{1,0:T(8,128)(2,1)}, f32[1,1920]{1,0:T(1,128)S(1)}) custom-call(s32[3]{0:T(128)S(1)} %pad_add_fusion.first, bf16[8,128,1920]{2,1,0:T(8,128)(2,1)} %get-tuple-element.194.grad_ref, bf16[8,128,896]{2,1,0:T(8,128)(2,1)S(1)} %bitcast.203, bf16[8,128,896]{2,1,0:T(8,128)(2,1)S(1)} %bitcast.217, ...), custom_call_target="tpu_custom_call" | custom-call | tf_op jit(solution)/shard_map/table_gradient/pallas_call | solution.py:914
  173.1 8.0 %word_logits.2 = bf16[4,128,3840]{2,1,0:T(8,128)(2,1)} custom-call(s32[2]{0:T(128)S(1)} %pad_add_fusion.1.place, bf16[8,128,896]{2,1,0:T(8,128)(2,1)S(1)} %bitcast.204, bf16[1920,768]{1,0:T(8,128)(2,1)} %refs_0_.1, bf16[960,768]{1,0:T(8,128)(2,1)S(1)} %copy-done.25, bf16[960,768]{1,0:T(8,128)(2,1)S(1)} %copy-done.22, ...), custom_call_target="tpu_custom_call" | custom-call | tf_op jit(solution)/shard_map/word_logits/pallas_call | solution.py:811
  181.1 5.1 %all-to-all-start = ((bf16[4,128,3840]{2,1,0:T(8,128)(2,1)}), bf16[4,128,3840]{2,1,0:T(8,128)(2,1)}, u32[]{:S(2)}, u32[]{:S(2)}) async-start(bf16[4,128,3840]{2,1,0:T(8,128)(2,1)} %word_logits.2), calls=%async_computation | async-start | bytes 7864320 | tf_op jit(solution)/shard_map/all_to_all | solution.py:1093
  192.8 3.2 fusion.14
  196.1 22.7 %tail_back.1 = (bf16[1024,768]{1,0:T(8,128)(2,1)S(1)}, bf16[1024,3072]{1,0:T(8,128)(2,1)}, f32[1024,768]{1,0:T(8,128)}, bf16[1024,768]{1,0:T(8,128)(2,1)S(1)}, b...) custom-call(f32[1024,768]{1,0:T(8,128)} %bitcast.280, ...), custom_call_target="tpu_custom_call" | custom-call | tf_op jit(solution)/shard_map/tail_back/pallas_call | solution.py:298
  221.1 8.5 %weight_grad.5 = (bf16[8,240,768]{2,1,0:T(8,128)(2,1)S(1)}, bf16[8,240,768]{2,1,0:T(8,128)(2,1)}) custom-call(s32[1]{0:T(128)} %bitcast.11.place, bf16[1024,3072]{1,0:T(8,128)(2,1)} %get-tuple-element.171.left_ref, bf16[1,1024,768]{2,1,0:T(8,128)(2,1)S(1)} %bitcast.254), custom_call_target="tpu_custom_call" | custom-call | tf_op jit(solution)/shard_map/weight_grad/pallas_call | solution.py:625
  231.9 9.7 %weight_grad.7 = (bf16[8,240,768]{2,1,0:T(8,128)(2,1)S(1)}, bf16[8,240,768]{2,1,0:T(8,128)(2,1)}) custom-call(s32[1]{0:T(128)} %bitcast.11.place, bf16[1024,768]{1,0:T(8,128)(2,1)S(1)} %copy-done.43, bf16[1,1024,3072]{2,1,0:T(8,128)(2,1)} %bitcast.282), custom_call_target="tpu_custom_call" | custom-call | tf_op jit(solution)/shard_map/weight_grad/pallas_call | solution.py:625
  248.7 2.7 add_split.10
  255.9 29.5 %attend_back.1.refs_0_.refs_1_.refs_15_ = bf16[3,1024,768]{2,1,0:T(8,128)(2,1)} custom-call(s32[2]{0:T(128)S(1)} %copy-done.63, bf16[1024,2304]{1,0:T(8,128)(2,1)} %copy-done.2, bf16[1024,2304]{1,0:T(8,128)(2,1)} %copy-done.2, bf16[1024,2304]{1,0:T(8,128)(2,1)} %copy-done.2, bf16[1024,768]{1,0:T(8,128)(2,1)S(1)} %copy-done.44, f32[12,2,512]{2,1,0:T(2,128)S(1)} %copy-done.53), custom_call_target="tpu_custom_call" | custom-call | tf_op jit(solution)/shard_map/attend_back/pallas_call | solution.py:182
  289.0 8.4 %word_logits.3 = bf16[4,128,3840]{2,1,0:T(8,128)(2,1)} custom-call(s32[2]{0:T(128)S(1)} %copy-done.70, bf16[8,128,896]{2,1,0:T(8,128)(2,1)} %bitcast.202, bf16[960,768]{1,0:T(8,128)(2,1)} %collective-permute-done.6.refs_0_, bf16[960,768]{1,0:T(8,128)(2,1)S(1)} %copy-done.46, bf16[960,768]{1,0:T(8,128)(2,1)} %collective-permute-done.27.refs_2_, ...), custom_call_target="tpu_custom_call" | custom-call | tf_op jit(solution)/shard_map/word_logits/pallas_call | solution.py:811
  297.5 5.1 %all-to-all-start.1 = ((bf16[4,128,3840]{2,1,0:T(8,128)(2,1)}), bf16[4,128,3840]{2,1,0:T(8,128)(2,1)}, u32[]{:S(2)}, u32[]{:S(2)}) async-start(bf16[4,128,3840]{2,1,0:T(8,128)(2,1)} %word_logits.3), calls=%async_computation.1 | async-start | bytes 7864320 | tf_op jit(solution)/shard_map/all_to_all | solution.py:1093
  304.1 3.1 cls_back.1
  324.3 10.1 %first_back.1 = (bf16[16,768]{1,0:T(8,128)(2,1)S(1)}, bf16[16,3072]{1,0:T(8,128)(2,1)S(1)}, bf16[16,768]{1,0:T(8,128)(2,1)S(1)}, f32[16,768]{1,0:T(8,128)S(1)}, ...) custom-call(s32[2]{0:T(128)S(1)} %copy-done.63, ...), custom_call_target="tpu_custom_call" | custom-call | tf_op jit(solution)/shard_map/first_back/pallas_call | solution.py:518
  338.7 6.2 %weight_grad.9 = (bf16[8,144,768]{2,1,0:T(8,128)(2,1)S(1)}, bf16[8,144,768]{2,1,0:T(8,128)(2,1)S(1)}) custom-call(s32[1]{0:T(128)} %bitcast.11.place, bf16[1024,768]{1,0:T(8,128)(2,1)S(1)} %copy-done.4, bf16[3,1024,768]{2,1,0:T(8,128)(2,1)} %copy-done.19), custom_call_target="tpu_custom_call" | custom-call | tf_op jit(solution)/shard_map/weight_grad/pallas_call | solution.py:625
  350.4 3.6 fusion.45
  359.3 8.3 %input_gradient.1 = f32[1024,768]{1,0:T(8,128)} custom-call(s32[1]{0:T(128)} %bitcast.decoder.section, bf16[3,1024,768]{2,1,0:T(8,128)(2,1)} %copy-done.19, f32[1024,768]{1,0:T(8,128)S(1)} %copy-done.12, f32[16,768]{1,0:T(8,128)S(1)} %get-tuple-element.280.first_ref, bf16[768,2304]{1,0:T(8,128)(2,1)} %bitcast.206), custom_call_target="tpu_custom_call" | custom-call | tf_op jit(solution)/shard_map/input_gradient/pallas_call | solution.py:573
  367.6 12.2 %assemble.1 = bf16[128,30720]{1,0:T(8,128)(2,1)} custom-call(s32[1]{0:T(128)} %bitcast.11.place, bf16[4,128,3840]{2,1,0:T(8,128)(2,1)} %all-to-all-done.near_ref, bf16[4,128,3840]{2,1,0:T(8,128)(2,1)} %all-to-all-done.1.side_ref), custom_call_target="tpu_custom_call" | custom-call | tf_op jit(solution)/shard_map/assemble/pallas_call | solution.py:960
  382.4 6.9 %collective-permute-done.42 = bf16[960,768]{1,0:T(8,128)(2,1)S(1)} collective-permute-done((bf16[960,768]{1,0:T(8,128)(2,1)}, bf16[960,768]{1,0:T(8,128)(2,1)S(1)}, u32[]{:S(2)}, u32[]{:S(2)}) %collective-permute-start.42) | collective-permute-done | bytes 1474592 | tf_op jit(solution)/shard_map/ppermute | solution.py:1016
  389.5 9.5 %collective-permute-done.43 = bf16[240,768]{1,0:T(8,128)(2,1)S(1)} collective-permute-done((bf16[240,768]{1,0:T(8,128)(2,1)S(1)}, bf16[240,768]{1,0:T(8,128)(2,1)S(1)}, u32[]{:S(2)}, u32[]{:S(2)}) %collective-permute-start.43) | collective-permute-done | bytes 368672 | tf_op jit(solution)/shard_map/ppermute | solution.py:47
  403.3 8.0 %collective-permute-done.44 = bf16[2,144,768]{2,1,0:T(8,128)(2,1)S(1)} collective-permute-done((bf16[2,144,768]{2,1,0:T(8,128)(2,1)S(1)}, bf16[2,144,768]{2,1,0:T(8,128)(2,1)S(1)}, u32[]{:S(2)}, u32[]{:S(2)}) %collective-permute-start.44) | collective-permute-done | bytes 442400 | tf_op jit(solution)/shard_map/ppermute | solution.py:47
  411.3 9.0 %collective-permute-done.47 = bf16[960,768]{1,0:T(8,128)(2,1)} collective-permute-done((bf16[960,768]{1,0:T(8,128)(2,1)}, bf16[960,768]{1,0:T(8,128)(2,1)}, u32[]{:S(2)}, u32[]{:S(2)}) %collective-permute-start.47) | collective-permute-done | bytes 1474592 | tf_op jit(solution)/shard_map/ppermute | solution.py:1016
  429.4 4.7 %convert_add_fusion = f32[1920,768]{1,0:T(8,128)} fusion(bf16[1920,768]{1,0:T(8,128)(2,1)S(1)} %copy-done.77, bf16[960,768]{1,0:T(8,128)(2,1)} %collective-permute-done.47, bf16[960,768]{1,0:T(8,128)(2,1)S(1)} %copy-done.81), kind=kLoop, calls=%fused_computation | loop fusion | flops 8847360 | bytes 11796480 | tf_op jit(solution)/shard_map/add | solution.py:1199
  (443 shorter events, 135.7 us)
Async XLA Ops:
  4.7 43.1 %collective-permute-start.1 = (bf16[480,768]{1,0:T(8,128)(2,1)S(1)}, bf16[480,768]{1,0:T(8,128)(2,1)}, u32[]{:S(2)}, u32[]{:S(2)}) collective-permute-start(bf16[480,768]{1,0:T(8,128)(2,1)S(1)} %get-tuple-element.340), channel_id=1, source_target_pairs={{0,8},{1,9},{2,10},{3,11},{4,12},{5,13},{6,14},{7,15},{8,0},{9,1},... | collective-permute-start | bytes 2211848 | tf_op jit(solution)/shard_map/ppermute | solution.py:47
  11.4 64.6 %collective-permute-start.6 = (bf16[960,768]{1,0:T(8,128)(2,1)}, bf16[960,768]{1,0:T(8,128)(2,1)}, u32[]{:S(2)}, u32[]{:S(2)}) collective-permute-start(bf16[960,768]{1,0:T(8,128)(2,1)} %constant_dynamic-slice_fusion.2), channel_id=1, source_target_pairs={{0,4},{1,5},{2,6},{3,7},{4,0},{5,1},{6,2},{7,3},{8,12},{9,13},{10,... | collective-permute-start | bytes 4423688 | tf_op jit(solution)/shard_map/ppermute | solution.py:47
  25.3 50.7 %collective-permute-start.3 = (bf16[480,768]{1,0:T(8,128)(2,1)}, bf16[480,768]{1,0:T(8,128)(2,1)}, u32[]{:S(2)}, u32[]{:S(2)}) collective-permute-start(bf16[480,768]{1,0:T(8,128)(2,1)} %get-tuple-element.339), channel_id=1, source_target_pairs={{0,8},{1,9},{2,10},{3,11},{4,12},{5,13},{6,14},{7,15},{8,0},{9,1},... | collective-permute-start | bytes 2211848 | tf_op jit(solution)/shard_map/ppermute | solution.py:47
  48.9 27.1 %collective-permute-start.2 = (bf16[480,768]{1,0:T(8,128)(2,1)}, bf16[480,768]{1,0:T(8,128)(2,1)S(1)}, u32[]{:S(2)}, u32[]{:S(2)}) collective-permute-start(bf16[480,768]{1,0:T(8,128)(2,1)} %collective-permute-done.1), channel_id=1, source_target_pairs={{0,16},{16,0},{1,17},{17,1},{2,18},{18,2},{3,19},{19,3},{4,20},{20... | collective-permute-start | bytes 2211848 | tf_op jit(solution)/shard_map/ppermute | solution.py:1016
  51.3 24.4 %collective-permute-start.4 = (bf16[1920]{0:T(1024)(128)(2,1)S(1)}, bf16[1920]{0:T(1024)(128)(2,1)S(1)}, u32[]{:S(2)}, u32[]{:S(2)}) collective-permute-start(bf16[1920]{0:T(1024)(128)(2,1)S(1)} %copy-done.99), channel_id=1, source_target_pairs={{0,8},{1,9},{2,10},{3,11},{4,12},{5,13},{6,14},{7,15},{8,0},{9,1},... | collective-permute-start | bytes 11528 | tf_op jit(solution)/shard_map/ppermute | solution.py:47
  51.6 24.4 %collective-permute-start.5 = (bf16[1920]{0:T(1024)(128)(2,1)S(1)}, bf16[1920]{0:T(1024)(128)(2,1)S(1)}, u32[]{:S(2)}, u32[]{:S(2)}) collective-permute-start(bf16[1920]{0:T(1024)(128)(2,1)S(1)} %copy-done.99), channel_id=1, source_target_pairs={{0,4},{1,5},{2,6},{3,7},{4,0},{5,1},{6,2},{7,3},{8,12},{9,13},{10,... | collective-permute-start | bytes 11528 | tf_op jit(solution)/shard_map/ppermute | solution.py:47
  76.0 17.4 %collective-permute-start.10 = (bf16[480,768]{1,0:T(8,128)(2,1)}, bf16[480,768]{1,0:T(8,128)(2,1)S(1)}, u32[]{:S(2)}, u32[]{:S(2)}) collective-permute-start(bf16[480,768]{1,0:T(8,128)(2,1)} %collective-permute-done.3), channel_id=1, source_target_pairs={{0,16},{16,0},{1,17},{17,1},{2,18},{18,2},{3,19},{19,3},{4,20},{20... | collective-permute-start | bytes 2211848 | tf_op jit(solution)/shard_map/ppermute | solution.py:1016
  96.2 14.0 %collective-permute-start.13 = (bf16[128,896]{1,0:T(8,128)(2,1)S(1)}, bf16[128,896]{1,0:T(8,128)(2,1)S(1)}, u32[]{:S(2)}, u32[]{:S(2)}) collective-permute-start(bf16[128,896]{1,0:T(8,128)(2,1)S(1)} %maximum_maximum_fusion), channel_id=1, source_target_pairs={{0,8},{1,9},{2,10},{3,11},{4,12},{5,13},{6,14},{7,15},{8,0},{9,1},... | collective-permute-start | bytes 688136 | tf_op jit(solution)/shard_map/ppermute | solution.py:47
  112.0 34.3 %collective-permute-start.17 = (bf16[960,768]{1,0:T(8,128)(2,1)}, bf16[960,768]{1,0:T(8,128)(2,1)S(1)}, u32[]{:S(2)}, u32[]{:S(2)}) collective-permute-start(bf16[960,768]{1,0:T(8,128)(2,1)} %collective-permute-done.6.refs_0_), channel_id=1, source_target_pairs={{0,16},{16,0},{1,17},{17,1},{2,18},{18,2},{3,19},{19,3},{4,20},{20... | collective-permute-start | bytes 4423688 | tf_op jit(solution)/shard_map/ppermute | solution.py:1016
  117.9 27.4 %collective-permute-start.20 = (bf16[128,896]{1,0:T(8,128)(2,1)}, bf16[128,896]{1,0:T(8,128)(2,1)}, u32[]{:S(2)}, u32[]{:S(2)}) collective-permute-start(bf16[128,896]{1,0:T(8,128)(2,1)} %copy-done.86), channel_id=1, source_target_pairs={{0,6},{1,7},{2,4},{3,5},{4,2},{5,3},{6,0},{7,1},{8,14},{9,15},{10,... | collective-permute-start | bytes 688136 | tf_op jit(solution)/shard_map/ppermute | solution.py:47
  120.6 24.7 %collective-permute-start.19 = (bf16[128,896]{1,0:T(8,128)(2,1)}, bf16[128,896]{1,0:T(8,128)(2,1)}, u32[]{:S(2)}, u32[]{:S(2)}) collective-permute-start(bf16[128,896]{1,0:T(8,128)(2,1)} %copy-done.86), channel_id=1, source_target_pairs={{0,4},{1,5},{2,6},{3,7},{4,0},{5,1},{6,2},{7,3},{8,12},{9,13},{10,... | collective-permute-start | bytes 688136 | tf_op jit(solution)/shard_map/ppermute | solution.py:47
  120.9 24.4 %collective-permute-start.18 = (bf16[128,896]{1,0:T(8,128)(2,1)}, bf16[128,896]{1,0:T(8,128)(2,1)}, u32[]{:S(2)}, u32[]{:S(2)}) collective-permute-start(bf16[128,896]{1,0:T(8,128)(2,1)} %copy-done.86), channel_id=1, source_target_pairs={{0,2},{1,3},{2,0},{3,1},{4,6},{5,7},{6,4},{7,5},{8,10},{9,11},{10,... | collective-permute-start | bytes 688136 | tf_op jit(solution)/shard_map/ppermute | solution.py:47
  122.2 23.0 %collective-permute-start.21 = (f32[8,1,128]{2,1,0:T(1,128)S(1)}, f32[8,1,128]{2,1,0:T(1,128)S(1)}, u32[]{:S(2)}, u32[]{:S(2)}) collective-permute-start(f32[8,1,128]{2,1,0:T(1,128)S(1)} %bitcast.270), channel_id=1, source_target_pairs={{0,8},{1,9},{2,10},{3,11},{4,12},{5,13},{6,14},{7,15},{8,0},{9,1},... | collective-permute-start | bytes 12296 | tf_op jit(solution)/shard_map/ppermute | solution.py:47
  149.0 23.2 %collective-permute-start.23 = (bf16[128,768]{1,0:T(8,128)(2,1)S(1)}, bf16[128,768]{1,0:T(8,128)(2,1)S(1)}, u32[]{:S(2)}, u32[]{:S(2)}) collective-permute-start(bf16[128,768]{1,0:T(8,128)(2,1)S(1)} %get-tuple-element.351), channel_id=1, source_target_pairs={{0,2},{1,3},{2,0},{3,1},{4,6},{5,7},{6,4},{7,5},{8,10},{9,11},{10,... | collective-permute-start | bytes 589832 | tf_op jit(solution)/shard_map/ppermute | solution.py:47
  150.6 21.7 %collective-permute-start.25 = (bf16[128,768]{1,0:T(8,128)(2,1)S(1)}, bf16[128,768]{1,0:T(8,128)(2,1)S(1)}, u32[]{:S(2)}, u32[]{:S(2)}) collective-permute-start(bf16[128,768]{1,0:T(8,128)(2,1)S(1)} %get-tuple-element.352), channel_id=1, source_target_pairs={{0,6},{1,7},{2,4},{3,5},{4,2},{5,3},{6,0},{7,1},{8,14},{9,15},{10,... | collective-permute-start | bytes 589832 | tf_op jit(solution)/shard_map/ppermute | solution.py:47
  150.9 21.4 %collective-permute-start.24 = (bf16[128,768]{1,0:T(8,128)(2,1)S(1)}, bf16[128,768]{1,0:T(8,128)(2,1)S(1)}, u32[]{:S(2)}, u32[]{:S(2)}) collective-permute-start(bf16[128,768]{1,0:T(8,128)(2,1)S(1)} %get-tuple-element.353), channel_id=1, source_target_pairs={{0,4},{1,5},{2,6},{3,7},{4,0},{5,1},{6,2},{7,3},{8,12},{9,13},{10,... | collective-permute-start | bytes 589832 | tf_op jit(solution)/shard_map/ppermute | solution.py:47
  181.1 61.9 %all-to-all-start = ((bf16[4,128,3840]{2,1,0:T(8,128)(2,1)}), bf16[4,128,3840]{2,1,0:T(8,128)(2,1)}, u32[]{:S(2)}, u32[]{:S(2)}) async-start(bf16[4,128,3840]{2,1,0:T(8,128)(2,1)} %word_logits.2), calls=%async_computation | async-start | bytes 7864320 | tf_op jit(solution)/shard_map/all_to_all | solution.py:1093
  186.3 34.8 %collective-permute-start.27 = (bf16[960,768]{1,0:T(8,128)(2,1)S(1)}, bf16[960,768]{1,0:T(8,128)(2,1)}, u32[]{:S(2)}, u32[]{:S(2)}) collective-permute-start(bf16[960,768]{1,0:T(8,128)(2,1)S(1)} %copy-done.26), channel_id=1, source_target_pairs={{0,4},{1,5},{2,6},{3,7},{4,0},{5,1},{6,2},{7,3},{8,12},{9,13},{10,... | collective-permute-start | bytes 4423688 | tf_op jit(solution)/shard_map/ppermute | solution.py:47
  186.7 32.1 %collective-permute-start.28 = (f32[1,1920]{1,0:T(1,128)S(1)}, f32[1,1920]{1,0:T(1,128)S(1)}, u32[]{:S(2)}, u32[]{:S(2)}) collective-permute-start(f32[1,1920]{1,0:T(1,128)S(1)} %copy-done.65), channel_id=1, source_target_pairs={{0,16},{16,0},{1,17},{17,1},{2,18},{18,2},{3,19},{19,3},{4,20},{20... | collective-permute-start | bytes 23048 | tf_op jit(solution)/shard_map/ppermute | solution.py:1016
  251.4 34.4 %collective-permute-start.31 = (bf16[2,2,240,768]{3,2,1,0:T(8,128)(2,1)S(1)}, bf16[2,2,240,768]{3,2,1,0:T(8,128)(2,1)S(1)}, u32[]{:S(2)}, u32[]{:S(2)}) collective-permute-start(bf16[2,2,240,768]{3,2,1,0:T(8,128)(2,1)S(1)} %get-tuple-element.239), channel_id=1, source_target_pairs={{0,4},{1,5},{2,6},{3,7},{4,0},{5,1},{6,2},{7,3},{8,12},{9,13},{10,... | collective-permute-start | bytes 4423688 | tf_op jit(solution)/shard_map/ppermute | solution.py:47
  251.8 34.3 %collective-permute-start.32 = (bf16[2,2,240,768]{3,2,1,0:T(8,128)(2,1)S(1)}, bf16[2,2,240,768]{3,2,1,0:T(8,128)(2,1)S(1)}, u32[]{:S(2)}, u32[]{:S(2)}) collective-permute-start(bf16[2,2,240,768]{3,2,1,0:T(8,128)(2,1)S(1)} %bitcast.273), channel_id=1, source_target_pairs={{0,2},{1,3},{2,0},{3,1},{4,6},{5,7},{6,4},{7,5},{8,10},{9,11},{10,... | collective-permute-start | bytes 4423688 | tf_op jit(solution)/shard_map/ppermute | solution.py:47
  253.5 35.5 %collective-permute-start.33 = (bf16[960,768]{1,0:T(8,128)(2,1)}, bf16[960,768]{1,0:T(8,128)(2,1)S(1)}, u32[]{:S(2)}, u32[]{:S(2)}) collective-permute-start(bf16[960,768]{1,0:T(8,128)(2,1)} %collective-permute-done.27.refs_2_), channel_id=1, source_target_pairs={{0,16},{16,0},{1,17},{17,1},{2,18},{18,2},{3,19},{19,3},{4,20},{20... | collective-permute-start | bytes 4423688 | tf_op jit(solution)/shard_map/ppermute | solution.py:1016
  297.5 50.5 %all-to-all-start.1 = ((bf16[4,128,3840]{2,1,0:T(8,128)(2,1)}), bf16[4,128,3840]{2,1,0:T(8,128)(2,1)}, u32[]{:S(2)}, u32[]{:S(2)}) async-start(bf16[4,128,3840]{2,1,0:T(8,128)(2,1)} %word_logits.3), calls=%async_computation.1 | async-start | bytes 7864320 | tf_op jit(solution)/shard_map/all_to_all | solution.py:1093
  312.0 26.5 %collective-permute-start.35 = (bf16[2,240,768]{2,1,0:T(8,128)(2,1)}, bf16[2,240,768]{2,1,0:T(8,128)(2,1)S(1)}, u32[]{:S(2)}, u32[]{:S(2)}) collective-permute-start(bf16[2,240,768]{2,1,0:T(8,128)(2,1)} %bitcast.275), channel_id=1, source_target_pairs={{0,4},{1,5},{2,6},{3,7},{4,0},{5,1},{6,2},{7,3},{8,12},{9,13},{10,... | collective-permute-start | bytes 2211848 | tf_op jit(solution)/shard_map/ppermute | solution.py:47
  354.0 35.3 %collective-permute-start.42 = (bf16[960,768]{1,0:T(8,128)(2,1)}, bf16[960,768]{1,0:T(8,128)(2,1)S(1)}, u32[]{:S(2)}, u32[]{:S(2)}) collective-permute-start(bf16[960,768]{1,0:T(8,128)(2,1)} %get-tuple-element.338), channel_id=1, source_target_pairs={{0,16},{16,0},{1,17},{17,1},{2,18},{18,2},{3,19},{19,3},{4,20},{20... | collective-permute-start | bytes 4423688 | tf_op jit(solution)/shard_map/ppermute | solution.py:1016
  354.7 27.6 %collective-permute-start.41 = (bf16[2,240,768]{2,1,0:T(8,128)(2,1)S(1)}, bf16[2,240,768]{2,1,0:T(8,128)(2,1)S(1)}, u32[]{:S(2)}, u32[]{:S(2)}) collective-permute-start(bf16[2,240,768]{2,1,0:T(8,128)(2,1)S(1)} %bitcast.274), channel_id=1, source_target_pairs={{0,2},{1,3},{2,0},{3,1},{4,6},{5,7},{6,4},{7,5},{8,10},{9,11},{10,... | collective-permute-start | bytes 2211848 | tf_op jit(solution)/shard_map/ppermute | solution.py:47
  356.6 63.7 %collective-permute-start.47 = (bf16[960,768]{1,0:T(8,128)(2,1)}, bf16[960,768]{1,0:T(8,128)(2,1)}, u32[]{:S(2)}, u32[]{:S(2)}) collective-permute-start(bf16[960,768]{1,0:T(8,128)(2,1)} %get-tuple-element.337), channel_id=1, source_target_pairs={{0,16},{16,0},{1,17},{17,1},{2,18},{18,2},{3,19},{19,3},{4,20},{20... | collective-permute-start | bytes 4423688 | tf_op jit(solution)/shard_map/ppermute | solution.py:1016
  357.1 23.4 %collective-permute-start.39 = (bf16[4,56,768]{2,1,0:T(8,128)(2,1)S(1)}, bf16[4,56,768]{2,1,0:T(8,128)(2,1)S(1)}, u32[]{:S(2)}, u32[]{:S(2)}) collective-permute-start(bf16[4,56,768]{2,1,0:T(8,128)(2,1)S(1)} %bitcast.291), channel_id=1, source_target_pairs={{0,2},{1,3},{2,0},{3,1},{4,6},{5,7},{6,4},{7,5},{8,10},{9,11},{10,... | collective-permute-start | bytes 1032200 | tf_op jit(solution)/shard_map/ppermute | solution.py:47
  358.6 40.4 %collective-permute-start.40 = (bf16[2,2,144,768]{3,2,1,0:T(8,128)(2,1)S(1)}, bf16[2,2,144,768]{3,2,1,0:T(8,128)(2,1)S(1)}, u32[]{:S(2)}, u32[]{:S(2)}) collective-permute-start(bf16[2,2,144,768]{3,2,1,0:T(8,128)(2,1)S(1)} %get-tuple-element.287), channel_id=1, source_target_pairs={{0,4},{1,5},{2,6},{3,7},{4,0},{5,1},{6,2},{7,3},{8,12},{9,13},{10,... | collective-permute-start | bytes 2654216 | tf_op jit(solution)/shard_map/ppermute | solution.py:47
  380.5 18.5 %collective-permute-start.43 = (bf16[240,768]{1,0:T(8,128)(2,1)S(1)}, bf16[240,768]{1,0:T(8,128)(2,1)S(1)}, u32[]{:S(2)}, u32[]{:S(2)}) collective-permute-start(bf16[240,768]{1,0:T(8,128)(2,1)S(1)} %bitcast.277), channel_id=1, source_target_pairs={{0,8},{1,9},{2,10},{3,11},{4,12},{5,13},{6,14},{7,15},{8,0},{9,1},... | collective-permute-start | bytes 1105928 | tf_op jit(solution)/shard_map/ppermute | solution.py:47
  382.3 38.0 %collective-permute-start.45 = (bf16[8,56,768]{2,1,0:T(8,128)(2,1)S(1)}, bf16[8,56,768]{2,1,0:T(8,128)(2,1)}, u32[]{:S(2)}, u32[]{:S(2)}) collective-permute-start(bf16[8,56,768]{2,1,0:T(8,128)(2,1)S(1)} %bitcast.286), channel_id=1, source_target_pairs={{0,1},{1,0},{2,3},{3,2},{4,5},{5,4},{6,7},{7,6},{8,9},{9,8},{10,11... | collective-permute-start | bytes 2064392 | tf_op jit(solution)/shard_map/ppermute | solution.py:47
  401.0 19.4 %collective-permute-start.46 = (bf16[240,768]{1,0:T(8,128)(2,1)S(1)}, bf16[240,768]{1,0:T(8,128)(2,1)S(1)}, u32[]{:S(2)}, u32[]{:S(2)}) collective-permute-start(bf16[240,768]{1,0:T(8,128)(2,1)S(1)} %bitcast.278), channel_id=1, source_target_pairs={{0,8},{1,9},{2,10},{3,11},{4,12},{5,13},{6,14},{7,15},{8,0},{9,1},... | collective-permute-start | bytes 1105928 | tf_op jit(solution)/shard_map/ppermute | solution.py:47
  (128 other events, 1067.6 us)

commit v3 on v2

--- a/solution.py
+++ b/solution.py
@@ -928,11 +928,12 @@
 
 def assemble_kernel(place, near_ref, side_ref, out_ref, *, quarter):
     turn = jnp.bitwise_xor(place[0] // quarter, pl.program_id(0))
-    for i, ref in enumerate((near_ref, side_ref)):
-
-        @pl.when(turn % 2 == i)
+    for side, ref in enumerate((near_ref, side_ref)):
+
+        @pl.when(turn % 2 == side)
         def _():
-            out_ref[...] = ref[0]
+            for i in range(ref.shape[0]):
+                out_ref[:, i * ref.shape[2] : (i + 1) * ref.shape[2]] = ref[i]
 
 
 def assembled(place, nears, sides):
@@ -944,26 +945,29 @@
         parts = jnp.take(parts, jnp.bitwise_xor(jnp.arange(4), place // quarter), axis=2)
         return parts.transpose(1, 2, 0, 3).reshape(picks, 2 * quarter * vocab)
 
+    together = 2
+    steps = quarter // together
+
     def spec(side):
         def index(b, j, p):
             turn = jnp.bitwise_xor(p[0] // quarter, b)
             last = jnp.bitwise_xor(p[0] // quarter, jnp.bitwise_xor(b, 1)) // 2
             first_of_pair = lax.rem(b, 2) == 0
             return (
-                jnp.where(lax.rem(turn, 2) == side, j, jnp.where(first_of_pair, 0, quarter - 1)),
+                jnp.where(lax.rem(turn, 2) == side, j, jnp.where(first_of_pair, 0, steps - 1)),
                 0,
                 jnp.where(lax.rem(turn, 2) == side, turn // 2, last),
             )
 
-        return pl.BlockSpec((1, picks, slice_rows), index)
+        return pl.BlockSpec((together, picks, slice_rows), index)
 
     return pl.pallas_call(
         functools.partial(assemble_kernel, quarter=quarter),
         grid_spec=pltpu.PrefetchScalarGridSpec(
             num_scalar_prefetch=1,
-            grid=(4, quarter),
+            grid=(4, steps),
             in_specs=[spec(0), spec(1)],
-            out_specs=pl.BlockSpec((picks, slice_rows), lambda b, j, _: (0, b * quarter + j)),
+            out_specs=pl.BlockSpec((picks, together * slice_rows), lambda b, j, _: (0, b * steps + j)),
         ),
         out_shape=jax.ShapeDtypeStruct((picks, 2 * quarter * vocab), BF16),
         compiler_params=pltpu.CompilerParams(vmem_limit_bytes=48 * MIB),
@@ -1195,11 +1199,12 @@
     joint_keep, joint_got, expand_sum, head_sum = tied(*joint_state[:2], expand_sum, head_sum)
     joint_keep, joint_send, axes = added((joint_keep, joint_got, joint_state[2]), order[2])
     joint_got = swapped(joint_send, order[2])
-    joint_keep, arriving, one_got, table_rest = tied(joint_keep, arriving, one_state[1], table_rest)
-    table_total = table_grad.astype(F32) + jnp.concatenate([table_top, table_rest]).astype(F32)
+    joint_keep, arriving, one_got = tied(joint_keep, arriving, one_state[1])
     one_state = one_state[0], one_got, one_state[2]
     contract_sum, mixer_sum = unstacked(rest_of(one_state, order[3:]), [(units // groups, width), (own, width)])
+    joint_got, table_rest = tied(joint_got, table_rest)
     joint_sum = unstacked(rest_of((joint_keep, joint_got, axes), order[3:]), [(own, 3 * width)])[0]
+    table_total = table_grad.astype(F32) + jnp.concatenate([table_top, table_rest]).astype(F32)
     rows_all = side_by_side(gathered, arriving, 1)
     small = jnp.sum(rows_all[:, counts[0] :].astype(F32), axis=0)
     small = small[: counts[1]] + small[counts[1] :]

time: 445 us -> 439 us (0.987)
  waiting for transfers between devices: 56.6 us -> 52.1 us
    unnamed x226 -> x220, local copies, waits for them, and re-layouts: 32.4 us -> 33.2 us
where the time goes in v3:
time: 439 us; the launch traced here: 435 us
  Pallas kernels  231 us (53%)
  starting transfers between devices  64.2 us (15%)
  waiting for transfers between devices  52.1 us (12%)
  local copies, waits for them, and re-layouts  51.7 us (12%)
  other arithmetic  22.5 us (5%)
  matrix products  7.68 us (2%)
  between operations  5.66 us (1%)
    ppermute x40, starting transfers between devices, swapped(): return lax.ppermute(block, 'dp', [(i, i ^ bit) for i in devices])  37.9 us
    unnamed x220, local copies, waits for them, and re-layouts  33.2 us
    ppermute x40, waiting for transfers between devices, swapped(): return lax.ppermute(block, 'dp', [(i, i ^ bit) for i in devices])  31.9 us
    pallas_call x1, Pallas kernels, attend_back(): pl.pallas_call(functools.partial(attend_back_kernel, head_dim=head_dim),...  29.5 us
    pallas_call x5, Pallas kernels, weight_grads(): pl.pallas_call(weight_grad_kernel, grid_spec=pltpu.PrefetchScalarGridSpec...  28 us
    pallas_call x1, Pallas kernels, tail_back(): pl.pallas_call(functools.partial(tail_back_kernel, chunk=min(chunk, hidde...  22.8 us
    pallas_call x1, Pallas kernels, layer_tail(): pl.pallas_call(functools.partial(tail_kernel, chunk=min(chunk, hidden)),...  22 us
    pallas_call x1, Pallas kernels, word_back(): pl.pallas_call(functools.partial(word_back_kernel, masked=masked), grid_s...  18.4 us
  transfers between devices with their start and end apart: 51, of which 18 were waited for; matrix products, arithmetic and copies ran while one was open for 9% of the time, Pallas kernels for 49%

profile of v3, /device:TPU:0, one launch (start us, length us, event | category | flops | bytes accessed | tf_op | source)
XLA Modules:
  0.0 434.6 jit_solution(14318297389801724381)
XLA Ops:
  4.7 4.0 collective-permute-start.1
  13.2 4.4 %project.1.refs_2_.qkv_ref = bf16[1024,2304]{1,0:T(8,128)(2,1)S(1)} custom-call(bf16[1024,768]{1,0:T(8,128)(2,1)S(1)} %bitcast.186, bf16[768,2304]{1,0:T(8,128)(2,1)S(1)} %bitcast.207, f32[1,2304]{1,0:T(1,128)S(1)} %broadcast_in_dim.53.shift_ref), custom_call_target="tpu_custom_call" | custom-call | tf_op jit(solution)/shard_map/project/pallas_call | solution.py:539
  17.6 4.1 cls_forward.1
  21.7 3.6 collective-permute-start
  29.6 17.6 %attend.1 = (bf16[1024,768]{1,0:T(8,128)(2,1)S(1)}, f32[12,2,512]{2,1,0:T(2,128)S(1)}) custom-call(s32[2]{0:T(128)S(1)} %copy-done.62, bf16[1024,2304]{1,0:T(8,128)(2,1)} %copy-done.2, bf16[1024,2304]{1,0:T(8,128)(2,1)} %copy-done.2, bf16[1024,2304]{1,0:T(8,128)(2,1)} %copy-done.2), custom_call_target="tpu_custom_call" | custom-call | tf_op jit(solution)/shard_map/attend/pallas_call | solution.py:127
  53.7 22.0 %layer_tail.1 = (bf16[1024,768]{1,0:T(8,128)(2,1)S(1)}, bf16[1024,768]{1,0:T(8,128)(2,1)S(1)}, f32[1024,128]{1,0:T(8,128)S(1)}, bf16[1024,768]{1,0:T(8,128)(2,1)...) custom-call(bf16[1024,768]{1,0:T(8,128)(2,1)} %copy-done.30, ...), custom_call_target="tpu_custom_call" | custom-call | tf_op jit(solution)/shard_map/layer_tail/pallas_call | solution.py:240
  84.1 7.7 %collective-permute-done.11 = bf16[1920]{0:T(1024)(128)(2,1)S(1)} collective-permute-done((bf16[1920]{0:T(1024)(128)(2,1)S(1)}, bf16[1920]{0:T(1024)(128)(2,1)S(1)}, u32[]{:S(2)}, u32[]{:S(2)}) %collective-permute-start.11) | collective-permute-done | bytes 3872 | tf_op jit(solution)/shard_map/ppermute | solution.py:47
  98.7 11.4 %word_scores.1 = (f32[8,1,128]{2,1,0:T(1,128)S(1)}, f32[8,1,128]{2,1,0:T(1,128)S(1)}) custom-call(s32[1]{0:T(128)} %bitcast.decoder.section, bf16[8,128,896]{2,1,0:T(8,128)(2,1)S(1)} %bitcast.200, bf16[1920,768]{1,0:T(8,128)(2,1)} %refs_0_.1, bf16[960,768]{1,0:T(8,128)(2,1)S(1)} %constant_dynamic-update-slice_fusion.mine_ref.refs_1_, ...), custom_call_target="tpu_custom_call" | custom-call | tf_op jit(solution)/shard_map/word_scores/pallas_call | solution.py:766
  117.9 2.7 collective-permute-start.20
  126.8 18.4 %word_back.1 = (bf16[8,128,1920]{2,1,0:T(8,128)(2,1)}, bf16[8,128,768]{2,1,0:T(8,128)(2,1)S(1)}, f32[8,1,128]{2,1,0:T(1,128)S(1)}) custom-call(s32[3]{0:T(128)S(1)} %pad_add_fusion.first, bf16[8,128,896]{2,1,0:T(8,128)(2,1)} %bitcast.201, f32[8,1,128]{2,1,0:T(1,128)S(1)} %bitcast.271, bf16[1920,768]{1,0:T(8,128)(2,1)} %refs_0_.1, ...), custom_call_target="tpu_custom_call" | custom-call | tf_op jit(solution)/shard_map/word_back/pallas_call | solution.py:863
  154.3 17.9 %table_gradient.1 = (bf16[1920,768]{1,0:T(8,128)(2,1)}, f32[1,1920]{1,0:T(1,128)S(1)}) custom-call(s32[3]{0:T(128)S(1)} %pad_add_fusion.first, bf16[8,128,1920]{2,1,0:T(8,128)(2,1)} %get-tuple-element.195.grad_ref, bf16[8,128,896]{2,1,0:T(8,128)(2,1)S(1)} %bitcast.203, bf16[8,128,896]{2,1,0:T(8,128)(2,1)S(1)} %bitcast.217, ...), custom_call_target="tpu_custom_call" | custom-call | tf_op jit(solution)/shard_map/table_gradient/pallas_call | solution.py:914
  173.1 8.0 %word_logits.2 = bf16[4,128,3840]{2,1,0:T(8,128)(2,1)} custom-call(s32[2]{0:T(128)S(1)} %pad_add_fusion.1.place, bf16[8,128,896]{2,1,0:T(8,128)(2,1)S(1)} %bitcast.204, bf16[1920,768]{1,0:T(8,128)(2,1)} %refs_0_.1, bf16[960,768]{1,0:T(8,128)(2,1)S(1)} %copy-done.25, bf16[960,768]{1,0:T(8,128)(2,1)S(1)} %copy-done.22, ...), custom_call_target="tpu_custom_call" | custom-call | tf_op jit(solution)/shard_map/word_logits/pallas_call | solution.py:811
  181.1 5.1 %all-to-all-start = ((bf16[4,128,3840]{2,1,0:T(8,128)(2,1)}), bf16[4,128,3840]{2,1,0:T(8,128)(2,1)}, u32[]{:S(2)}, u32[]{:S(2)}) async-start(bf16[4,128,3840]{2,1,0:T(8,128)(2,1)} %word_logits.2), calls=%async_computation | async-start | bytes 7864320 | tf_op jit(solution)/shard_map/all_to_all | solution.py:1097
  192.9 3.2 fusion.14
  196.1 22.8 %tail_back.1 = (bf16[1024,768]{1,0:T(8,128)(2,1)S(1)}, bf16[1024,3072]{1,0:T(8,128)(2,1)}, f32[1024,768]{1,0:T(8,128)}, bf16[1024,768]{1,0:T(8,128)(2,1)S(1)}, b...) custom-call(f32[1024,768]{1,0:T(8,128)} %bitcast.280, ...), custom_call_target="tpu_custom_call" | custom-call | tf_op jit(solution)/shard_map/tail_back/pallas_call | solution.py:298
  221.1 8.5 %weight_grad.5 = (bf16[8,240,768]{2,1,0:T(8,128)(2,1)S(1)}, bf16[8,240,768]{2,1,0:T(8,128)(2,1)}) custom-call(s32[1]{0:T(128)} %bitcast.11.place, bf16[1024,3072]{1,0:T(8,128)(2,1)} %get-tuple-element.172.left_ref, bf16[1,1024,768]{2,1,0:T(8,128)(2,1)S(1)} %bitcast.254), custom_call_target="tpu_custom_call" | custom-call | tf_op jit(solution)/shard_map/weight_grad/pallas_call | solution.py:625
  232.0 9.7 %weight_grad.7 = (bf16[8,240,768]{2,1,0:T(8,128)(2,1)S(1)}, bf16[8,240,768]{2,1,0:T(8,128)(2,1)}) custom-call(s32[1]{0:T(128)} %bitcast.11.place, bf16[1024,768]{1,0:T(8,128)(2,1)S(1)} %copy-done.43, bf16[1,1024,3072]{2,1,0:T(8,128)(2,1)} %bitcast.282), custom_call_target="tpu_custom_call" | custom-call | tf_op jit(solution)/shard_map/weight_grad/pallas_call | solution.py:625
  256.0 29.5 %attend_back.1.refs_0_.refs_1_.refs_15_ = bf16[3,1024,768]{2,1,0:T(8,128)(2,1)} custom-call(s32[2]{0:T(128)S(1)} %copy-done.63, bf16[1024,2304]{1,0:T(8,128)(2,1)} %copy-done.2, bf16[1024,2304]{1,0:T(8,128)(2,1)} %copy-done.2, bf16[1024,2304]{1,0:T(8,128)(2,1)} %copy-done.2, bf16[1024,768]{1,0:T(8,128)(2,1)S(1)} %copy-done.44, f32[12,2,512]{2,1,0:T(2,128)S(1)} %copy-done.53), custom_call_target="tpu_custom_call" | custom-call | tf_op jit(solution)/shard_map/attend_back/pallas_call | solution.py:182
  289.1 8.4 %word_logits.3 = bf16[4,128,3840]{2,1,0:T(8,128)(2,1)} custom-call(s32[2]{0:T(128)S(1)} %copy-done.70, bf16[8,128,896]{2,1,0:T(8,128)(2,1)} %bitcast.202, bf16[960,768]{1,0:T(8,128)(2,1)} %collective-permute-done.6.refs_0_, bf16[960,768]{1,0:T(8,128)(2,1)S(1)} %copy-done.46, bf16[960,768]{1,0:T(8,128)(2,1)} %collective-permute-done.27.refs_2_, ...), custom_call_target="tpu_custom_call" | custom-call | tf_op jit(solution)/shard_map/word_logits/pallas_call | solution.py:811
  297.5 5.1 %all-to-all-start.1 = ((bf16[4,128,3840]{2,1,0:T(8,128)(2,1)}), bf16[4,128,3840]{2,1,0:T(8,128)(2,1)}, u32[]{:S(2)}, u32[]{:S(2)}) async-start(bf16[4,128,3840]{2,1,0:T(8,128)(2,1)} %word_logits.3), calls=%async_computation.1 | async-start | bytes 7864320 | tf_op jit(solution)/shard_map/all_to_all | solution.py:1097
  304.2 3.1 cls_back.1
  324.4 10.1 %first_back.1 = (bf16[16,768]{1,0:T(8,128)(2,1)S(1)}, bf16[16,3072]{1,0:T(8,128)(2,1)S(1)}, bf16[16,768]{1,0:T(8,128)(2,1)S(1)}, f32[16,768]{1,0:T(8,128)S(1)}, ...) custom-call(s32[2]{0:T(128)S(1)} %copy-done.63, ...), custom_call_target="tpu_custom_call" | custom-call | tf_op jit(solution)/shard_map/first_back/pallas_call | solution.py:518
  338.8 6.2 %weight_grad.9 = (bf16[8,144,768]{2,1,0:T(8,128)(2,1)S(1)}, bf16[8,144,768]{2,1,0:T(8,128)(2,1)S(1)}) custom-call(s32[1]{0:T(128)} %bitcast.11.place, bf16[1024,768]{1,0:T(8,128)(2,1)S(1)} %copy-done.4, bf16[3,1024,768]{2,1,0:T(8,128)(2,1)} %copy-done.19), custom_call_target="tpu_custom_call" | custom-call | tf_op jit(solution)/shard_map/weight_grad/pallas_call | solution.py:625
  350.4 3.1 fusion.45
  360.0 8.3 %input_gradient.1 = f32[1024,768]{1,0:T(8,128)} custom-call(s32[1]{0:T(128)} %bitcast.decoder.section, bf16[3,1024,768]{2,1,0:T(8,128)(2,1)} %copy-done.19, f32[1024,768]{1,0:T(8,128)S(1)} %copy-done.12, f32[16,768]{1,0:T(8,128)S(1)} %get-tuple-element.281.first_ref, bf16[768,2304]{1,0:T(8,128)(2,1)} %bitcast.206), custom_call_target="tpu_custom_call" | custom-call | tf_op jit(solution)/shard_map/input_gradient/pallas_call | solution.py:573
  368.4 8.9 %assemble.1 = bf16[128,30720]{1,0:T(8,128)(2,1)} custom-call(s32[1]{0:T(128)} %bitcast.11.place, bf16[4,128,3840]{2,1,0:T(8,128)(2,1)} %all-to-all-done.near_ref, bf16[4,128,3840]{2,1,0:T(8,128)(2,1)} %all-to-all-done.1.side_ref), custom_call_target="tpu_custom_call" | custom-call | tf_op jit(solution)/shard_map/assemble/pallas_call | solution.py:964
  377.6 3.9 collective-permute-done.41
  381.5 6.5 %collective-permute-done.42 = bf16[960,768]{1,0:T(8,128)(2,1)S(1)} collective-permute-done((bf16[960,768]{1,0:T(8,128)(2,1)S(1)}, bf16[960,768]{1,0:T(8,128)(2,1)S(1)}, u32[]{:S(2)}, u32[]{:S(2)}) %collective-permute-start.42) | collective-permute-done | bytes 1474592 | tf_op jit(solution)/shard_map/ppermute | solution.py:1020
  396.8 4.0 collective-permute-done.44
  401.0 8.0 %collective-permute-done.46 = bf16[240,768]{1,0:T(8,128)(2,1)S(1)} collective-permute-done((bf16[240,768]{1,0:T(8,128)(2,1)S(1)}, bf16[240,768]{1,0:T(8,128)(2,1)S(1)}, u32[]{:S(2)}, u32[]{:S(2)}) %collective-permute-start.46) | collective-permute-done | bytes 368672 | tf_op jit(solution)/shard_map/ppermute | solution.py:47
  417.8 8.3 %collective-permute-done.48 = bf16[960,768]{1,0:T(8,128)(2,1)} collective-permute-done((bf16[960,768]{1,0:T(8,128)(2,1)}, bf16[960,768]{1,0:T(8,128)(2,1)}, u32[]{:S(2)}, u32[]{:S(2)}) %collective-permute-start.48) | collective-permute-done | bytes 1474592 | tf_op jit(solution)/shard_map/ppermute | solution.py:1020
  427.6 5.6 %convert_add_fusion = f32[1920,768]{1,0:T(8,128)} fusion(bf16[1920,768]{1,0:T(8,128)(2,1)} %get-tuple-element.291, bf16[960,768]{1,0:T(8,128)(2,1)} %collective-permute-done.48, bf16[960,768]{1,0:T(8,128)(2,1)S(1)} %copy-done.80), kind=kLoop, calls=%fused_computation | loop fusion | flops 8847360 | bytes 11796480 | tf_op jit(solution)/shard_map/add | solution.py:1207
  (437 shorter events, 138.6 us)
Async XLA Ops:
  4.7 43.1 %collective-permute-start.1 = (bf16[480,768]{1,0:T(8,128)(2,1)S(1)}, bf16[480,768]{1,0:T(8,128)(2,1)}, u32[]{:S(2)}, u32[]{:S(2)}) collective-permute-start(bf16[480,768]{1,0:T(8,128)(2,1)S(1)} %get-tuple-element.342), channel_id=1, source_target_pairs={{0,8},{1,9},{2,10},{3,11},{4,12},{5,13},{6,14},{7,15},{8,0},{9,1},... | collective-permute-start | bytes 2211848 | tf_op jit(solution)/shard_map/ppermute | solution.py:47
  11.4 64.6 %collective-permute-start.6 = (bf16[960,768]{1,0:T(8,128)(2,1)}, bf16[960,768]{1,0:T(8,128)(2,1)}, u32[]{:S(2)}, u32[]{:S(2)}) collective-permute-start(bf16[960,768]{1,0:T(8,128)(2,1)} %constant_dynamic-slice_fusion.2), channel_id=1, source_target_pairs={{0,4},{1,5},{2,6},{3,7},{4,0},{5,1},{6,2},{7,3},{8,12},{9,13},{10,... | collective-permute-start | bytes 4423688 | tf_op jit(solution)/shard_map/ppermute | solution.py:47
  25.3 50.7 %collective-permute-start.3 = (bf16[480,768]{1,0:T(8,128)(2,1)}, bf16[480,768]{1,0:T(8,128)(2,1)}, u32[]{:S(2)}, u32[]{:S(2)}) collective-permute-start(bf16[480,768]{1,0:T(8,128)(2,1)} %get-tuple-element.341), channel_id=1, source_target_pairs={{0,8},{1,9},{2,10},{3,11},{4,12},{5,13},{6,14},{7,15},{8,0},{9,1},... | collective-permute-start | bytes 2211848 | tf_op jit(solution)/shard_map/ppermute | solution.py:47
  49.0 27.1 %collective-permute-start.2 = (bf16[480,768]{1,0:T(8,128)(2,1)}, bf16[480,768]{1,0:T(8,128)(2,1)S(1)}, u32[]{:S(2)}, u32[]{:S(2)}) collective-permute-start(bf16[480,768]{1,0:T(8,128)(2,1)} %collective-permute-done.1), channel_id=1, source_target_pairs={{0,16},{16,0},{1,17},{17,1},{2,18},{18,2},{3,19},{19,3},{4,20},{20... | collective-permute-start | bytes 2211848 | tf_op jit(solution)/shard_map/ppermute | solution.py:1020
  51.3 24.4 %collective-permute-start.4 = (bf16[1920]{0:T(1024)(128)(2,1)S(1)}, bf16[1920]{0:T(1024)(128)(2,1)S(1)}, u32[]{:S(2)}, u32[]{:S(2)}) collective-permute-start(bf16[1920]{0:T(1024)(128)(2,1)S(1)} %copy-done.96), channel_id=1, source_target_pairs={{0,8},{1,9},{2,10},{3,11},{4,12},{5,13},{6,14},{7,15},{8,0},{9,1},... | collective-permute-start | bytes 11528 | tf_op jit(solution)/shard_map/ppermute | solution.py:47
  51.6 24.4 %collective-permute-start.5 = (bf16[1920]{0:T(1024)(128)(2,1)S(1)}, bf16[1920]{0:T(1024)(128)(2,1)S(1)}, u32[]{:S(2)}, u32[]{:S(2)}) collective-permute-start(bf16[1920]{0:T(1024)(128)(2,1)S(1)} %copy-done.96), channel_id=1, source_target_pairs={{0,4},{1,5},{2,6},{3,7},{4,0},{5,1},{6,2},{7,3},{8,12},{9,13},{10,... | collective-permute-start | bytes 11528 | tf_op jit(solution)/shard_map/ppermute | solution.py:47
  76.1 17.4 %collective-permute-start.10 = (bf16[480,768]{1,0:T(8,128)(2,1)}, bf16[480,768]{1,0:T(8,128)(2,1)S(1)}, u32[]{:S(2)}, u32[]{:S(2)}) collective-permute-start(bf16[480,768]{1,0:T(8,128)(2,1)} %collective-permute-done.3), channel_id=1, source_target_pairs={{0,16},{16,0},{1,17},{17,1},{2,18},{18,2},{3,19},{19,3},{4,20},{20... | collective-permute-start | bytes 2211848 | tf_op jit(solution)/shard_map/ppermute | solution.py:1020
  96.3 13.9 %collective-permute-start.13 = (bf16[128,896]{1,0:T(8,128)(2,1)S(1)}, bf16[128,896]{1,0:T(8,128)(2,1)S(1)}, u32[]{:S(2)}, u32[]{:S(2)}) collective-permute-start(bf16[128,896]{1,0:T(8,128)(2,1)S(1)} %maximum_maximum_fusion), channel_id=1, source_target_pairs={{0,8},{1,9},{2,10},{3,11},{4,12},{5,13},{6,14},{7,15},{8,0},{9,1},... | collective-permute-start | bytes 688136 | tf_op jit(solution)/shard_map/ppermute | solution.py:47
  112.0 34.3 %collective-permute-start.17 = (bf16[960,768]{1,0:T(8,128)(2,1)}, bf16[960,768]{1,0:T(8,128)(2,1)S(1)}, u32[]{:S(2)}, u32[]{:S(2)}) collective-permute-start(bf16[960,768]{1,0:T(8,128)(2,1)} %collective-permute-done.6.refs_0_), channel_id=1, source_target_pairs={{0,16},{16,0},{1,17},{17,1},{2,18},{18,2},{3,19},{19,3},{4,20},{20... | collective-permute-start | bytes 4423688 | tf_op jit(solution)/shard_map/ppermute | solution.py:1020
  117.9 27.4 %collective-permute-start.20 = (bf16[128,896]{1,0:T(8,128)(2,1)}, bf16[128,896]{1,0:T(8,128)(2,1)}, u32[]{:S(2)}, u32[]{:S(2)}) collective-permute-start(bf16[128,896]{1,0:T(8,128)(2,1)} %copy-done.83), channel_id=1, source_target_pairs={{0,6},{1,7},{2,4},{3,5},{4,2},{5,3},{6,0},{7,1},{8,14},{9,15},{10,... | collective-permute-start | bytes 688136 | tf_op jit(solution)/shard_map/ppermute | solution.py:47
  120.6 24.7 %collective-permute-start.19 = (bf16[128,896]{1,0:T(8,128)(2,1)}, bf16[128,896]{1,0:T(8,128)(2,1)}, u32[]{:S(2)}, u32[]{:S(2)}) collective-permute-start(bf16[128,896]{1,0:T(8,128)(2,1)} %copy-done.83), channel_id=1, source_target_pairs={{0,4},{1,5},{2,6},{3,7},{4,0},{5,1},{6,2},{7,3},{8,12},{9,13},{10,... | collective-permute-start | bytes 688136 | tf_op jit(solution)/shard_map/ppermute | solution.py:47
  120.9 24.4 %collective-permute-start.18 = (bf16[128,896]{1,0:T(8,128)(2,1)}, bf16[128,896]{1,0:T(8,128)(2,1)}, u32[]{:S(2)}, u32[]{:S(2)}) collective-permute-start(bf16[128,896]{1,0:T(8,128)(2,1)} %copy-done.83), channel_id=1, source_target_pairs={{0,2},{1,3},{2,0},{3,1},{4,6},{5,7},{6,4},{7,5},{8,10},{9,11},{10,... | collective-permute-start | bytes 688136 | tf_op jit(solution)/shard_map/ppermute | solution.py:47
  122.2 23.0 %collective-permute-start.21 = (f32[8,1,128]{2,1,0:T(1,128)S(1)}, f32[8,1,128]{2,1,0:T(1,128)S(1)}, u32[]{:S(2)}, u32[]{:S(2)}) collective-permute-start(f32[8,1,128]{2,1,0:T(1,128)S(1)} %bitcast.270), channel_id=1, source_target_pairs={{0,8},{1,9},{2,10},{3,11},{4,12},{5,13},{6,14},{7,15},{8,0},{9,1},... | collective-permute-start | bytes 12296 | tf_op jit(solution)/shard_map/ppermute | solution.py:47
  149.0 23.2 %collective-permute-start.23 = (bf16[128,768]{1,0:T(8,128)(2,1)S(1)}, bf16[128,768]{1,0:T(8,128)(2,1)S(1)}, u32[]{:S(2)}, u32[]{:S(2)}) collective-permute-start(bf16[128,768]{1,0:T(8,128)(2,1)S(1)} %get-tuple-element.353), channel_id=1, source_target_pairs={{0,2},{1,3},{2,0},{3,1},{4,6},{5,7},{6,4},{7,5},{8,10},{9,11},{10,... | collective-permute-start | bytes 589832 | tf_op jit(solution)/shard_map/ppermute | solution.py:47
  150.6 21.7 %collective-permute-start.25 = (bf16[128,768]{1,0:T(8,128)(2,1)S(1)}, bf16[128,768]{1,0:T(8,128)(2,1)S(1)}, u32[]{:S(2)}, u32[]{:S(2)}) collective-permute-start(bf16[128,768]{1,0:T(8,128)(2,1)S(1)} %get-tuple-element.354), channel_id=1, source_target_pairs={{0,6},{1,7},{2,4},{3,5},{4,2},{5,3},{6,0},{7,1},{8,14},{9,15},{10,... | collective-permute-start | bytes 589832 | tf_op jit(solution)/shard_map/ppermute | solution.py:47
  150.9 21.4 %collective-permute-start.24 = (bf16[128,768]{1,0:T(8,128)(2,1)S(1)}, bf16[128,768]{1,0:T(8,128)(2,1)S(1)}, u32[]{:S(2)}, u32[]{:S(2)}) collective-permute-start(bf16[128,768]{1,0:T(8,128)(2,1)S(1)} %get-tuple-element.355), channel_id=1, source_target_pairs={{0,4},{1,5},{2,6},{3,7},{4,0},{5,1},{6,2},{7,3},{8,12},{9,13},{10,... | collective-permute-start | bytes 589832 | tf_op jit(solution)/shard_map/ppermute | solution.py:47
  181.1 61.9 %all-to-all-start = ((bf16[4,128,3840]{2,1,0:T(8,128)(2,1)}), bf16[4,128,3840]{2,1,0:T(8,128)(2,1)}, u32[]{:S(2)}, u32[]{:S(2)}) async-start(bf16[4,128,3840]{2,1,0:T(8,128)(2,1)} %word_logits.2), calls=%async_computation | async-start | bytes 7864320 | tf_op jit(solution)/shard_map/all_to_all | solution.py:1097
  186.3 34.8 %collective-permute-start.27 = (bf16[960,768]{1,0:T(8,128)(2,1)S(1)}, bf16[960,768]{1,0:T(8,128)(2,1)}, u32[]{:S(2)}, u32[]{:S(2)}) collective-permute-start(bf16[960,768]{1,0:T(8,128)(2,1)S(1)} %copy-done.26), channel_id=1, source_target_pairs={{0,4},{1,5},{2,6},{3,7},{4,0},{5,1},{6,2},{7,3},{8,12},{9,13},{10,... | collective-permute-start | bytes 4423688 | tf_op jit(solution)/shard_map/ppermute | solution.py:47
  186.7 32.1 %collective-permute-start.28 = (f32[1,1920]{1,0:T(1,128)S(1)}, f32[1,1920]{1,0:T(1,128)S(1)}, u32[]{:S(2)}, u32[]{:S(2)}) collective-permute-start(f32[1,1920]{1,0:T(1,128)S(1)} %copy-done.65), channel_id=1, source_target_pairs={{0,16},{16,0},{1,17},{17,1},{2,18},{18,2},{3,19},{19,3},{4,20},{20... | collective-permute-start | bytes 23048 | tf_op jit(solution)/shard_map/ppermute | solution.py:1020
  251.5 34.4 %collective-permute-start.31 = (bf16[2,2,240,768]{3,2,1,0:T(8,128)(2,1)S(1)}, bf16[2,2,240,768]{3,2,1,0:T(8,128)(2,1)S(1)}, u32[]{:S(2)}, u32[]{:S(2)}) collective-permute-start(bf16[2,2,240,768]{3,2,1,0:T(8,128)(2,1)S(1)} %get-tuple-element.240), channel_id=1, source_target_pairs={{0,4},{1,5},{2,6},{3,7},{4,0},{5,1},{6,2},{7,3},{8,12},{9,13},{10,... | collective-permute-start | bytes 4423688 | tf_op jit(solution)/shard_map/ppermute | solution.py:47
  251.9 34.3 %collective-permute-start.32 = (bf16[2,2,240,768]{3,2,1,0:T(8,128)(2,1)S(1)}, bf16[2,2,240,768]{3,2,1,0:T(8,128)(2,1)S(1)}, u32[]{:S(2)}, u32[]{:S(2)}) collective-permute-start(bf16[2,2,240,768]{3,2,1,0:T(8,128)(2,1)S(1)} %bitcast.273), channel_id=1, source_target_pairs={{0,2},{1,3},{2,0},{3,1},{4,6},{5,7},{6,4},{7,5},{8,10},{9,11},{10,... | collective-permute-start | bytes 4423688 | tf_op jit(solution)/shard_map/ppermute | solution.py:47
  253.5 35.5 %collective-permute-start.33 = (bf16[960,768]{1,0:T(8,128)(2,1)}, bf16[960,768]{1,0:T(8,128)(2,1)S(1)}, u32[]{:S(2)}, u32[]{:S(2)}) collective-permute-start(bf16[960,768]{1,0:T(8,128)(2,1)} %collective-permute-done.27.refs_2_), channel_id=1, source_target_pairs={{0,16},{16,0},{1,17},{17,1},{2,18},{18,2},{3,19},{19,3},{4,20},{20... | collective-permute-start | bytes 4423688 | tf_op jit(solution)/shard_map/ppermute | solution.py:1020
  297.5 50.6 %all-to-all-start.1 = ((bf16[4,128,3840]{2,1,0:T(8,128)(2,1)}), bf16[4,128,3840]{2,1,0:T(8,128)(2,1)}, u32[]{:S(2)}, u32[]{:S(2)}) async-start(bf16[4,128,3840]{2,1,0:T(8,128)(2,1)} %word_logits.3), calls=%async_computation.1 | async-start | bytes 7864320 | tf_op jit(solution)/shard_map/all_to_all | solution.py:1097
  312.1 26.4 %collective-permute-start.35 = (bf16[2,240,768]{2,1,0:T(8,128)(2,1)}, bf16[2,240,768]{2,1,0:T(8,128)(2,1)S(1)}, u32[]{:S(2)}, u32[]{:S(2)}) collective-permute-start(bf16[2,240,768]{2,1,0:T(8,128)(2,1)} %bitcast.275), channel_id=1, source_target_pairs={{0,4},{1,5},{2,6},{3,7},{4,0},{5,1},{6,2},{7,3},{8,12},{9,13},{10,... | collective-permute-start | bytes 2211848 | tf_op jit(solution)/shard_map/ppermute | solution.py:47
  353.6 34.4 %collective-permute-start.42 = (bf16[960,768]{1,0:T(8,128)(2,1)S(1)}, bf16[960,768]{1,0:T(8,128)(2,1)S(1)}, u32[]{:S(2)}, u32[]{:S(2)}) collective-permute-start(bf16[960,768]{1,0:T(8,128)(2,1)S(1)} %get-tuple-element.340), channel_id=1, source_target_pairs={{0,16},{16,0},{1,17},{17,1},{2,18},{18,2},{3,19},{19,3},{4,20},{20... | collective-permute-start | bytes 4423688 | tf_op jit(solution)/shard_map/ppermute | solution.py:1020
  355.9 21.4 %collective-permute-start.39 = (bf16[4,56,768]{2,1,0:T(8,128)(2,1)S(1)}, bf16[4,56,768]{2,1,0:T(8,128)(2,1)S(1)}, u32[]{:S(2)}, u32[]{:S(2)}) collective-permute-start(bf16[4,56,768]{2,1,0:T(8,128)(2,1)S(1)} %bitcast.291), channel_id=1, source_target_pairs={{0,2},{1,3},{2,0},{3,1},{4,6},{5,7},{6,4},{7,5},{8,10},{9,11},{10,... | collective-permute-start | bytes 1032200 | tf_op jit(solution)/shard_map/ppermute | solution.py:47
  356.8 31.4 %collective-permute-start.40 = (bf16[2,2,144,768]{3,2,1,0:T(8,128)(2,1)S(1)}, bf16[2,2,144,768]{3,2,1,0:T(8,128)(2,1)S(1)}, u32[]{:S(2)}, u32[]{:S(2)}) collective-permute-start(bf16[2,2,144,768]{3,2,1,0:T(8,128)(2,1)S(1)} %get-tuple-element.288), channel_id=1, source_target_pairs={{0,4},{1,5},{2,6},{3,7},{4,0},{5,1},{6,2},{7,3},{8,12},{9,13},{10,... | collective-permute-start | bytes 2654216 | tf_op jit(solution)/shard_map/ppermute | solution.py:47
  357.7 23.8 %collective-permute-start.41 = (bf16[2,240,768]{2,1,0:T(8,128)(2,1)S(1)}, bf16[2,240,768]{2,1,0:T(8,128)(2,1)S(1)}, u32[]{:S(2)}, u32[]{:S(2)}) collective-permute-start(bf16[2,240,768]{2,1,0:T(8,128)(2,1)S(1)} %bitcast.274), channel_id=1, source_target_pairs={{0,2},{1,3},{2,0},{3,1},{4,6},{5,7},{6,4},{7,5},{8,10},{9,11},{10,... | collective-permute-start | bytes 2211848 | tf_op jit(solution)/shard_map/ppermute | solution.py:47
  359.4 28.8 %collective-permute-start.43 = (bf16[240,768]{1,0:T(8,128)(2,1)S(1)}, bf16[240,768]{1,0:T(8,128)(2,1)}, u32[]{:S(2)}, u32[]{:S(2)}) collective-permute-start(bf16[240,768]{1,0:T(8,128)(2,1)S(1)} %bitcast.277), channel_id=1, source_target_pairs={{0,8},{1,9},{2,10},{3,11},{4,12},{5,13},{6,14},{7,15},{8,0},{9,1},... | collective-permute-start | bytes 1105928 | tf_op jit(solution)/shard_map/ppermute | solution.py:47
  377.5 31.4 %collective-permute-start.45 = (bf16[8,56,768]{2,1,0:T(8,128)(2,1)S(1)}, bf16[8,56,768]{2,1,0:T(8,128)(2,1)}, u32[]{:S(2)}, u32[]{:S(2)}) collective-permute-start(bf16[8,56,768]{2,1,0:T(8,128)(2,1)S(1)} %bitcast.286), channel_id=1, source_target_pairs={{0,1},{1,0},{2,3},{3,2},{4,5},{5,4},{6,7},{7,6},{8,9},{9,8},{10,11... | collective-permute-start | bytes 2064392 | tf_op jit(solution)/shard_map/ppermute | solution.py:47
  390.2 18.7 %collective-permute-start.46 = (bf16[240,768]{1,0:T(8,128)(2,1)S(1)}, bf16[240,768]{1,0:T(8,128)(2,1)S(1)}, u32[]{:S(2)}, u32[]{:S(2)}) collective-permute-start(bf16[240,768]{1,0:T(8,128)(2,1)S(1)} %bitcast.278), channel_id=1, source_target_pairs={{0,8},{1,9},{2,10},{3,11},{4,12},{5,13},{6,14},{7,15},{8,0},{9,1},... | collective-permute-start | bytes 1105928 | tf_op jit(solution)/shard_map/ppermute | solution.py:47
  392.4 33.7 %collective-permute-start.48 = (bf16[960,768]{1,0:T(8,128)(2,1)}, bf16[960,768]{1,0:T(8,128)(2,1)}, u32[]{:S(2)}, u32[]{:S(2)}) collective-permute-start(bf16[960,768]{1,0:T(8,128)(2,1)} %get-tuple-element.339), channel_id=1, source_target_pairs={{0,16},{16,0},{1,17},{17,1},{2,18},{18,2},{3,19},{19,3},{4,20},{20... | collective-permute-start | bytes 4423688 | tf_op jit(solution)/shard_map/ppermute | solution.py:1020
  (125 other events, 1053.4 us)

commit v4 on v3

--- a/solution.py
+++ b/solution.py
@@ -104,11 +104,12 @@
     k = k_ref[...]
     v_t = v_ref[...].T
     head_of = lax.broadcasted_iota(jnp.int32, (rows, lanes), 1) // head_dim
-    visible = lax.broadcasted_iota(jnp.int32, (rows, rows), 0) < length
+    half = rows // 2
+    visible = lax.broadcasted_iota(jnp.int32, (rows - half, rows), 0) < length - half
     parts = []
     for head in range(lanes // head_dim):
         scores = back_mul(k, jnp.where(head_of == head, q, jnp.zeros_like(q)))
-        scores = jnp.where(visible, scores, HIDDEN)
+        scores = jnp.concatenate([scores[:half], jnp.where(visible, scores[half:], HIDDEN)])
         peak = jnp.max(scores, axis=0, keepdims=True)
         powers = jnp.exp(scores - peak)
         total = jnp.sum(powers, axis=0, keepdims=True)
@@ -153,12 +154,14 @@
     v = v_ref[...]
     grad = grad_ref[...]
     head_of = lax.broadcasted_iota(jnp.int32, (rows, lanes), 1) // head_dim
-    visible = lax.broadcasted_iota(jnp.int32, (rows, rows), 0) < length
+    half = rows // 2
+    visible = lax.broadcasted_iota(jnp.int32, (rows - half, rows), 0) < length - half
     totals = [jnp.zeros((rows, lanes), F32)] * 3
     for head in range(lanes // head_dim):
         mine = head_of == head
         scores = back_mul(k, jnp.where(mine, q, jnp.zeros_like(q)))
-        share = jnp.where(visible, jnp.exp(scores - log_ref[0, head : head + 1, :]), 0.0)
+        share = jnp.exp(scores - log_ref[0, head : head + 1, :])
+        share = jnp.concatenate([share[:half], jnp.where(visible, share[half:], 0.0)])
         share_grad = back_mul(jnp.where(mine, v, jnp.zeros_like(v)), grad)
         inner = jnp.sum(share * share_grad, axis=0, keepdims=True)
         score_grad = (share * (share_grad - inner)).astype(BF16)
@@ -1133,7 +1136,7 @@
     logits_side = exchanged(logits_side)
     cls_grad = passed_along(cls_back(parts, one, joint, count), "section", -1)
     cls_grad, table_grad = tied(cls_grad, table_grad)
-    table_top = across(table_grad[:half])
+    table_other = across(table_grad)
 
     branch_f, hidden_f, mixed_f, one_f, sums_f, shift_f, parts, part_sums = first_back(
         cls_grad, kept, mats, gain, qkv, parts, lengths
@@ -1185,8 +1188,7 @@
             input_grad, logits_near, logits_side = tied(input_grad, logits_near, logits_side)
             logits_out = assembled(place32, logits_near, logits_side)
             logits_out, arriving = tied(logits_out, arriving)
-    logits_out, one_got, table_top = tied(logits_out, one_state[1], table_top)
-    table_rest = across(table_grad[half:])
+    logits_out, one_got = tied(logits_out, one_state[1])
     one_halves = added((one_state[0], one_got, one_state[2]), order[2])
     logits_out, one_now = tied(logits_out, one_halves[:2])
     one_state = sent((*one_now, one_halves[2]), order[2])
@@ -1202,9 +1204,9 @@
     joint_keep, arriving, one_got = tied(joint_keep, arriving, one_state[1])
     one_state = one_state[0], one_got, one_state[2]
     contract_sum, mixer_sum = unstacked(rest_of(one_state, order[3:]), [(units // groups, width), (own, width)])
-    joint_got, table_rest = tied(joint_got, table_rest)
+    joint_got, table_other = tied(joint_got, table_other)
     joint_sum = unstacked(rest_of((joint_keep, joint_got, axes), order[3:]), [(own, 3 * width)])[0]
-    table_total = table_grad.astype(F32) + jnp.concatenate([table_top, table_rest]).astype(F32)
+    table_total = table_grad.astype(F32) + table_other.astype(F32)
     rows_all = side_by_side(gathered, arriving, 1)
     small = jnp.sum(rows_all[:, counts[0] :].astype(F32), axis=0)
     small = small[: counts[1]] + small[counts[1] :]

time: 439 us -> 468 us (1.066)
  waiting for transfers between devices: 52.1 us -> 86.6 us
    ppermute x7 -> x6, waiting for transfers between devices: 17.5 us -> 43.4 us  [on_device(): across = lambda array: lax.ppermute(array, 'section', [(0, 1), (1, 0)])]
    ppermute x40, waiting for transfers between devices: 31.9 us -> 40.2 us  [swapped(): return lax.ppermute(block, 'dp', [(i, i ^ bit) for i in devices])]
    ppermute x7 -> x6, starting transfers between devices: 10.9 us -> 9.51 us  [on_device(): across = lambda array: lax.ppermute(array, 'section', [(0, 1), (1, 0)])]
    unnamed x220 -> x224, local copies, waits for them, and re-layouts: 33.2 us -> 32.3 us
  transfers between devices with their start and end apart: 51 -> 50, of which waited for: 18 -> 21; matrix products, arithmetic and copies ran while one was open for 9% -> 8% of each run, Pallas kernels for 49% -> 45%
where the time goes in v4:
time: 468 us; the launch traced here: 464 us
  Pallas kernels  230 us (49%)
  waiting for transfers between devices  86.6 us (19%)
  starting transfers between devices  63.9 us (14%)
  local copies, waits for them, and re-layouts  47.7 us (10%)
  other arithmetic  22 us (5%)
  matrix products  7.68 us (2%)
  between operations  5.66 us (1%)
    ppermute x6, waiting for transfers between devices, on_device(): across = lambda array: lax.ppermute(array, 'section', [(0, 1), (1, 0)])  43.4 us
    ppermute x40, waiting for transfers between devices, swapped(): return lax.ppermute(block, 'dp', [(i, i ^ bit) for i in devices])  40.2 us
    ppermute x40, starting transfers between devices, swapped(): return lax.ppermute(block, 'dp', [(i, i ^ bit) for i in devices])  39 us
    unnamed x224, local copies, waits for them, and re-layouts  32.3 us
    pallas_call x1, Pallas kernels, attend_back(): pl.pallas_call(functools.partial(attend_back_kernel, head_dim=head_dim),...  29.2 us
    pallas_call x5, Pallas kernels, weight_grads(): pl.pallas_call(weight_grad_kernel, grid_spec=pltpu.PrefetchScalarGridSpec...  28 us
    pallas_call x1, Pallas kernels, tail_back(): pl.pallas_call(functools.partial(tail_back_kernel, chunk=min(chunk, hidde...  22.8 us
    pallas_call x1, Pallas kernels, layer_tail(): pl.pallas_call(functools.partial(tail_kernel, chunk=min(chunk, hidden)),...  22 us
  transfers between devices with their start and end apart: 50, of which 21 were waited for; matrix products, arithmetic and copies ran while one was open for 8% of the time, Pallas kernels for 45%

profile of v4, /device:TPU:0, one launch (start us, length us, event | category | flops | bytes accessed | tf_op | source)
XLA Modules:
  0.0 463.5 jit_solution(13595669279476289899)
XLA Ops:
  4.7 4.0 collective-permute-start.1
  13.2 4.4 project.1.refs_2_.qkv_ref
  17.6 4.1 cls_forward.1
  21.7 3.6 collective-permute-start
  29.6 17.1 %attend.1 = (bf16[1024,768]{1,0:T(8,128)(2,1)S(1)}, f32[12,2,512]{2,1,0:T(2,128)S(1)}) custom-call(s32[2]{0:T(128)S(1)} %copy-done.62, bf16[1024,2304]{1,0:T(8,128)(2,1)} %copy-done.2, bf16[1024,2304]{1,0:T(8,128)(2,1)} %copy-done.2, bf16[1024,2304]{1,0:T(8,128)(2,1)} %copy-done.2), custom_call_target="tpu_custom_call" | custom-call | tf_op jit(solution)/shard_map/attend/pallas_call | solution.py:128
  53.2 22.0 %layer_tail.1 = (bf16[1024,768]{1,0:T(8,128)(2,1)S(1)}, bf16[1024,768]{1,0:T(8,128)(2,1)S(1)}, f32[1024,128]{1,0:T(8,128)S(1)}, bf16[1024,768]{1,0:T(8,128)(2,1)...) custom-call(bf16[1024,768]{1,0:T(8,128)(2,1)} %copy-done.30, ...), custom_call_target="tpu_custom_call" | custom-call | tf_op jit(solution)/shard_map/layer_tail/pallas_call | solution.py:243
  83.6 8.1 %collective-permute-done.11 = bf16[1920]{0:T(1024)(128)(2,1)S(1)} collective-permute-done((bf16[1920]{0:T(1024)(128)(2,1)S(1)}, bf16[1920]{0:T(1024)(128)(2,1)S(1)}, u32[]{:S(2)}, u32[]{:S(2)}) %collective-permute-start.11) | collective-permute-done | bytes 3872 | tf_op jit(solution)/shard_map/ppermute | solution.py:47
  98.3 11.4 %word_scores.1 = (f32[8,1,128]{2,1,0:T(1,128)S(1)}, f32[8,1,128]{2,1,0:T(1,128)S(1)}) custom-call(s32[1]{0:T(128)} %bitcast.decoder.section, bf16[8,128,896]{2,1,0:T(8,128)(2,1)S(1)} %bitcast.200, bf16[1920,768]{1,0:T(8,128)(2,1)} %refs_0_.1, bf16[960,768]{1,0:T(8,128)(2,1)S(1)} %constant_dynamic-update-slice_fusion.mine_ref.refs_1_, ...), custom_call_target="tpu_custom_call" | custom-call | tf_op jit(solution)/shard_map/word_scores/pallas_call | solution.py:769
  117.6 3.0 collective-permute-start.20
  126.8 18.4 %word_back.1 = (bf16[8,128,1920]{2,1,0:T(8,128)(2,1)}, bf16[8,128,768]{2,1,0:T(8,128)(2,1)S(1)}, f32[8,1,128]{2,1,0:T(1,128)S(1)}) custom-call(s32[3]{0:T(128)S(1)} %pad_add_fusion.first, bf16[8,128,896]{2,1,0:T(8,128)(2,1)} %bitcast.201, f32[8,1,128]{2,1,0:T(1,128)S(1)} %bitcast.271, bf16[1920,768]{1,0:T(8,128)(2,1)} %refs_0_.1, ...), custom_call_target="tpu_custom_call" | custom-call | tf_op jit(solution)/shard_map/word_back/pallas_call | solution.py:866
  154.3 17.9 %table_gradient.1 = (bf16[1920,768]{1,0:T(8,128)(2,1)}, f32[1,1920]{1,0:T(1,128)S(1)}) custom-call(s32[3]{0:T(128)S(1)} %pad_add_fusion.first, bf16[8,128,1920]{2,1,0:T(8,128)(2,1)} %get-tuple-element.194.grad_ref, bf16[8,128,896]{2,1,0:T(8,128)(2,1)S(1)} %bitcast.203, bf16[8,128,896]{2,1,0:T(8,128)(2,1)S(1)} %bitcast.217, ...), custom_call_target="tpu_custom_call" | custom-call | tf_op jit(solution)/shard_map/table_gradient/pallas_call | solution.py:917
  173.1 8.0 %word_logits.2 = bf16[4,128,3840]{2,1,0:T(8,128)(2,1)} custom-call(s32[2]{0:T(128)S(1)} %pad_add_fusion.1.place, bf16[8,128,896]{2,1,0:T(8,128)(2,1)S(1)} %bitcast.204, bf16[1920,768]{1,0:T(8,128)(2,1)} %refs_0_.1, bf16[960,768]{1,0:T(8,128)(2,1)S(1)} %copy-done.25, bf16[960,768]{1,0:T(8,128)(2,1)S(1)} %copy-done.22, ...), custom_call_target="tpu_custom_call" | custom-call | tf_op jit(solution)/shard_map/word_logits/pallas_call | solution.py:814
  181.1 5.1 %all-to-all-start = ((bf16[4,128,3840]{2,1,0:T(8,128)(2,1)}), bf16[4,128,3840]{2,1,0:T(8,128)(2,1)}, u32[]{:S(2)}, u32[]{:S(2)}) async-start(bf16[4,128,3840]{2,1,0:T(8,128)(2,1)} %word_logits.2), calls=%async_computation | async-start | bytes 7864320 | tf_op jit(solution)/shard_map/all_to_all | solution.py:1100
  192.9 3.2 fusion.14
  196.1 22.8 %tail_back.1 = (bf16[1024,768]{1,0:T(8,128)(2,1)S(1)}, bf16[1024,3072]{1,0:T(8,128)(2,1)}, f32[1024,768]{1,0:T(8,128)}, bf16[1024,768]{1,0:T(8,128)(2,1)S(1)}, b...) custom-call(f32[1024,768]{1,0:T(8,128)} %bitcast.280, ...), custom_call_target="tpu_custom_call" | custom-call | tf_op jit(solution)/shard_map/tail_back/pallas_call | solution.py:301
  221.1 8.5 %weight_grad.5 = (bf16[8,240,768]{2,1,0:T(8,128)(2,1)S(1)}, bf16[8,240,768]{2,1,0:T(8,128)(2,1)}) custom-call(s32[1]{0:T(128)} %bitcast.11.place, bf16[1024,3072]{1,0:T(8,128)(2,1)} %get-tuple-element.171.left_ref, bf16[1,1024,768]{2,1,0:T(8,128)(2,1)S(1)} %bitcast.254), custom_call_target="tpu_custom_call" | custom-call | tf_op jit(solution)/shard_map/weight_grad/pallas_call | solution.py:628
  232.0 9.7 %weight_grad.7 = (bf16[8,240,768]{2,1,0:T(8,128)(2,1)S(1)}, bf16[8,240,768]{2,1,0:T(8,128)(2,1)}) custom-call(s32[1]{0:T(128)} %bitcast.11.place, bf16[1024,768]{1,0:T(8,128)(2,1)S(1)} %copy-done.43, bf16[1,1024,3072]{2,1,0:T(8,128)(2,1)} %bitcast.282), custom_call_target="tpu_custom_call" | custom-call | tf_op jit(solution)/shard_map/weight_grad/pallas_call | solution.py:628
  248.8 2.7 add_split.10
  256.0 29.2 %attend_back.1.refs_0_.refs_1_.refs_15_ = bf16[3,1024,768]{2,1,0:T(8,128)(2,1)} custom-call(s32[2]{0:T(128)S(1)} %copy-done.63, bf16[1024,2304]{1,0:T(8,128)(2,1)} %copy-done.2, bf16[1024,2304]{1,0:T(8,128)(2,1)} %copy-done.2, bf16[1024,2304]{1,0:T(8,128)(2,1)} %copy-done.2, bf16[1024,768]{1,0:T(8,128)(2,1)S(1)} %copy-done.44, f32[12,2,512]{2,1,0:T(2,128)S(1)} %copy-done.53), custom_call_target="tpu_custom_call" | custom-call | tf_op jit(solution)/shard_map/attend_back/pallas_call | solution.py:185
  289.1 8.4 %word_logits.3 = bf16[4,128,3840]{2,1,0:T(8,128)(2,1)} custom-call(s32[2]{0:T(128)S(1)} %copy-done.70, bf16[8,128,896]{2,1,0:T(8,128)(2,1)} %bitcast.202, bf16[960,768]{1,0:T(8,128)(2,1)} %collective-permute-done.6.refs_0_, bf16[960,768]{1,0:T(8,128)(2,1)S(1)} %copy-done.46, bf16[960,768]{1,0:T(8,128)(2,1)} %collective-permute-done.27.refs_2_, ...), custom_call_target="tpu_custom_call" | custom-call | tf_op jit(solution)/shard_map/word_logits/pallas_call | solution.py:814
  297.5 5.1 %all-to-all-start.1 = ((bf16[4,128,3840]{2,1,0:T(8,128)(2,1)}), bf16[4,128,3840]{2,1,0:T(8,128)(2,1)}, u32[]{:S(2)}, u32[]{:S(2)}) async-start(bf16[4,128,3840]{2,1,0:T(8,128)(2,1)} %word_logits.3), calls=%async_computation.1 | async-start | bytes 7864320 | tf_op jit(solution)/shard_map/all_to_all | solution.py:1100
  304.3 3.1 cls_back.1
  324.1 10.1 %first_back.1 = (bf16[16,768]{1,0:T(8,128)(2,1)S(1)}, bf16[16,3072]{1,0:T(8,128)(2,1)S(1)}, bf16[16,768]{1,0:T(8,128)(2,1)S(1)}, f32[16,768]{1,0:T(8,128)S(1)}, ...) custom-call(s32[2]{0:T(128)S(1)} %copy-done.63, ...), custom_call_target="tpu_custom_call" | custom-call | tf_op jit(solution)/shard_map/first_back/pallas_call | solution.py:521
  338.6 6.2 %weight_grad.9 = (bf16[8,144,768]{2,1,0:T(8,128)(2,1)S(1)}, bf16[8,144,768]{2,1,0:T(8,128)(2,1)S(1)}) custom-call(s32[1]{0:T(128)} %bitcast.11.place, bf16[1024,768]{1,0:T(8,128)(2,1)S(1)} %copy-done.4, bf16[3,1024,768]{2,1,0:T(8,128)(2,1)} %copy-done.19), custom_call_target="tpu_custom_call" | custom-call | tf_op jit(solution)/shard_map/weight_grad/pallas_call | solution.py:628
  352.4 3.5 collective-permute-done.38
  360.1 8.3 %input_gradient.1 = f32[1024,768]{1,0:T(8,128)} custom-call(s32[1]{0:T(128)} %bitcast.decoder.section, bf16[3,1024,768]{2,1,0:T(8,128)(2,1)} %copy-done.19, f32[1024,768]{1,0:T(8,128)S(1)} %copy-done.12, f32[16,768]{1,0:T(8,128)S(1)} %get-tuple-element.280.first_ref, bf16[768,2304]{1,0:T(8,128)(2,1)} %bitcast.206), custom_call_target="tpu_custom_call" | custom-call | tf_op jit(solution)/shard_map/input_gradient/pallas_call | solution.py:576
  368.4 8.9 %assemble.1 = bf16[128,30720]{1,0:T(8,128)(2,1)} custom-call(s32[1]{0:T(128)} %bitcast.11.place, bf16[4,128,3840]{2,1,0:T(8,128)(2,1)} %all-to-all-done.near_ref, bf16[4,128,3840]{2,1,0:T(8,128)(2,1)} %all-to-all-done.1.side_ref), custom_call_target="tpu_custom_call" | custom-call | tf_op jit(solution)/shard_map/assemble/pallas_call | solution.py:967
  377.6 3.9 collective-permute-done.41
  393.3 2.9 collective-permute-done.43
  396.3 8.5 %collective-permute-done.45 = bf16[240,768]{1,0:T(8,128)(2,1)S(1)} collective-permute-done((bf16[240,768]{1,0:T(8,128)(2,1)S(1)}, bf16[240,768]{1,0:T(8,128)(2,1)S(1)}, u32[]{:S(2)}, u32[]{:S(2)}) %collective-permute-start.45) | collective-permute-done | bytes 368672 | tf_op jit(solution)/shard_map/ppermute | solution.py:47
  413.9 40.7 %collective-permute-done.47 = bf16[1920,768]{1,0:T(8,128)(2,1)} collective-permute-done((bf16[1920,768]{1,0:T(8,128)(2,1)}, bf16[1920,768]{1,0:T(8,128)(2,1)}, u32[]{:S(2)}, u32[]{:S(2)}) %collective-permute-start.47) | collective-permute-done | bytes 2949152 | tf_op jit(solution)/shard_map/ppermute | solution.py:1023
  456.1 6.0 %convert_add_fusion = f32[1920,768]{1,0:T(8,128)} fusion(bf16[1920,768]{1,0:T(8,128)(2,1)} %collective-permute-done.47, bf16[1920,768]{1,0:T(8,128)(2,1)} %get-tuple-element.313), kind=kLoop, calls=%fused_computation | loop fusion | flops 4423680 | bytes 11796480 | tf_op jit(solution)/shard_map/add | solution.py:1209
  (438 shorter events, 138.8 us)
Async XLA Ops:
  4.7 42.6 %collective-permute-start.1 = (bf16[480,768]{1,0:T(8,128)(2,1)S(1)}, bf16[480,768]{1,0:T(8,128)(2,1)}, u32[]{:S(2)}, u32[]{:S(2)}) collective-permute-start(bf16[480,768]{1,0:T(8,128)(2,1)S(1)} %get-tuple-element.338), channel_id=1, source_target_pairs={{0,8},{1,9},{2,10},{3,11},{4,12},{5,13},{6,14},{7,15},{8,0},{9,1},... | collective-permute-start | bytes 2211848 | tf_op jit(solution)/shard_map/ppermute | solution.py:47
  11.4 64.6 %collective-permute-start.6 = (bf16[960,768]{1,0:T(8,128)(2,1)}, bf16[960,768]{1,0:T(8,128)(2,1)}, u32[]{:S(2)}, u32[]{:S(2)}) collective-permute-start(bf16[960,768]{1,0:T(8,128)(2,1)} %constant_dynamic-slice_fusion.2), channel_id=1, source_target_pairs={{0,4},{1,5},{2,6},{3,7},{4,0},{5,1},{6,2},{7,3},{8,12},{9,13},{10,... | collective-permute-start | bytes 4423688 | tf_op jit(solution)/shard_map/ppermute | solution.py:47
  25.3 50.7 %collective-permute-start.3 = (bf16[480,768]{1,0:T(8,128)(2,1)}, bf16[480,768]{1,0:T(8,128)(2,1)}, u32[]{:S(2)}, u32[]{:S(2)}) collective-permute-start(bf16[480,768]{1,0:T(8,128)(2,1)} %get-tuple-element.337), channel_id=1, source_target_pairs={{0,8},{1,9},{2,10},{3,11},{4,12},{5,13},{6,14},{7,15},{8,0},{9,1},... | collective-permute-start | bytes 2211848 | tf_op jit(solution)/shard_map/ppermute | solution.py:47
  48.5 27.5 %collective-permute-start.2 = (bf16[480,768]{1,0:T(8,128)(2,1)}, bf16[480,768]{1,0:T(8,128)(2,1)S(1)}, u32[]{:S(2)}, u32[]{:S(2)}) collective-permute-start(bf16[480,768]{1,0:T(8,128)(2,1)} %collective-permute-done.1), channel_id=1, source_target_pairs={{0,16},{16,0},{1,17},{17,1},{2,18},{18,2},{3,19},{19,3},{4,20},{20... | collective-permute-start | bytes 2211848 | tf_op jit(solution)/shard_map/ppermute | solution.py:1023
  50.8 24.4 %collective-permute-start.4 = (bf16[1920]{0:T(1024)(128)(2,1)S(1)}, bf16[1920]{0:T(1024)(128)(2,1)S(1)}, u32[]{:S(2)}, u32[]{:S(2)}) collective-permute-start(bf16[1920]{0:T(1024)(128)(2,1)S(1)} %copy-done.98), channel_id=1, source_target_pairs={{0,8},{1,9},{2,10},{3,11},{4,12},{5,13},{6,14},{7,15},{8,0},{9,1},... | collective-permute-start | bytes 11528 | tf_op jit(solution)/shard_map/ppermute | solution.py:47
  51.1 24.9 %collective-permute-start.5 = (bf16[1920]{0:T(1024)(128)(2,1)S(1)}, bf16[1920]{0:T(1024)(128)(2,1)S(1)}, u32[]{:S(2)}, u32[]{:S(2)}) collective-permute-start(bf16[1920]{0:T(1024)(128)(2,1)S(1)} %copy-done.98), channel_id=1, source_target_pairs={{0,4},{1,5},{2,6},{3,7},{4,0},{5,1},{6,2},{7,3},{8,12},{9,13},{10,... | collective-permute-start | bytes 11528 | tf_op jit(solution)/shard_map/ppermute | solution.py:47
  76.1 17.4 %collective-permute-start.10 = (bf16[480,768]{1,0:T(8,128)(2,1)}, bf16[480,768]{1,0:T(8,128)(2,1)S(1)}, u32[]{:S(2)}, u32[]{:S(2)}) collective-permute-start(bf16[480,768]{1,0:T(8,128)(2,1)} %collective-permute-done.3), channel_id=1, source_target_pairs={{0,16},{16,0},{1,17},{17,1},{2,18},{18,2},{3,19},{19,3},{4,20},{20... | collective-permute-start | bytes 2211848 | tf_op jit(solution)/shard_map/ppermute | solution.py:1023
  96.3 13.6 %collective-permute-start.13 = (bf16[128,896]{1,0:T(8,128)(2,1)S(1)}, bf16[128,896]{1,0:T(8,128)(2,1)S(1)}, u32[]{:S(2)}, u32[]{:S(2)}) collective-permute-start(bf16[128,896]{1,0:T(8,128)(2,1)S(1)} %maximum_maximum_fusion), channel_id=1, source_target_pairs={{0,8},{1,9},{2,10},{3,11},{4,12},{5,13},{6,14},{7,15},{8,0},{9,1},... | collective-permute-start | bytes 688136 | tf_op jit(solution)/shard_map/ppermute | solution.py:47
  112.0 34.3 %collective-permute-start.17 = (bf16[960,768]{1,0:T(8,128)(2,1)}, bf16[960,768]{1,0:T(8,128)(2,1)S(1)}, u32[]{:S(2)}, u32[]{:S(2)}) collective-permute-start(bf16[960,768]{1,0:T(8,128)(2,1)} %collective-permute-done.6.refs_0_), channel_id=1, source_target_pairs={{0,16},{16,0},{1,17},{17,1},{2,18},{18,2},{3,19},{19,3},{4,20},{20... | collective-permute-start | bytes 4423688 | tf_op jit(solution)/shard_map/ppermute | solution.py:1023
  117.6 27.6 %collective-permute-start.20 = (bf16[128,896]{1,0:T(8,128)(2,1)}, bf16[128,896]{1,0:T(8,128)(2,1)}, u32[]{:S(2)}, u32[]{:S(2)}) collective-permute-start(bf16[128,896]{1,0:T(8,128)(2,1)} %copy-done.85), channel_id=1, source_target_pairs={{0,6},{1,7},{2,4},{3,5},{4,2},{5,3},{6,0},{7,1},{8,14},{9,15},{10,... | collective-permute-start | bytes 688136 | tf_op jit(solution)/shard_map/ppermute | solution.py:47
  120.6 24.7 %collective-permute-start.19 = (bf16[128,896]{1,0:T(8,128)(2,1)}, bf16[128,896]{1,0:T(8,128)(2,1)}, u32[]{:S(2)}, u32[]{:S(2)}) collective-permute-start(bf16[128,896]{1,0:T(8,128)(2,1)} %copy-done.85), channel_id=1, source_target_pairs={{0,4},{1,5},{2,6},{3,7},{4,0},{5,1},{6,2},{7,3},{8,12},{9,13},{10,... | collective-permute-start | bytes 688136 | tf_op jit(solution)/shard_map/ppermute | solution.py:47
  120.6 24.7 %collective-permute-start.18 = (bf16[128,896]{1,0:T(8,128)(2,1)}, bf16[128,896]{1,0:T(8,128)(2,1)}, u32[]{:S(2)}, u32[]{:S(2)}) collective-permute-start(bf16[128,896]{1,0:T(8,128)(2,1)} %copy-done.85), channel_id=1, source_target_pairs={{0,2},{1,3},{2,0},{3,1},{4,6},{5,7},{6,4},{7,5},{8,10},{9,11},{10,... | collective-permute-start | bytes 688136 | tf_op jit(solution)/shard_map/ppermute | solution.py:47
  122.1 23.2 %collective-permute-start.21 = (f32[8,1,128]{2,1,0:T(1,128)S(1)}, f32[8,1,128]{2,1,0:T(1,128)S(1)}, u32[]{:S(2)}, u32[]{:S(2)}) collective-permute-start(f32[8,1,128]{2,1,0:T(1,128)S(1)} %bitcast.270), channel_id=1, source_target_pairs={{0,8},{1,9},{2,10},{3,11},{4,12},{5,13},{6,14},{7,15},{8,0},{9,1},... | collective-permute-start | bytes 12296 | tf_op jit(solution)/shard_map/ppermute | solution.py:47
  149.0 23.2 %collective-permute-start.23 = (bf16[128,768]{1,0:T(8,128)(2,1)S(1)}, bf16[128,768]{1,0:T(8,128)(2,1)S(1)}, u32[]{:S(2)}, u32[]{:S(2)}) collective-permute-start(bf16[128,768]{1,0:T(8,128)(2,1)S(1)} %get-tuple-element.349), channel_id=1, source_target_pairs={{0,2},{1,3},{2,0},{3,1},{4,6},{5,7},{6,4},{7,5},{8,10},{9,11},{10,... | collective-permute-start | bytes 589832 | tf_op jit(solution)/shard_map/ppermute | solution.py:47
  150.6 21.7 %collective-permute-start.25 = (bf16[128,768]{1,0:T(8,128)(2,1)S(1)}, bf16[128,768]{1,0:T(8,128)(2,1)S(1)}, u32[]{:S(2)}, u32[]{:S(2)}) collective-permute-start(bf16[128,768]{1,0:T(8,128)(2,1)S(1)} %get-tuple-element.350), channel_id=1, source_target_pairs={{0,6},{1,7},{2,4},{3,5},{4,2},{5,3},{6,0},{7,1},{8,14},{9,15},{10,... | collective-permute-start | bytes 589832 | tf_op jit(solution)/shard_map/ppermute | solution.py:47
  150.9 21.4 %collective-permute-start.24 = (bf16[128,768]{1,0:T(8,128)(2,1)S(1)}, bf16[128,768]{1,0:T(8,128)(2,1)S(1)}, u32[]{:S(2)}, u32[]{:S(2)}) collective-permute-start(bf16[128,768]{1,0:T(8,128)(2,1)S(1)} %get-tuple-element.351), channel_id=1, source_target_pairs={{0,4},{1,5},{2,6},{3,7},{4,0},{5,1},{6,2},{7,3},{8,12},{9,13},{10,... | collective-permute-start | bytes 589832 | tf_op jit(solution)/shard_map/ppermute | solution.py:47
  181.1 61.9 %all-to-all-start = ((bf16[4,128,3840]{2,1,0:T(8,128)(2,1)}), bf16[4,128,3840]{2,1,0:T(8,128)(2,1)}, u32[]{:S(2)}, u32[]{:S(2)}) async-start(bf16[4,128,3840]{2,1,0:T(8,128)(2,1)} %word_logits.2), calls=%async_computation | async-start | bytes 7864320 | tf_op jit(solution)/shard_map/all_to_all | solution.py:1100
  186.3 34.8 %collective-permute-start.27 = (bf16[960,768]{1,0:T(8,128)(2,1)S(1)}, bf16[960,768]{1,0:T(8,128)(2,1)}, u32[]{:S(2)}, u32[]{:S(2)}) collective-permute-start(bf16[960,768]{1,0:T(8,128)(2,1)S(1)} %copy-done.26), channel_id=1, source_target_pairs={{0,4},{1,5},{2,6},{3,7},{4,0},{5,1},{6,2},{7,3},{8,12},{9,13},{10,... | collective-permute-start | bytes 4423688 | tf_op jit(solution)/shard_map/ppermute | solution.py:47
  186.7 32.1 %collective-permute-start.28 = (f32[1,1920]{1,0:T(1,128)S(1)}, f32[1,1920]{1,0:T(1,128)S(1)}, u32[]{:S(2)}, u32[]{:S(2)}) collective-permute-start(f32[1,1920]{1,0:T(1,128)S(1)} %copy-done.65), channel_id=1, source_target_pairs={{0,16},{16,0},{1,17},{17,1},{2,18},{18,2},{3,19},{19,3},{4,20},{20... | collective-permute-start | bytes 23048 | tf_op jit(solution)/shard_map/ppermute | solution.py:1023
  251.5 34.4 %collective-permute-start.31 = (bf16[2,2,240,768]{3,2,1,0:T(8,128)(2,1)S(1)}, bf16[2,2,240,768]{3,2,1,0:T(8,128)(2,1)S(1)}, u32[]{:S(2)}, u32[]{:S(2)}) collective-permute-start(bf16[2,2,240,768]{3,2,1,0:T(8,128)(2,1)S(1)} %get-tuple-element.239), channel_id=1, source_target_pairs={{0,4},{1,5},{2,6},{3,7},{4,0},{5,1},{6,2},{7,3},{8,12},{9,13},{10,... | collective-permute-start | bytes 4423688 | tf_op jit(solution)/shard_map/ppermute | solution.py:47
  251.9 34.3 %collective-permute-start.32 = (bf16[2,2,240,768]{3,2,1,0:T(8,128)(2,1)S(1)}, bf16[2,2,240,768]{3,2,1,0:T(8,128)(2,1)S(1)}, u32[]{:S(2)}, u32[]{:S(2)}) collective-permute-start(bf16[2,2,240,768]{3,2,1,0:T(8,128)(2,1)S(1)} %bitcast.273), channel_id=1, source_target_pairs={{0,2},{1,3},{2,0},{3,1},{4,6},{5,7},{6,4},{7,5},{8,10},{9,11},{10,... | collective-permute-start | bytes 4423688 | tf_op jit(solution)/shard_map/ppermute | solution.py:47
  253.5 35.6 %collective-permute-start.33 = (bf16[960,768]{1,0:T(8,128)(2,1)}, bf16[960,768]{1,0:T(8,128)(2,1)S(1)}, u32[]{:S(2)}, u32[]{:S(2)}) collective-permute-start(bf16[960,768]{1,0:T(8,128)(2,1)} %collective-permute-done.27.refs_2_), channel_id=1, source_target_pairs={{0,16},{16,0},{1,17},{17,1},{2,18},{18,2},{3,19},{19,3},{4,20},{20... | collective-permute-start | bytes 4423688 | tf_op jit(solution)/shard_map/ppermute | solution.py:1023
  297.5 50.6 %all-to-all-start.1 = ((bf16[4,128,3840]{2,1,0:T(8,128)(2,1)}), bf16[4,128,3840]{2,1,0:T(8,128)(2,1)}, u32[]{:S(2)}, u32[]{:S(2)}) async-start(bf16[4,128,3840]{2,1,0:T(8,128)(2,1)} %word_logits.3), calls=%async_computation.1 | async-start | bytes 7864320 | tf_op jit(solution)/shard_map/all_to_all | solution.py:1100
  312.2 26.2 %collective-permute-start.35 = (bf16[2,240,768]{2,1,0:T(8,128)(2,1)}, bf16[2,240,768]{2,1,0:T(8,128)(2,1)S(1)}, u32[]{:S(2)}, u32[]{:S(2)}) collective-permute-start(bf16[2,240,768]{2,1,0:T(8,128)(2,1)} %bitcast.275), channel_id=1, source_target_pairs={{0,4},{1,5},{2,6},{3,7},{4,0},{5,1},{6,2},{7,3},{8,12},{9,13},{10,... | collective-permute-start | bytes 2211848 | tf_op jit(solution)/shard_map/ppermute | solution.py:47
  356.0 21.4 %collective-permute-start.39 = (bf16[4,56,768]{2,1,0:T(8,128)(2,1)S(1)}, bf16[4,56,768]{2,1,0:T(8,128)(2,1)S(1)}, u32[]{:S(2)}, u32[]{:S(2)}) collective-permute-start(bf16[4,56,768]{2,1,0:T(8,128)(2,1)S(1)} %bitcast.291), channel_id=1, source_target_pairs={{0,2},{1,3},{2,0},{3,1},{4,6},{5,7},{6,4},{7,5},{8,10},{9,11},{10,... | collective-permute-start | bytes 1032200 | tf_op jit(solution)/shard_map/ppermute | solution.py:47
  356.4 28.9 %collective-permute-start.40 = (bf16[2,2,144,768]{3,2,1,0:T(8,128)(2,1)S(1)}, bf16[2,2,144,768]{3,2,1,0:T(8,128)(2,1)S(1)}, u32[]{:S(2)}, u32[]{:S(2)}) collective-permute-start(bf16[2,2,144,768]{3,2,1,0:T(8,128)(2,1)S(1)} %get-tuple-element.287), channel_id=1, source_target_pairs={{0,4},{1,5},{2,6},{3,7},{4,0},{5,1},{6,2},{7,3},{8,12},{9,13},{10,... | collective-permute-start | bytes 2654216 | tf_op jit(solution)/shard_map/ppermute | solution.py:47
  357.5 24.1 %collective-permute-start.41 = (bf16[2,240,768]{2,1,0:T(8,128)(2,1)S(1)}, bf16[2,240,768]{2,1,0:T(8,128)(2,1)S(1)}, u32[]{:S(2)}, u32[]{:S(2)}) collective-permute-start(bf16[2,240,768]{2,1,0:T(8,128)(2,1)S(1)} %bitcast.274), channel_id=1, source_target_pairs={{0,2},{1,3},{2,0},{3,1},{4,6},{5,7},{6,4},{7,5},{8,10},{9,11},{10,... | collective-permute-start | bytes 2211848 | tf_op jit(solution)/shard_map/ppermute | solution.py:47
  359.1 24.7 %collective-permute-start.42 = (bf16[240,768]{1,0:T(8,128)(2,1)S(1)}, bf16[240,768]{1,0:T(8,128)(2,1)S(1)}, u32[]{:S(2)}, u32[]{:S(2)}) collective-permute-start(bf16[240,768]{1,0:T(8,128)(2,1)S(1)} %bitcast.277), channel_id=1, source_target_pairs={{0,8},{1,9},{2,10},{3,11},{4,12},{5,13},{6,14},{7,15},{8,0},{9,1},... | collective-permute-start | bytes 1105928 | tf_op jit(solution)/shard_map/ppermute | solution.py:47
  377.6 27.3 %collective-permute-start.44 = (bf16[8,56,768]{2,1,0:T(8,128)(2,1)S(1)}, bf16[8,56,768]{2,1,0:T(8,128)(2,1)}, u32[]{:S(2)}, u32[]{:S(2)}) collective-permute-start(bf16[8,56,768]{2,1,0:T(8,128)(2,1)S(1)} %bitcast.286), channel_id=1, source_target_pairs={{0,1},{1,0},{2,3},{3,2},{4,5},{5,4},{6,7},{7,6},{8,9},{9,8},{10,11... | collective-permute-start | bytes 2064392 | tf_op jit(solution)/shard_map/ppermute | solution.py:47
  387.3 17.6 %collective-permute-start.45 = (bf16[240,768]{1,0:T(8,128)(2,1)S(1)}, bf16[240,768]{1,0:T(8,128)(2,1)S(1)}, u32[]{:S(2)}, u32[]{:S(2)}) collective-permute-start(bf16[240,768]{1,0:T(8,128)(2,1)S(1)} %bitcast.278), channel_id=1, source_target_pairs={{0,8},{1,9},{2,10},{3,11},{4,12},{5,13},{6,14},{7,15},{8,0},{9,1},... | collective-permute-start | bytes 1105928 | tf_op jit(solution)/shard_map/ppermute | solution.py:47
  390.6 64.1 %collective-permute-start.47 = (bf16[1920,768]{1,0:T(8,128)(2,1)}, bf16[1920,768]{1,0:T(8,128)(2,1)}, u32[]{:S(2)}, u32[]{:S(2)}) collective-permute-start(bf16[1920,768]{1,0:T(8,128)(2,1)} %get-tuple-element.313), channel_id=1, source_target_pairs={{0,16},{16,0},{1,17},{17,1},{2,18},{18,2},{3,19},{19,3},{4,20},{20... | collective-permute-start | bytes 8847368 | tf_op jit(solution)/shard_map/ppermute | solution.py:1023
  409.1 45.5 %collective-permute-start.46 = (bf16[144,768]{1,0:T(8,128)(2,1)S(1)}, bf16[144,768]{1,0:T(8,128)(2,1)S(1)}, u32[]{:S(2)}, u32[]{:S(2)}) collective-permute-start(bf16[144,768]{1,0:T(8,128)(2,1)S(1)} %bitcast.279), channel_id=1, source_target_pairs={{0,8},{1,9},{2,10},{3,11},{4,12},{5,13},{6,14},{7,15},{8,0},{9,1},... | collective-permute-start | bytes 663560 | tf_op jit(solution)/shard_map/ppermute | solution.py:47
  (126 other events, 1043.2 us)
